TPU v7x, 512 devices: a whole 4x4x16 slice. The times are simulated.
512 devices in a mesh: row: 32 (over z, x_lo), tensor: 8 (over y, x_hi), seq: 2 (over core).
Axes of the slice: x: 4 (x_hi: 2, x_lo: 2; x = x_hi * 2 + x_lo), y: 4, z: 16, core: 2. Of those that a mesh axis runs over, the one named last changes fastest.
Arguments:
- student: bfloat16 [8192, 5120], P(('seq', 'row'), 'tensor'), parts along dimension 0, may hold values from -6 to 6
- teacher: bfloat16 [8192, 8192], P(('seq', 'row'), 'tensor'), parts along dimension 0, may hold values from -6 to 6
- counts: int32 [6], P('seq'), parts along dimension 0, may hold values from 1 to 3072, 4096 in all
Outputs:
- gradient: bfloat16 [8192, 5120], P(('seq', 'row'), 'tensor'), parts along dimension 0
There are 2 independent parts, one for each index of `seq`. A program takes and returns all parts, laid end to end along the dimension named above; each array names one. Nothing has to cross between parts.
Inputs may be any that keep to these rules, and one draw needn't show every extreme that they name: The counts sum to 4096; the largest is exactly 3072.
All inputs are finite; a program needn't handle non-finite values.
Results may differ from a plain program's by a relative error of at most 0.0049.
Values may be sent and summed in bfloat16 or wider, within the bound.
No kernel may reach another device: no remote copies, remote signals or barrier semaphores. Data moves between devices by JAX's collectives and lax.ppermute only.
A program may use at most 64 MiB of HBM per device.

v0:
```python
import math

import jax
import jax.numpy as jnp
from jax import lax
from jax.sharding import PartitionSpec as P


def segment_of(positions, seq_ends):
    return jnp.sum((positions[:, None] >= seq_ends[None, :-1]).astype(jnp.int32), axis=1)


def on_device(student, teacher, counts):
    rows_dev = student.shape[0]
    tensor_size = lax.axis_size("tensor")
    student_scale = 1.0 / math.sqrt(student.shape[1] * tensor_size)
    teacher_scale = 1.0 / math.sqrt(teacher.shape[1] * tensor_size)
    contraction = (((1,), (1,)), ((), ()))
    everyone = lax.all_gather(student, "row", axis=0, tiled=True)
    total_rows = everyone.shape[0]
    initial = (
        lax.dot_general(student, everyone, contraction, preferred_element_type=jnp.float32)
        * student_scale
    )
    product = (
        lax.dot_general(
            teacher,
            lax.all_gather(teacher, "row", axis=0, tiled=True),
            contraction,
            preferred_element_type=jnp.float32,
        )
        * teacher_scale
    )
    partial_value = initial - product
    seq_ends = jnp.cumsum(counts)
    my_rows = lax.axis_index("row") * rows_dev + jnp.arange(rows_dev, dtype=jnp.int32)
    my_segment = segment_of(my_rows, seq_ends)
    summed = lax.psum(partial_value, "tensor")
    other_segment = segment_of(jnp.arange(total_rows, dtype=jnp.int32), seq_ends)
    difference = jnp.where(my_segment[:, None] == other_segment[None, :], summed, 0.0).astype(
        jnp.bfloat16
    )
    gradient = jnp.dot(difference, everyone, preferred_element_type=jnp.float32)
    seq_index = jnp.arange(counts.shape[0], dtype=jnp.int32)
    row_length = jnp.sum(
        jnp.where(my_segment[:, None] == seq_index[None, :], counts[None, :], 0), axis=1
    )
    return (gradient * lax.rsqrt(row_length.astype(jnp.float32))[:, None]).astype(jnp.bfloat16)


def solution(mesh):
    in_specs = (P(("seq", "row"), "tensor"), P(("seq", "row"), "tensor"), P("seq"))
    out_specs = P(("seq", "row"), "tensor")
    return jax.shard_map(
        on_device, mesh=mesh, in_specs=in_specs, out_specs=out_specs, check_vma=False
    )
```

profile of v0, /device:TPU:2, one launch (start us, length us, event | category | flops | bytes accessed | tf_op | source)
XLA Modules:
  0.0 468.5 jit_solution(972883597094934063)
XLA Ops:
  6.5 0.0 all-gather.5.cloned.1.call-start
  6.5 0.7 all-gather.5.cloned.1.call-update
  7.3 0.0 all-gather.3.cloned.1.call-start
  7.3 0.7 all-gather.3.cloned.1.call-update
  8.0 0.8 reduce-window.4
  8.8 0.1 fusion.6
  8.9 0.7 select_reduce_fusion
  9.7 0.1 fusion.5
  9.8 0.0 copy-start
  9.8 199.8 %all-gather.5.cloned.1.call-done = bf16[4096,1024]{1,0:T(8,128)(2,1)} async-done(((bf16[128,1024]{1,0:T(8,128)(2,1)}), bf16[4096,1024]{1,0:T(8,128)(2,1)}) %all-gather.5.cloned.1.call-update) | async-done | bytes 8388624 | tf_op jit(solution)/shard_map/all_gather | solution.py:28
  209.6 7.7 %convolution_multiply_fusion = f32[128,4096]{1,0:T(8,128)} fusion(bf16[128,1024]{1,0:T(8,128)(2,1)} %param.4, bf16[4096,1024]{1,0:T(8,128)(2,1)} %all-gather.5.cloned.1.call-done), kind=kOutput, calls=%fused_computation | convolution fusion | flops 1074266112 | bytes 10747904 | tf_op jit(solution)/shard_map/dot_general | solution.py:26
  217.3 139.8 %all-gather.3.cloned.1.call-done = bf16[4096,640]{1,0:T(8,128)(2,1)} async-done(((bf16[128,640]{1,0:T(8,128)(2,1)}), bf16[4096,640]{1,0:T(8,128)(2,1)}) %all-gather.3.cloned.1.call-update) | async-done | bytes 5242896 | tf_op jit(solution)/shard_map/all_gather | solution.py:19
  357.1 0.0 copy-done
  357.1 4.9 %fusion = f32[128,4096]{1,0:T(8,128)S(1)} fusion(f32[128,4096]{1,0:T(8,128)} %convolution_multiply_fusion, bf16[128,640]{1,0:T(8,128)(2,1)S(1)} %copy-done, bf16[4096,640]{1,0:T(8,128)(2,1)} %all-gather.3.cloned.1.call-done), kind=kOutput, calls=%fused_computation.2 | convolution fusion | flops 672137216 | bytes 9601024 | tf_op jit(solution)/shard_map/dot_general | solution.py:22
  362.0 95.5 %all-reduce.1 = bf16[128,4096]{1,0:T(8,128)(2,1)S(1)} all-reduce(f32[128,4096]{1,0:T(8,128)S(1)} %fusion), channel_id=1, replica_groups=mesh['row'=32,'tensor'=8,'seq'=2] {'tensor'}, use_global_device_ids=true, to_apply=%region_3.4 | all-reduce | flops 524288 | bytes 3145728 | tf_op jit(solution)/shard_map/psum | solution.py:38
  457.5 4.2 fusion.1
  (3 shorter events, 0.0 us)
Async XLA Ops:
  6.5 203.1 %all-gather.5.cloned.1.call-start = ((), (), s32[]{:S(2)}) async-start(), calls=%async_computation.1 | async-start | bytes 8650752 | tf_op jit(solution)/shard_map/all_gather | solution.py:28
  7.3 349.8 %all-gather.3.cloned.1.call-start = ((), (), s32[]{:S(2)}) async-start(), calls=%async_computation | async-start | bytes 5406720 | tf_op jit(solution)/shard_map/all_gather | solution.py:19
  9.8 347.3 %copy-start = (bf16[128,640]{1,0:T(8,128)(2,1)S(1)}, bf16[128,640]{1,0:T(8,128)(2,1)}, u32[]{:S(2)}) copy-start(bf16[128,640]{1,0:T(8,128)(2,1)} %param.3) | copy-start | bytes 491524
Sparse Core Ops, SparseCore 0:
  9.4 200.1 all-gather.4
  211.7 145.3 all-gather.2
where the time goes:
time: 469 us; the launch traced here: 468 us
  waiting for transfers between devices  341 us (73%)
  blocking collectives  95.5 us (20%)
  matrix products  16.8 us (4%)
  between operations  13.4 us (3%)
    all_gather x1, waiting for transfers between devices, on_device(): lax.all_gather(teacher, 'row', axis=0, tiled=True)  200 us
    all_gather x1, waiting for transfers between devices, on_device(): everyone = lax.all_gather(student, 'row', axis=0, tiled=True)  140 us
    psum x1, blocking collectives, on_device(): summed = lax.psum(partial_value, 'tensor')  95.5 us
  transfers between devices with their start and end apart: 2, of which 2 were waited for; matrix products, arithmetic and copies ran while one was open for 2% of the time, Pallas kernels for 0%

commit v1 on v0

v1 whole, which is shorter than its diff:
```python
import math

import jax
import jax.numpy as jnp
from jax import lax
from jax.sharding import Mesh, PartitionSpec as P

TENSOR = ("y", "xh")
SWAP = [(0, 1), (1, 0)]


def segment_of(positions, seq_ends):
    return jnp.sum((positions[:, None] >= seq_ends[None, :-1]).astype(jnp.int32), axis=1)


def on_device(student, teacher, counts):
    rows, ds = student.shape
    nz, nt = lax.axis_size("z"), lax.axis_size(TENSOR)
    student_scale = 1.0 / math.sqrt(ds * nt)
    teacher_scale = 1.0 / math.sqrt(teacher.shape[1] * nt)
    contraction = (((1,), (1,)), ((), ()))
    z, xl, t = lax.axis_index("z"), lax.axis_index("xl"), lax.axis_index(TENSOR)

    own = jnp.concatenate([student, teacher], axis=1)
    column = lax.all_gather(own, "z", axis=0, tiled=True)
    other = lax.ppermute(own, "xl", SWAP)
    both = jnp.concatenate([own, other], axis=0)
    gram_s = lax.dot_general(
        both[:, :ds], column[:, :ds], contraction, preferred_element_type=jnp.float32
    )
    gram_t = lax.dot_general(
        both[:, ds:], column[:, ds:], contraction, preferred_element_type=jnp.float32
    )
    partial = (gram_s * student_scale - gram_t * teacher_scale).astype(jnp.bfloat16)

    seq_ends = jnp.cumsum(counts)
    r = jnp.arange(rows, dtype=jnp.int32)
    row_of = jnp.concatenate([(2 * z + xl) * rows + r, (2 * z + 1 - xl) * rows + r])
    col_of = ((2 * jnp.arange(nz, dtype=jnp.int32) + xl)[:, None] * rows + r[None, :]).reshape(-1)
    row_segment = segment_of(row_of, seq_ends)
    col_segment = segment_of(col_of, seq_ends)

    share = 2 * rows // nt
    parts = lax.all_to_all(partial.reshape(nt, share, nz * rows), TENSOR, 0, 0)
    summed = jnp.sum(parts.astype(jnp.float32), axis=0)
    my_segment = lax.dynamic_slice(row_segment, (t * share,), (share,))
    difference = jnp.where(my_segment[:, None] == col_segment[None, :], summed, 0.0).astype(
        jnp.bfloat16
    )
    copies = jnp.broadcast_to(difference[None], (nt,) + difference.shape)
    whole = lax.all_to_all(copies, TENSOR, 0, 0).reshape(2 * rows, nz * rows)
    gradient = jnp.dot(whole, column[:, :ds], preferred_element_type=jnp.float32)
    away = lax.ppermute(gradient[rows:].astype(jnp.bfloat16), "xl", SWAP)
    total = gradient[:rows] + away.astype(jnp.float32)

    seq_index = jnp.arange(counts.shape[0], dtype=jnp.int32)
    row_length = jnp.sum(
        jnp.where(row_segment[:rows, None] == seq_index[None, :], counts[None, :], 0), axis=1
    )
    return (total * lax.rsqrt(row_length.astype(jnp.float32))[:, None]).astype(jnp.bfloat16)


def solution(mesh):
    split = Mesh(mesh.devices.reshape(-1, 2, 4, 2, 2), ("z", "xl", "y", "xh", "seq"))
    spec = P(("seq", "z", "xl"), ("y", "xh"))
    return jax.shard_map(
        on_device, mesh=split, in_specs=(spec, spec, P("seq")), out_specs=spec, check_vma=False
    )
```

time: 469 us -> 174 us (0.37)
  waiting for transfers between devices: 341 us -> 124 us
  blocking collectives: 95.5 us -> 0 us
  starting transfers between devices: 0.04 us -> 20.5 us
  matrix products: 16.8 us -> 10 us
    all_gather x2 -> x1, waiting for transfers between devices: 340 us -> 80.7 us  [on_device(): column = lax.all_gather(own, 'z', axis=0, tiled=True)]
    psum x1 -> x0, blocking collectives: 95.5 us -> none  [on_device(): summed = lax.psum(partial_value, 'tensor')]
    all_to_all x0 -> x2, waiting for transfers between devices: none -> 32.9 us  [the longest x1 16.5 us: on_device(): parts = lax.all_to_all(partial.reshape(nt, share, nz * rows), TENSOR, 0, 0)]
    ppermute x0 -> x2, starting transfers between devices: none -> 11.2 us  [the longest x1 7.82 us: on_device(): other = lax.ppermute(own, 'xl', SWAP)]
    ppermute x0 -> x2, waiting for transfers between devices: none -> 10.1 us  [the longest x1 6.28 us: on_device(): other = lax.ppermute(own, 'xl', SWAP)]
    all_to_all x0 -> x2, starting transfers between devices: none -> 9.36 us  [the longest x1 5.8 us: on_device(): parts = lax.all_to_all(partial.reshape(nt, share, nz * rows), TENSOR, 0, 0)]
    dot_general x3, matrix products: 16.8 us -> 10 us  [the longest x1 3.72 us: on_device(): lax.dot_general(both[:, :ds], column[:, :ds], contraction, preferred_elem...]
  transfers between devices with their start and end apart: 2 -> 5, of which waited for: 2 -> 5; matrix products, arithmetic and copies ran while one was open for 2% -> 0% of each run, Pallas kernels for 0% -> 0%
where the time goes in v1:
time: 174 us; the launch traced here: 173 us
  waiting for transfers between devices  124 us (71%)
  starting transfers between devices  20.5 us (12%)
  between operations  13.5 us (8%)
  matrix products  10 us (6%)
  local copies, waits for them, and re-layouts  3.86 us (2%)
    all_gather x1, waiting for transfers between devices, on_device(): column = lax.all_gather(own, 'z', axis=0, tiled=True)  80.7 us
    all_to_all x1, waiting for transfers between devices, on_device(): parts = lax.all_to_all(partial.reshape(nt, share, nz * rows), TENSOR, 0, 0)  16.5 us
    all_to_all x1, waiting for transfers between devices, on_device(): whole = lax.all_to_all(copies, TENSOR, 0, 0).reshape(2 * rows, nz * rows)  16.4 us
    ppermute x1, starting transfers between devices, on_device(): other = lax.ppermute(own, 'xl', SWAP)  7.82 us
    ppermute x1, waiting for transfers between devices, on_device(): other = lax.ppermute(own, 'xl', SWAP)  6.28 us
    all_to_all x1, starting transfers between devices, on_device(): parts = lax.all_to_all(partial.reshape(nt, share, nz * rows), TENSOR, 0, 0)  5.8 us
    ppermute x1, waiting for transfers between devices, on_device(): away = lax.ppermute(gradient[rows:].astype(jnp.bfloat16), 'xl', SWAP)  3.82 us
    dot_general x1, matrix products, on_device(): lax.dot_general(both[:, :ds], column[:, :ds], contraction, preferred_elem...  3.72 us
  transfers between devices with their start and end apart: 5, of which 5 were waited for; matrix products, arithmetic and copies ran while one was open for 0% of the time, Pallas kernels for 0%

profile of v1, /device:TPU:2, one launch (start us, length us, event | category | flops | bytes accessed | tf_op | source)
XLA Modules:
  0.0 173.2 jit_solution(10729701902324567313)
XLA Ops:
  6.5 0.0 all-gather.2.cloned.1.call-start
  6.5 0.9 constant_dynamic-update-slice_fusion.1
  7.5 1.0 constant_dynamic-update-slice_fusion
  8.4 0.0 copy-start
  8.5 0.8 copy-done
  9.2 0.0 all-gather.2.cloned.1.call-update
  9.2 7.8 %collective-permute-start = (bf16[128,1664]{1,0:T(8,128)(2,1)}, bf16[128,1664]{1,0:T(8,128)(2,1)S(1)}, u32[]{:S(2)}, u32[]{:S(2)}) collective-permute-start(bf16[128,1664]{1,0:T(8,128)(2,1)} %copy-done), channel_id=1, source_target_pairs={{0,16},{16,0},{1,17},{17,1},{2,18},{18,2},{3,19},{19,3},{4,20},{20... | collective-permute-start | bytes 1277960 | tf_op jit(solution)/shard_map/ppermute | solution.py:26
  17.1 0.0 copy-start.1
  17.1 6.3 %collective-permute-done = bf16[128,1664]{1,0:T(8,128)(2,1)S(1)} collective-permute-done((bf16[128,1664]{1,0:T(8,128)(2,1)}, bf16[128,1664]{1,0:T(8,128)(2,1)S(1)}, u32[]{:S(2)}, u32[]{:S(2)}) %collective-permute-start) | collective-permute-done | bytes 426016 | tf_op jit(solution)/shard_map/ppermute | solution.py:26
  23.4 80.7 %all-gather.2.cloned.1.call-done = bf16[2048,1664]{1,0:T(8,128)(2,1)} async-done(((bf16[128,1664]{1,0:T(8,128)(2,1)}), bf16[2048,1664]{1,0:T(8,128)(2,1)}) %all-gather.2.cloned.1.call-update) | async-done | bytes 6815760 | tf_op jit(solution)/shard_map/all_gather | solution.py:25
  104.1 3.6 %fusion.3 = f32[256,2048]{1,0:T(8,128)S(1)} fusion(bf16[2048,1664]{1,0:T(8,128)(2,1)} %all-gather.2.cloned.1.call-done, bf16[128,1664]{1,0:T(8,128)(2,1)S(1)} %collective-permute-done, bf16[128,1664]{1,0:T(8,128)(2,1)} %copy-done), kind=kOutput, calls=%fused_computation.4 | convolution fusion | flops 1075314688 | bytes 7143424 | tf_op jit(solution)/shard_map/dot_general | solution.py:31
  107.6 0.0 copy-done.1
  107.7 0.0 copy-start.2
  107.7 3.7 %fusion.6 = bf16[256,2048]{1,0:T(8,128)(2,1)} fusion(f32[256,2048]{1,0:T(8,128)S(1)} %fusion.3, bf16[2048,1664]{1,0:T(8,128)(2,1)} %all-gather.2.cloned.1.call-done, bf16[128,1664]{1,0:T(8,128)(2,1)S(1)} %collective-permute-done, bf16[128,1664]{1,0:T(8,128)(2,1)S(1)} %copy-done.1), kind=kOutput, calls=%fused_computation.5 | convolution fusion | flops 673316864 | bytes 6619136 | tf_op jit(solution)/shard_map/dot_general | solution.py:28
  111.4 5.8 %all-to-all-start = ((bf16[8,32,2048]{2,1,0:T(8,128)(2,1)}), bf16[8,32,2048]{2,1,0:T(8,128)(2,1)S(1)}, u32[]{:S(2)}, u32[]{:S(2)}) async-start(bf16[8,32,2048]{2,1,0:T(8,128)(2,1)} %bitcast.3), calls=%async_computation | async-start | bytes 2097152 | tf_op jit(solution)/shard_map/all_to_all | solution.py:44
  117.2 0.0 copy-done.2
  117.2 0.2 reduce-window.4
  117.4 0.1 fusion.17
  117.5 0.1 dynamic_slice.3
  117.6 0.1 add_bitcast_fusion
  117.6 0.1 fusion.16
  117.7 16.5 %all-to-all-done = bf16[8,32,2048]{2,1,0:T(8,128)(2,1)S(1)} async-done(((bf16[8,32,2048]{2,1,0:T(8,128)(2,1)}), bf16[8,32,2048]{2,1,0:T(8,128)(2,1)S(1)}, u32[]{:S(2)}, u32[]{:S(2)}) %all-to-all-start) | async-done | bytes 1048608 | tf_op jit(solution)/shard_map/all_to_all | solution.py:44
  134.2 0.1 convert_reduce_fusion
  134.4 0.1 select_convert_fusion
  134.5 1.1 broadcast_in_dim.15
  135.6 3.6 %all-to-all-start.1 = ((bf16[8,32,2048]{2,1,0:T(8,128)(2,1)}), bf16[8,32,2048]{2,1,0:T(8,128)(2,1)S(1)}, u32[]{:S(2)}, u32[]{:S(2)}) async-start(bf16[8,32,2048]{2,1,0:T(8,128)(2,1)} %broadcast_in_dim.15), calls=%async_computation.1 | async-start | bytes 2097152 | tf_op jit(solution)/shard_map/all_to_all | solution.py:51
  139.1 0.1 select_reduce_fusion
  139.2 16.4 %all-to-all-done.1 = bf16[8,32,2048]{2,1,0:T(8,128)(2,1)S(1)} async-done(((bf16[8,32,2048]{2,1,0:T(8,128)(2,1)}), bf16[8,32,2048]{2,1,0:T(8,128)(2,1)S(1)}, u32[]{:S(2)}, u32[]{:S(2)}) %all-to-all-start.1) | async-done | bytes 1048608 | tf_op jit(solution)/shard_map/all_to_all | solution.py:51
  155.6 2.7 %fusion.7 = f32[256,640]{1,0:T(8,128)S(1)} fusion(bf16[256,2048]{1,0:T(8,128)(2,1)S(1)} %bitcast.8, bf16[2048,1664]{1,0:T(8,128)(2,1)} %all-gather.2.cloned.1.call-done), kind=kOutput, calls=%fused_computation.6 | convolution fusion | flops 671088640 | bytes 4325376 | tf_op jit(solution)/shard_map/dot_general | solution.py:52
  158.4 3.4 %collective-permute-start.1 = (bf16[128,640]{1,0:T(8,128)(2,1)S(1)}, bf16[128,640]{1,0:T(8,128)(2,1)S(1)}, u32[]{:S(2)}, u32[]{:S(2)}) collective-permute-start(bf16[128,640]{1,0:T(8,128)(2,1)S(1)} %slice.55), channel_id=1, source_target_pairs={{0,16},{16,0},{1,17},{17,1},{2,18},{18,2},{3,19},{19,3},{4,20},{20... | collective-permute-start | bytes 491528 | tf_op jit(solution)/shard_map/ppermute | solution.py:53
  161.8 3.8 %collective-permute-done.1 = bf16[128,640]{1,0:T(8,128)(2,1)S(1)} collective-permute-done((bf16[128,640]{1,0:T(8,128)(2,1)S(1)}, bf16[128,640]{1,0:T(8,128)(2,1)S(1)}, u32[]{:S(2)}, u32[]{:S(2)}) %collective-permute-start.1) | collective-permute-done | bytes 163872 | tf_op jit(solution)/shard_map/ppermute | solution.py:53
  165.6 0.8 fusion.12
  (7 shorter events, 0.0 us)
Async XLA Ops:
  6.5 97.5 %all-gather.2.cloned.1.call-start = ((), (), s32[]{:S(2)}) async-start(), calls=%async_computation.2 | async-start | bytes 7241728 | tf_op jit(solution)/shard_map/all_gather | solution.py:25
  8.4 0.8 copy-start
  9.2 14.1 %collective-permute-start = (bf16[128,1664]{1,0:T(8,128)(2,1)}, bf16[128,1664]{1,0:T(8,128)(2,1)S(1)}, u32[]{:S(2)}, u32[]{:S(2)}) collective-permute-start(bf16[128,1664]{1,0:T(8,128)(2,1)} %copy-done), channel_id=1, source_target_pairs={{0,16},{16,0},{1,17},{17,1},{2,18},{18,2},{3,19},{19,3},{4,20},{20... | collective-permute-start | bytes 1277960 | tf_op jit(solution)/shard_map/ppermute | solution.py:26
  17.1 90.6 %copy-start.1 = (bf16[128,1664]{1,0:T(8,128)(2,1)S(1)}, bf16[128,1664]{1,0:T(8,128)(2,1)}, u32[]{:S(2)}) copy-start(bf16[128,1664]{1,0:T(8,128)(2,1)} %copy-done) | copy-start | bytes 1277956
  107.7 9.6 %copy-start.2 = (s32[3]{0:T(128)S(1)}, s32[3]{0:T(128)}, u32[]{:S(2)}) copy-start(s32[3]{0:T(128)} %param.5) | copy-start | bytes 40
  111.4 22.9 %all-to-all-start = ((bf16[8,32,2048]{2,1,0:T(8,128)(2,1)}), bf16[8,32,2048]{2,1,0:T(8,128)(2,1)S(1)}, u32[]{:S(2)}, u32[]{:S(2)}) async-start(bf16[8,32,2048]{2,1,0:T(8,128)(2,1)} %bitcast.3), calls=%async_computation | async-start | bytes 2097152 | tf_op jit(solution)/shard_map/all_to_all | solution.py:44
  135.6 20.1 %all-to-all-start.1 = ((bf16[8,32,2048]{2,1,0:T(8,128)(2,1)}), bf16[8,32,2048]{2,1,0:T(8,128)(2,1)S(1)}, u32[]{:S(2)}, u32[]{:S(2)}) async-start(bf16[8,32,2048]{2,1,0:T(8,128)(2,1)} %broadcast_in_dim.15), calls=%async_computation.1 | async-start | bytes 2097152 | tf_op jit(solution)/shard_map/all_to_all | solution.py:51
  158.4 7.2 %collective-permute-start.1 = (bf16[128,640]{1,0:T(8,128)(2,1)S(1)}, bf16[128,640]{1,0:T(8,128)(2,1)S(1)}, u32[]{:S(2)}, u32[]{:S(2)}) collective-permute-start(bf16[128,640]{1,0:T(8,128)(2,1)S(1)} %slice.55), channel_id=1, source_target_pairs={{0,16},{16,0},{1,17},{17,1},{2,18},{18,2},{3,19},{19,3},{4,20},{20... | collective-permute-start | bytes 491528 | tf_op jit(solution)/shard_map/ppermute | solution.py:53
Sparse Core Ops, SparseCore 0:
  9.4 94.5 all-gather.1

commit v2 on v0

v2 whole, which is shorter than its diff:
```python
import math

import jax
import jax.numpy as jnp
from jax import lax
from jax.experimental import pallas as pl
from jax.experimental.pallas import tpu as pltpu
from jax.sharding import Mesh, PartitionSpec as P

TENSOR = ("y", "xh")
ROW = ("z", "xl", "seq")
NZ, NX, NSEQ, NT = 16, 2, 2, 8

ELEMENTS = ((0, 0), (-2, 0), (-4, 1), (3, 0), (3, 1), (4, 0), (4, 1))
FIRST = ((1, 0, (-2, 0)), (3, 0, (3, 0)))
SECOND = ((2, 1, (-2, 1)), (6, 3, (1, 1)), (5, 3, (1, 0)), (4, 3, (0, 1)))
TILES = (
    (0, 0), (0, 1), (0, 3), (0, 4), (0, 5), (0, 6),
    (1, 2), (1, 3), (1, 4), (1, 5), (1, 6),
    (2, 3), (2, 4), (2, 5), (2, 6),
    (3, 4), (3, 5), (3, 6),
)
ONE_SIDED = ((0, 0), (2, 5), (2, 6), (3, 4))
F32, BF16 = jnp.float32, jnp.bfloat16


def place(z, x, s):
    return (z % NZ * NX + x) * NSEQ + s


def moves(step, back):
    pairs = []
    for z in range(NZ):
        for x in range(NX):
            for s in range(NSEQ):
                far = place(z + (step[0] if s == 0 else -step[0]), x ^ step[1], s)
                here = place(z, x, s)
                pairs.append((here, far) if back else (far, here))
    return pairs


def fetch(block, step):
    return lax.ppermute(block, ROW, moves(step, False))


def give(block, step):
    return lax.ppermute(block, ROW, moves(step, True))


def gather(own):
    held = {0: own}
    for group in (FIRST, SECOND):
        for element, source, step in group:
            held[element] = fetch(held[source], step)
    return [held[i] for i in range(len(ELEMENTS))]


def tile_dot(left, right):
    return lax.dot_general(left, right, (((1,), (1,)), ((), ())), preferred_element_type=F32)


def rights_of(left):
    return [b for a, b in TILES if a == left]


def teacher_kernel(scale, *refs):
    blocks, out = refs[:-1], refs[-1]
    k = 0
    for left in sorted({a for a, _ in TILES}):
        rights = rights_of(left)
        right = jnp.concatenate([blocks[b][...] for b in rights], axis=0)
        product = tile_dot(blocks[left][...], right) * scale
        for i in range(len(rights)):
            n = product.shape[0]
            out[k] = product[:, i * n : (i + 1) * n]
            k += 1


def student_kernel(scale, *refs):
    blocks, teacher, out = refs[:-2], refs[-2], refs[-1]
    share = out.shape[1] // len(TILES)
    k = 0
    for left in sorted({a for a, _ in TILES}):
        rights = rights_of(left)
        right = jnp.concatenate([blocks[b][...] for b in rights], axis=0)
        product = tile_dot(blocks[left][...], right) * scale
        for i in range(len(rights)):
            n = product.shape[0]
            tile = (product[:, i * n : (i + 1) * n] - teacher[k]).astype(BF16)
            out[:, k * share : (k + 1) * share, :] = tile.reshape(NT, share, n)
            k += 1


def mask_kernel(where_ref, parts, out):
    share = parts.shape[1] // len(TILES)
    n = parts.shape[2]
    first_end, second_end, part = where_ref[0], where_ref[1], where_ref[2]

    def segment(r):
        return (r >= first_end).astype(jnp.int32) + (r >= second_end).astype(jnp.int32)

    for k, (a, b) in enumerate(TILES):
        rows = slice(k * share, (k + 1) * share)
        total = parts[0, rows, :].astype(F32)
        for s in range(1, NT):
            total += parts[s, rows, :].astype(F32)
        r = where_ref[3 + a] + part * share + lax.broadcasted_iota(jnp.int32, (share, n), 0)
        c = where_ref[3 + b] + lax.broadcasted_iota(jnp.int32, (share, n), 1)
        kept = jnp.where(segment(r) == segment(c), total, 0.0).astype(BF16)
        for s in range(NT):
            out[s, rows, :] = kept


def terms_of(a):
    straight = [(k, b) for k, (p, b) in enumerate(TILES) if p == a]
    turned = [(k, p) for k, (p, b) in enumerate(TILES) if b == a and (p, b) not in ONE_SIDED]
    return straight, turned


def gradient_kernel(wanted, *refs):
    tiles, blocks, outs = refs[0], refs[1 : 1 + len(ELEMENTS)], refs[1 + len(ELEMENTS) :]
    share = tiles.shape[1] // len(TILES)
    n = tiles.shape[2]

    def tile(k):
        return tiles[:, k * share : (k + 1) * share, :].reshape(NT * share, n)

    for out, a in zip(outs, wanted, strict=True):
        straight, turned = terms_of(a)
        total = None
        if straight:
            total = jnp.dot(
                jnp.concatenate([tile(k) for k, _ in straight], axis=1),
                jnp.concatenate([blocks[b][...] for _, b in straight], axis=0),
                preferred_element_type=F32,
            )
        if turned:
            more = lax.dot_general(
                jnp.concatenate([tile(k) for k, _ in turned], axis=0),
                jnp.concatenate([blocks[b][...] for _, b in turned], axis=0),
                (((0,), (0,)), ((), ())),
                preferred_element_type=F32,
            )
            total = more if total is None else total + more
        out[...] = total.astype(out.dtype)


def call(kernel, out_shape, flops, *operands, smem=0):
    vmem = pl.BlockSpec(memory_space=pltpu.VMEM)
    specs = [pl.BlockSpec(memory_space=pltpu.SMEM)] * smem + [vmem] * (len(operands) - smem)
    several = isinstance(out_shape, (list, tuple))
    moved = sum(x.size * x.dtype.itemsize for x in operands)
    return pl.pallas_call(
        kernel,
        out_shape=out_shape,
        in_specs=specs,
        out_specs=[vmem] * len(out_shape) if several else vmem,
        compiler_params=pltpu.CompilerParams(vmem_limit_bytes=40 * 1024 * 1024),
        cost_estimate=pl.CostEstimate(flops=flops, bytes_accessed=moved, transcendentals=0),
    )(*operands)


def on_device(student, teacher, counts):
    rows, ds = student.shape
    dt = teacher.shape[1]
    count = len(TILES)
    share = rows // NT
    z, x, s = lax.axis_index("z"), lax.axis_index("xl"), lax.axis_index("seq")

    teachers = gather(teacher)
    students = gather(student)

    gram_t = call(
        lambda *refs: teacher_kernel(1.0 / math.sqrt(dt * NT), *refs),
        jax.ShapeDtypeStruct((count, rows, rows), F32),
        2 * count * rows * rows * dt,
        *teachers,
    )
    partial = call(
        lambda *refs: student_kernel(1.0 / math.sqrt(ds * NT), *refs),
        jax.ShapeDtypeStruct((NT, count * share, rows), BF16),
        2 * count * rows * rows * ds,
        *students,
        gram_t,
    )

    ends = jnp.cumsum(counts)
    sign = 1 - 2 * s
    starts = [(((z + sign * ez) % NZ) * NX + (x ^ ex)) * rows for ez, ex in ELEMENTS]
    where = jnp.stack([ends[0], ends[1], lax.axis_index(TENSOR)] + starts).astype(jnp.int32)
    parts = lax.all_to_all(partial, TENSOR, 0, 0)
    copies = call(
        mask_kernel,
        jax.ShapeDtypeStruct(parts.shape, BF16),
        NT * count * share * rows,
        where,
        parts,
        smem=1,
    )
    tiles = lax.all_to_all(copies, TENSOR, 0, 0)

    far = [e for e, _, _ in SECOND]
    near = [0] + [e for e, _, _ in FIRST]
    block = 2 * rows * rows * ds
    given = call(
        lambda *refs: gradient_kernel(far, *refs),
        [jax.ShapeDtypeStruct((rows, ds), BF16)] * len(far),
        14 * block,
        tiles,
        *students,
    )
    kept = call(
        lambda *refs: gradient_kernel(near, *refs),
        [jax.ShapeDtypeStruct((rows, ds), F32)] * len(near),
        18 * block,
        tiles,
        *students,
    )
    sums = dict(zip(near, kept, strict=True))
    for (_, target, step), value in zip(SECOND, given, strict=True):
        sums[target] = sums[target] + give(value, step).astype(F32)
    for element, target, step in FIRST:
        sums[target] = sums[target] + give(sums[element].astype(BF16), step).astype(F32)

    r = starts[0] + jnp.arange(rows, dtype=jnp.int32)
    segment = jnp.sum((r[:, None] >= ends[None, :-1]).astype(jnp.int32), axis=1)
    index = jnp.arange(counts.shape[0], dtype=jnp.int32)
    length = jnp.sum(jnp.where(segment[:, None] == index[None, :], counts[None, :], 0), axis=1)
    return (sums[0] * lax.rsqrt(length.astype(F32))[:, None]).astype(BF16)


def solution(mesh):
    split = Mesh(mesh.devices.reshape(NZ, NX, 4, 2, NSEQ), ("z", "xl", "y", "xh", "seq"))
    spec = P(("seq", "z", "xl"), TENSOR)
    return jax.shard_map(
        on_device, mesh=split, in_specs=(spec, spec, P("seq")), out_specs=spec, check_vma=False
    )
```

time: 469 us -> 146 us (0.31)
  the two profiles are of different devices: /device:TPU:2 before, /device:TPU:32 now
where the time goes in v2:
time: 146 us; the launch traced here: 145 us
  starting transfers between devices  83.3 us (57%)
  waiting for transfers between devices  51.2 us (35%)
  Pallas kernels  6.33 us (4%)
  local copies, waits for them, and re-layouts  2.97 us (2%)
    ppermute x12, starting transfers between devices, fetch(): return lax.ppermute(block, ROW, moves(step, False))  54.7 us
    ppermute x12, waiting for transfers between devices, fetch(): return lax.ppermute(block, ROW, moves(step, False))  19.5 us
    ppermute x6, starting transfers between devices, give(): return lax.ppermute(block, ROW, moves(step, True))  19.2 us
    all_to_all x1, waiting for transfers between devices, on_device(): tiles = lax.all_to_all(copies, TENSOR, 0, 0)  12.7 us
    ppermute x6, waiting for transfers between devices, give(): return lax.ppermute(block, ROW, moves(step, True))  9.79 us
    all_to_all x1, waiting for transfers between devices, on_device(): parts = lax.all_to_all(partial, TENSOR, 0, 0)  9.29 us
    pallas_call x5, Pallas kernels, call(): pl.pallas_call(kernel, out_shape=out_shape, in_specs=specs, out_specs=[vm...  6.33 us
    all_to_all x1, starting transfers between devices, on_device(): parts = lax.all_to_all(partial, TENSOR, 0, 0)  5.33 us
  transfers between devices with their start and end apart: 20, of which 8 were waited for; matrix products, arithmetic and copies ran while one was open for 2% of the time, Pallas kernels for 2%

profile of v2, /device:TPU:32, one launch (start us, length us, event | category | flops | bytes accessed | tf_op | source)
XLA Modules:
  0.0 145.4 jit_solution(15162275415027373359)
XLA Ops:
  0.0 11.5 %collective-permute-start.8 = (bf16[128,1024]{1,0:T(8,128)(2,1)}, bf16[128,1024]{1,0:T(8,128)(2,1)S(1)}, u32[]{:S(2)}, u32[]{:S(2)}) collective-permute-start(bf16[128,1024]{1,0:T(8,128)(2,1)} %refs_0_.2), channel_id=1, source_target_pairs={{96,0},{417,1},{112,16},{433,17},{128,32},{449,33},{144,48},{465,4... | collective-permute-start | bytes 786440 | tf_op jit(solution)/shard_map/ppermute | solution.py:43
  11.5 1.9 %collective-permute-start.6 = (bf16[128,1024]{1,0:T(8,128)(2,1)}, bf16[128,1024]{1,0:T(8,128)(2,1)S(1)}, u32[]{:S(2)}, u32[]{:S(2)}) collective-permute-start(bf16[128,1024]{1,0:T(8,128)(2,1)} %refs_0_.2), channel_id=1, source_target_pairs={{448,0},{65,1},{464,16},{81,17},{480,32},{97,33},{496,48},{113,49}... | collective-permute-start | bytes 786440 | tf_op jit(solution)/shard_map/ppermute | solution.py:43
  13.4 6.5 %collective-permute-start.2 = (bf16[128,640]{1,0:T(8,128)(2,1)}, bf16[128,640]{1,0:T(8,128)(2,1)S(1)}, u32[]{:S(2)}, u32[]{:S(2)}) collective-permute-start(bf16[128,640]{1,0:T(8,128)(2,1)} %refs_1_.3), channel_id=1, source_target_pairs={{96,0},{417,1},{112,16},{433,17},{128,32},{449,33},{144,48},{465,4... | collective-permute-start | bytes 491528 | tf_op jit(solution)/shard_map/ppermute | solution.py:43
  19.9 5.4 %collective-permute-done.8.refs_3_ = bf16[128,1024]{1,0:T(8,128)(2,1)S(1)} collective-permute-done((bf16[128,1024]{1,0:T(8,128)(2,1)}, bf16[128,1024]{1,0:T(8,128)(2,1)S(1)}, u32[]{:S(2)}, u32[]{:S(2)}) %collective-permute-start.8) | collective-permute-done | bytes 262176 | tf_op jit(solution)/shard_map/ppermute | solution.py:43
  25.3 2.5 %collective-permute-start.10 = (bf16[128,1024]{1,0:T(8,128)(2,1)S(1)}, bf16[128,1024]{1,0:T(8,128)(2,1)S(1)}, u32[]{:S(2)}, u32[]{:S(2)}) collective-permute-start(bf16[128,1024]{1,0:T(8,128)(2,1)S(1)} %collective-permute-done.8.refs_3_), channel_id=1, source_target_pairs={{32,0},{481,1},{48,16},{497,17},{64,32},{1,33},{80,48},{17,49},{96... | collective-permute-start | bytes 786440 | tf_op jit(solution)/shard_map/ppermute | solution.py:43
  27.9 8.1 %collective-permute-start.11 = (bf16[128,1024]{1,0:T(8,128)(2,1)S(1)}, bf16[128,1024]{1,0:T(8,128)(2,1)S(1)}, u32[]{:S(2)}, u32[]{:S(2)}) collective-permute-start(bf16[128,1024]{1,0:T(8,128)(2,1)S(1)} %collective-permute-done.8.refs_3_), channel_id=1, source_target_pairs={{48,0},{497,1},{32,16},{481,17},{80,32},{17,33},{64,48},{1,49},{11... | collective-permute-start | bytes 786440 | tf_op jit(solution)/shard_map/ppermute | solution.py:43
  36.0 3.8 %collective-permute-start.9 = (bf16[128,1024]{1,0:T(8,128)(2,1)S(1)}, bf16[128,1024]{1,0:T(8,128)(2,1)S(1)}, u32[]{:S(2)}, u32[]{:S(2)}) collective-permute-start(bf16[128,1024]{1,0:T(8,128)(2,1)S(1)} %collective-permute-done.8.refs_3_), channel_id=1, source_target_pairs={{16,0},{17,1},{0,16},{1,17},{48,32},{49,33},{32,48},{33,49},{80,64... | collective-permute-start | bytes 786440 | tf_op jit(solution)/shard_map/ppermute | solution.py:43
  39.7 0.0 collective-permute-done.2.refs_3_.refs_4_
  39.7 1.9 %collective-permute-start = (bf16[128,640]{1,0:T(8,128)(2,1)}, bf16[128,640]{1,0:T(8,128)(2,1)S(1)}, u32[]{:S(2)}, u32[]{:S(2)}) collective-permute-start(bf16[128,640]{1,0:T(8,128)(2,1)} %refs_1_.3), channel_id=1, source_target_pairs={{448,0},{65,1},{464,16},{81,17},{480,32},{97,33},{496,48},{113,49}... | collective-permute-start | bytes 491528 | tf_op jit(solution)/shard_map/ppermute | solution.py:43
  41.7 0.0 collective-permute-done.6.refs_1_
  41.7 1.9 %collective-permute-start.7 = (bf16[128,1024]{1,0:T(8,128)(2,1)S(1)}, bf16[128,1024]{1,0:T(8,128)(2,1)S(1)}, u32[]{:S(2)}, u32[]{:S(2)}) collective-permute-start(bf16[128,1024]{1,0:T(8,128)(2,1)S(1)} %collective-permute-done.6.refs_1_), channel_id=1, source_target_pairs={{464,0},{81,1},{448,16},{65,17},{496,32},{113,33},{480,48},{97,49}... | collective-permute-start | bytes 786440 | tf_op jit(solution)/shard_map/ppermute | solution.py:43
  43.6 7.5 %collective-permute-done.refs_1_.refs_2_ = bf16[128,640]{1,0:T(8,128)(2,1)S(1)} collective-permute-done((bf16[128,640]{1,0:T(8,128)(2,1)}, bf16[128,640]{1,0:T(8,128)(2,1)S(1)}, u32[]{:S(2)}, u32[]{:S(2)}) %collective-permute-start) | collective-permute-done | bytes 163872 | tf_op jit(solution)/shard_map/ppermute | solution.py:43
  51.1 6.5 %collective-permute-start.3 = (bf16[128,640]{1,0:T(8,128)(2,1)S(1)}, bf16[128,640]{1,0:T(8,128)(2,1)S(1)}, u32[]{:S(2)}, u32[]{:S(2)}) collective-permute-start(bf16[128,640]{1,0:T(8,128)(2,1)S(1)} %collective-permute-done.2.refs_3_.refs_4_), channel_id=1, source_target_pairs={{16,0},{17,1},{0,16},{1,17},{48,32},{49,33},{32,48},{33,49},{80,64... | collective-permute-start | bytes 491528 | tf_op jit(solution)/shard_map/ppermute | solution.py:43
  57.6 0.0 collective-permute-done.10.refs_5_
  57.6 1.9 %collective-permute-start.4 = (bf16[128,640]{1,0:T(8,128)(2,1)S(1)}, bf16[128,640]{1,0:T(8,128)(2,1)S(1)}, u32[]{:S(2)}, u32[]{:S(2)}) collective-permute-start(bf16[128,640]{1,0:T(8,128)(2,1)S(1)} %collective-permute-done.2.refs_3_.refs_4_), channel_id=1, source_target_pairs={{32,0},{481,1},{48,16},{497,17},{64,32},{1,33},{80,48},{17,49},{96... | collective-permute-start | bytes 491528 | tf_op jit(solution)/shard_map/ppermute | solution.py:43
  59.5 0.0 collective-permute-done.11.refs_6_
  59.5 5.3 %collective-permute-start.5 = (bf16[128,640]{1,0:T(8,128)(2,1)S(1)}, bf16[128,640]{1,0:T(8,128)(2,1)S(1)}, u32[]{:S(2)}, u32[]{:S(2)}) collective-permute-start(bf16[128,640]{1,0:T(8,128)(2,1)S(1)} %collective-permute-done.2.refs_3_.refs_4_), channel_id=1, source_target_pairs={{48,0},{497,1},{32,16},{481,17},{80,32},{17,33},{64,48},{1,49},{11... | collective-permute-start | bytes 491528 | tf_op jit(solution)/shard_map/ppermute | solution.py:43
  64.8 0.0 collective-permute-done.9.refs_4_
  64.9 2.9 %collective-permute-start.1 = (bf16[128,640]{1,0:T(8,128)(2,1)S(1)}, bf16[128,640]{1,0:T(8,128)(2,1)S(1)}, u32[]{:S(2)}, u32[]{:S(2)}) collective-permute-start(bf16[128,640]{1,0:T(8,128)(2,1)S(1)} %collective-permute-done.refs_1_.refs_2_), channel_id=1, source_target_pairs={{464,0},{81,1},{448,16},{65,17},{496,32},{113,33},{480,48},{97,49}... | collective-permute-start | bytes 491528 | tf_op jit(solution)/shard_map/ppermute | solution.py:43
  67.7 0.0 collective-permute-done.7.refs_2_
  67.8 0.9 copy-done.1
  68.7 1.6 %shard_map.37.refs_7_ = f32[18,128,128]{2,1,0:T(8,128)S(1)} custom-call(bf16[128,1024]{1,0:T(8,128)(2,1)S(1)} %copy-done.1, bf16[128,1024]{1,0:T(8,128)(2,1)S(1)} %collective-permute-done.6.refs_1_, bf16[128,1024]{1,0:T(8,128)(2,1)S(1)} %collective-permute-done.7.refs_2_, bf16[128,1024]{1,0:T(8,128)(2,1)S(1)} %collective-permute-done.8.refs_3_, ...), custom_call_target="tpu_custom_call" | custom-call | flops 603979776 | bytes 1835008 | tf_op jit(solution)/shard_map/pallas_call | solution.py:153
  70.3 0.0 collective-permute-done.3.refs_4_.refs_5_
  70.3 6.6 %collective-permute-done.1.refs_2_.refs_3_ = bf16[128,640]{1,0:T(8,128)(2,1)S(1)} collective-permute-done((bf16[128,640]{1,0:T(8,128)(2,1)S(1)}, bf16[128,640]{1,0:T(8,128)(2,1)S(1)}, u32[]{:S(2)}, u32[]{:S(2)}) %collective-permute-start.1) | collective-permute-done | bytes 163872 | tf_op jit(solution)/shard_map/ppermute | solution.py:43
  76.9 1.9 %shard_map.38 = bf16[8,288,128]{2,1,0:T(8,128)(2,1)} custom-call(bf16[128,640]{1,0:T(8,128)(2,1)S(1)} %copy-done, bf16[128,640]{1,0:T(8,128)(2,1)S(1)} %collective-permute-done.refs_1_.refs_2_, bf16[128,640]{1,0:T(8,128)(2,1)S(1)} %collective-permute-done.1.refs_2_.refs_3_, bf16[128,640]{1,0:T(8,128)(2,1)S(1)} %collective-permute-done.2.refs_3_.refs_4_, ...), custom_call_target="tpu_custom_call" | custom-call | flops 377487360 | bytes 2326528 | tf_op jit(solution)/shard_map/pallas_call | solution.py:153
  78.8 5.3 %all-to-all-start = ((bf16[8,288,128]{2,1,0:T(8,128)(2,1)}), bf16[8,288,128]{2,1,0:T(8,128)(2,1)S(1)}, u32[]{:S(2)}, u32[]{:S(2)}) async-start(bf16[8,288,128]{2,1,0:T(8,128)(2,1)} %shard_map.38), calls=%async_computation | async-start | bytes 1179648 | tf_op jit(solution)/shard_map/all_to_all | solution.py:191
  84.1 0.2 reduce-window.4
  84.3 0.6 fusion.1
  84.9 1.4 stack.35.where_ref
  86.3 9.3 %all-to-all-done.parts = bf16[8,288,128]{2,1,0:T(8,128)(2,1)S(1)} async-done(((bf16[8,288,128]{2,1,0:T(8,128)(2,1)}), bf16[8,288,128]{2,1,0:T(8,128)(2,1)S(1)}, u32[]{:S(2)}, u32[]{:S(2)}) %all-to-all-start) | async-done | bytes 589856 | tf_op jit(solution)/shard_map/all_to_all | solution.py:191
  95.6 1.5 %shard_map.39 = bf16[8,288,128]{2,1,0:T(8,128)(2,1)} custom-call(s32[10]{0:T(128)S(1)} %stack.35.where_ref, bf16[8,288,128]{2,1,0:T(8,128)(2,1)S(1)} %all-to-all-done.parts), custom_call_target="tpu_custom_call" | custom-call | flops 294912 | bytes 589864 | tf_op jit(solution)/shard_map/pallas_call | solution.py:153
  97.1 4.1 %all-to-all-start.1 = ((bf16[8,288,128]{2,1,0:T(8,128)(2,1)}), bf16[8,288,128]{2,1,0:T(8,128)(2,1)S(1)}, u32[]{:S(2)}, u32[]{:S(2)}) async-start(bf16[8,288,128]{2,1,0:T(8,128)(2,1)} %shard_map.39), calls=%async_computation.1 | async-start | bytes 1179648 | tf_op jit(solution)/shard_map/all_to_all | solution.py:200
  101.2 12.7 %all-to-all-done.1.refs_0_ = bf16[8,288,128]{2,1,0:T(8,128)(2,1)S(1)} async-done(((bf16[8,288,128]{2,1,0:T(8,128)(2,1)}), bf16[8,288,128]{2,1,0:T(8,128)(2,1)S(1)}, u32[]{:S(2)}, u32[]{:S(2)}) %all-to-all-start.1) | async-done | bytes 589856 | tf_op jit(solution)/shard_map/all_to_all | solution.py:200
  113.8 0.7 shard_map.41
  114.5 1.9 %collective-permute-start.12 = (bf16[128,640]{1,0:T(8,128)(2,1)S(1)}, bf16[128,640]{1,0:T(8,128)(2,1)S(1)}, u32[]{:S(2)}, u32[]{:S(2)}) collective-permute-start(bf16[128,640]{1,0:T(8,128)(2,1)S(1)} %get-tuple-element.14), channel_id=1, source_target_pairs={{0,464},{1,81},{16,448},{17,65},{32,496},{33,113},{48,480},{49,97}... | collective-permute-start | bytes 491528 | tf_op jit(solution)/shard_map/ppermute | solution.py:47
  116.4 0.1 fusion
  116.5 0.1 select_reduce_fusion
  116.6 3.9 %collective-permute-start.14 = (bf16[128,640]{1,0:T(8,128)(2,1)S(1)}, bf16[128,640]{1,0:T(8,128)(2,1)S(1)}, u32[]{:S(2)}, u32[]{:S(2)}) collective-permute-start(bf16[128,640]{1,0:T(8,128)(2,1)S(1)} %get-tuple-element.16), channel_id=1, source_target_pairs={{0,48},{1,497},{16,32},{17,481},{32,80},{33,17},{48,64},{49,1},{64... | collective-permute-start | bytes 491528 | tf_op jit(solution)/shard_map/ppermute | solution.py:47
  120.5 4.3 %collective-permute-start.15 = (bf16[128,640]{1,0:T(8,128)(2,1)S(1)}, bf16[128,640]{1,0:T(8,128)(2,1)S(1)}, u32[]{:S(2)}, u32[]{:S(2)}) collective-permute-start(bf16[128,640]{1,0:T(8,128)(2,1)S(1)} %get-tuple-element.17), channel_id=1, source_target_pairs={{0,32},{1,481},{16,48},{17,497},{32,64},{33,1},{48,80},{49,17},{64... | collective-permute-start | bytes 491528 | tf_op jit(solution)/shard_map/ppermute | solution.py:47
  124.8 2.4 %collective-permute-start.16 = (bf16[128,640]{1,0:T(8,128)(2,1)S(1)}, bf16[128,640]{1,0:T(8,128)(2,1)S(1)}, u32[]{:S(2)}, u32[]{:S(2)}) collective-permute-start(bf16[128,640]{1,0:T(8,128)(2,1)S(1)} %get-tuple-element.18), channel_id=1, source_target_pairs={{0,16},{1,17},{16,0},{17,1},{32,48},{33,49},{48,32},{49,33},{64,80... | collective-permute-start | bytes 491528 | tf_op jit(solution)/shard_map/ppermute | solution.py:47
  127.2 0.7 shard_map.40
  128.0 3.2 %collective-permute-start.13 = (bf16[128,640]{1,0:T(8,128)(2,1)S(1)}, bf16[128,640]{1,0:T(8,128)(2,1)S(1)}, u32[]{:S(2)}, u32[]{:S(2)}) collective-permute-start(bf16[128,640]{1,0:T(8,128)(2,1)S(1)} %add_convert_fusion.1), channel_id=1, source_target_pairs={{0,448},{1,65},{16,464},{17,81},{32,480},{33,97},{48,496},{49,113}... | collective-permute-start | bytes 491528 | tf_op jit(solution)/shard_map/ppermute | solution.py:47
  131.2 0.8 collective-permute-done.16
  132.0 0.1 add_convert_fusion
  132.1 3.5 %collective-permute-start.17 = (bf16[128,640]{1,0:T(8,128)(2,1)S(1)}, bf16[128,640]{1,0:T(8,128)(2,1)S(1)}, u32[]{:S(2)}, u32[]{:S(2)}) collective-permute-start(bf16[128,640]{1,0:T(8,128)(2,1)S(1)} %add_convert_fusion), channel_id=1, source_target_pairs={{0,96},{1,417},{16,112},{17,433},{32,128},{33,449},{48,144},{49,46... | collective-permute-start | bytes 491528 | tf_op jit(solution)/shard_map/ppermute | solution.py:47
  135.6 1.2 collective-permute-done.13
  136.8 7.8 %collective-permute-done.17 = bf16[128,640]{1,0:T(8,128)(2,1)S(1)} collective-permute-done((bf16[128,640]{1,0:T(8,128)(2,1)S(1)}, bf16[128,640]{1,0:T(8,128)(2,1)S(1)}, u32[]{:S(2)}, u32[]{:S(2)}) %collective-permute-start.17) | collective-permute-done | bytes 163872 | tf_op jit(solution)/shard_map/ppermute | solution.py:47
  144.6 0.8 multiply_convert_fusion
  (14 shorter events, 0.1 us)
Async XLA Ops:
  0.0 76.9 %copy-start = (bf16[128,640]{1,0:T(8,128)(2,1)S(1)}, bf16[128,640]{1,0:T(8,128)(2,1)}, u32[]{:S(2)}) copy-start(bf16[128,640]{1,0:T(8,128)(2,1)} %refs_1_.3) | copy-start | bytes 491524
  0.0 25.3 %collective-permute-start.8 = (bf16[128,1024]{1,0:T(8,128)(2,1)}, bf16[128,1024]{1,0:T(8,128)(2,1)S(1)}, u32[]{:S(2)}, u32[]{:S(2)}) collective-permute-start(bf16[128,1024]{1,0:T(8,128)(2,1)} %refs_0_.2), channel_id=1, source_target_pairs={{96,0},{417,1},{112,16},{433,17},{128,32},{449,33},{144,48},{465,4... | collective-permute-start | bytes 786440 | tf_op jit(solution)/shard_map/ppermute | solution.py:43
  11.5 30.1 %collective-permute-start.6 = (bf16[128,1024]{1,0:T(8,128)(2,1)}, bf16[128,1024]{1,0:T(8,128)(2,1)S(1)}, u32[]{:S(2)}, u32[]{:S(2)}) collective-permute-start(bf16[128,1024]{1,0:T(8,128)(2,1)} %refs_0_.2), channel_id=1, source_target_pairs={{448,0},{65,1},{464,16},{81,17},{480,32},{97,33},{496,48},{113,49}... | collective-permute-start | bytes 786440 | tf_op jit(solution)/shard_map/ppermute | solution.py:43
  13.4 26.3 %collective-permute-start.2 = (bf16[128,640]{1,0:T(8,128)(2,1)}, bf16[128,640]{1,0:T(8,128)(2,1)S(1)}, u32[]{:S(2)}, u32[]{:S(2)}) collective-permute-start(bf16[128,640]{1,0:T(8,128)(2,1)} %refs_1_.3), channel_id=1, source_target_pairs={{96,0},{417,1},{112,16},{433,17},{128,32},{449,33},{144,48},{465,4... | collective-permute-start | bytes 491528 | tf_op jit(solution)/shard_map/ppermute | solution.py:43
  25.3 32.2 %collective-permute-start.10 = (bf16[128,1024]{1,0:T(8,128)(2,1)S(1)}, bf16[128,1024]{1,0:T(8,128)(2,1)S(1)}, u32[]{:S(2)}, u32[]{:S(2)}) collective-permute-start(bf16[128,1024]{1,0:T(8,128)(2,1)S(1)} %collective-permute-done.8.refs_3_), channel_id=1, source_target_pairs={{32,0},{481,1},{48,16},{497,17},{64,32},{1,33},{80,48},{17,49},{96... | collective-permute-start | bytes 786440 | tf_op jit(solution)/shard_map/ppermute | solution.py:43
  27.9 31.7 %collective-permute-start.11 = (bf16[128,1024]{1,0:T(8,128)(2,1)S(1)}, bf16[128,1024]{1,0:T(8,128)(2,1)S(1)}, u32[]{:S(2)}, u32[]{:S(2)}) collective-permute-start(bf16[128,1024]{1,0:T(8,128)(2,1)S(1)} %collective-permute-done.8.refs_3_), channel_id=1, source_target_pairs={{48,0},{497,1},{32,16},{481,17},{80,32},{17,33},{64,48},{1,49},{11... | collective-permute-start | bytes 786440 | tf_op jit(solution)/shard_map/ppermute | solution.py:43
  36.0 28.9 %collective-permute-start.9 = (bf16[128,1024]{1,0:T(8,128)(2,1)S(1)}, bf16[128,1024]{1,0:T(8,128)(2,1)S(1)}, u32[]{:S(2)}, u32[]{:S(2)}) collective-permute-start(bf16[128,1024]{1,0:T(8,128)(2,1)S(1)} %collective-permute-done.8.refs_3_), channel_id=1, source_target_pairs={{16,0},{17,1},{0,16},{1,17},{48,32},{49,33},{32,48},{33,49},{80,64... | collective-permute-start | bytes 786440 | tf_op jit(solution)/shard_map/ppermute | solution.py:43
  39.7 11.4 %collective-permute-start = (bf16[128,640]{1,0:T(8,128)(2,1)}, bf16[128,640]{1,0:T(8,128)(2,1)S(1)}, u32[]{:S(2)}, u32[]{:S(2)}) collective-permute-start(bf16[128,640]{1,0:T(8,128)(2,1)} %refs_1_.3), channel_id=1, source_target_pairs={{448,0},{65,1},{464,16},{81,17},{480,32},{97,33},{496,48},{113,49}... | collective-permute-start | bytes 491528 | tf_op jit(solution)/shard_map/ppermute | solution.py:43
  41.7 26.1 %collective-permute-start.7 = (bf16[128,1024]{1,0:T(8,128)(2,1)S(1)}, bf16[128,1024]{1,0:T(8,128)(2,1)S(1)}, u32[]{:S(2)}, u32[]{:S(2)}) collective-permute-start(bf16[128,1024]{1,0:T(8,128)(2,1)S(1)} %collective-permute-done.6.refs_1_), channel_id=1, source_target_pairs={{464,0},{81,1},{448,16},{65,17},{496,32},{113,33},{480,48},{97,49}... | collective-permute-start | bytes 786440 | tf_op jit(solution)/shard_map/ppermute | solution.py:43
  51.1 19.2 %collective-permute-start.3 = (bf16[128,640]{1,0:T(8,128)(2,1)S(1)}, bf16[128,640]{1,0:T(8,128)(2,1)S(1)}, u32[]{:S(2)}, u32[]{:S(2)}) collective-permute-start(bf16[128,640]{1,0:T(8,128)(2,1)S(1)} %collective-permute-done.2.refs_3_.refs_4_), channel_id=1, source_target_pairs={{16,0},{17,1},{0,16},{1,17},{48,32},{49,33},{32,48},{33,49},{80,64... | collective-permute-start | bytes 491528 | tf_op jit(solution)/shard_map/ppermute | solution.py:43
  57.6 12.8 %collective-permute-start.4 = (bf16[128,640]{1,0:T(8,128)(2,1)S(1)}, bf16[128,640]{1,0:T(8,128)(2,1)S(1)}, u32[]{:S(2)}, u32[]{:S(2)}) collective-permute-start(bf16[128,640]{1,0:T(8,128)(2,1)S(1)} %collective-permute-done.2.refs_3_.refs_4_), channel_id=1, source_target_pairs={{32,0},{481,1},{48,16},{497,17},{64,32},{1,33},{80,48},{17,49},{96... | collective-permute-start | bytes 491528 | tf_op jit(solution)/shard_map/ppermute | solution.py:43
  59.5 10.8 %collective-permute-start.5 = (bf16[128,640]{1,0:T(8,128)(2,1)S(1)}, bf16[128,640]{1,0:T(8,128)(2,1)S(1)}, u32[]{:S(2)}, u32[]{:S(2)}) collective-permute-start(bf16[128,640]{1,0:T(8,128)(2,1)S(1)} %collective-permute-done.2.refs_3_.refs_4_), channel_id=1, source_target_pairs={{48,0},{497,1},{32,16},{481,17},{80,32},{17,33},{64,48},{1,49},{11... | collective-permute-start | bytes 491528 | tf_op jit(solution)/shard_map/ppermute | solution.py:43
  64.9 12.1 %collective-permute-start.1 = (bf16[128,640]{1,0:T(8,128)(2,1)S(1)}, bf16[128,640]{1,0:T(8,128)(2,1)S(1)}, u32[]{:S(2)}, u32[]{:S(2)}) collective-permute-start(bf16[128,640]{1,0:T(8,128)(2,1)S(1)} %collective-permute-done.refs_1_.refs_2_), channel_id=1, source_target_pairs={{464,0},{81,1},{448,16},{65,17},{496,32},{113,33},{480,48},{97,49}... | collective-permute-start | bytes 491528 | tf_op jit(solution)/shard_map/ppermute | solution.py:43
  67.7 1.0 copy-start.1
  78.8 5.3 %copy-start.2 = (s32[3]{0:T(128)S(1)}, s32[3]{0:T(128)}, u32[]{:S(2)}) copy-start(s32[3]{0:T(128)} %param.5) | copy-start | bytes 40
  78.8 16.8 %all-to-all-start = ((bf16[8,288,128]{2,1,0:T(8,128)(2,1)}), bf16[8,288,128]{2,1,0:T(8,128)(2,1)S(1)}, u32[]{:S(2)}, u32[]{:S(2)}) async-start(bf16[8,288,128]{2,1,0:T(8,128)(2,1)} %shard_map.38), calls=%async_computation | async-start | bytes 1179648 | tf_op jit(solution)/shard_map/all_to_all | solution.py:191
  97.1 16.8 %all-to-all-start.1 = ((bf16[8,288,128]{2,1,0:T(8,128)(2,1)}), bf16[8,288,128]{2,1,0:T(8,128)(2,1)S(1)}, u32[]{:S(2)}, u32[]{:S(2)}) async-start(bf16[8,288,128]{2,1,0:T(8,128)(2,1)} %shard_map.39), calls=%async_computation.1 | async-start | bytes 1179648 | tf_op jit(solution)/shard_map/all_to_all | solution.py:200
  114.5 13.4 %collective-permute-start.12 = (bf16[128,640]{1,0:T(8,128)(2,1)S(1)}, bf16[128,640]{1,0:T(8,128)(2,1)S(1)}, u32[]{:S(2)}, u32[]{:S(2)}) collective-permute-start(bf16[128,640]{1,0:T(8,128)(2,1)S(1)} %get-tuple-element.14), channel_id=1, source_target_pairs={{0,464},{1,81},{16,448},{17,65},{32,496},{33,113},{48,480},{49,97}... | collective-permute-start | bytes 491528 | tf_op jit(solution)/shard_map/ppermute | solution.py:47
  116.6 14.6 %collective-permute-start.14 = (bf16[128,640]{1,0:T(8,128)(2,1)S(1)}, bf16[128,640]{1,0:T(8,128)(2,1)S(1)}, u32[]{:S(2)}, u32[]{:S(2)}) collective-permute-start(bf16[128,640]{1,0:T(8,128)(2,1)S(1)} %get-tuple-element.16), channel_id=1, source_target_pairs={{0,48},{1,497},{16,32},{17,481},{32,80},{33,17},{48,64},{49,1},{64... | collective-permute-start | bytes 491528 | tf_op jit(solution)/shard_map/ppermute | solution.py:47
  120.5 10.8 %collective-permute-start.15 = (bf16[128,640]{1,0:T(8,128)(2,1)S(1)}, bf16[128,640]{1,0:T(8,128)(2,1)S(1)}, u32[]{:S(2)}, u32[]{:S(2)}) collective-permute-start(bf16[128,640]{1,0:T(8,128)(2,1)S(1)} %get-tuple-element.17), channel_id=1, source_target_pairs={{0,32},{1,481},{16,48},{17,497},{32,64},{33,1},{48,80},{49,17},{64... | collective-permute-start | bytes 491528 | tf_op jit(solution)/shard_map/ppermute | solution.py:47
  124.8 7.2 %collective-permute-start.16 = (bf16[128,640]{1,0:T(8,128)(2,1)S(1)}, bf16[128,640]{1,0:T(8,128)(2,1)S(1)}, u32[]{:S(2)}, u32[]{:S(2)}) collective-permute-start(bf16[128,640]{1,0:T(8,128)(2,1)S(1)} %get-tuple-element.18), channel_id=1, source_target_pairs={{0,16},{1,17},{16,0},{17,1},{32,48},{33,49},{48,32},{49,33},{64,80... | collective-permute-start | bytes 491528 | tf_op jit(solution)/shard_map/ppermute | solution.py:47
  128.0 8.8 %collective-permute-start.13 = (bf16[128,640]{1,0:T(8,128)(2,1)S(1)}, bf16[128,640]{1,0:T(8,128)(2,1)S(1)}, u32[]{:S(2)}, u32[]{:S(2)}) collective-permute-start(bf16[128,640]{1,0:T(8,128)(2,1)S(1)} %add_convert_fusion.1), channel_id=1, source_target_pairs={{0,448},{1,65},{16,464},{17,81},{32,480},{33,97},{48,496},{49,113}... | collective-permute-start | bytes 491528 | tf_op jit(solution)/shard_map/ppermute | solution.py:47
  132.1 12.5 %collective-permute-start.17 = (bf16[128,640]{1,0:T(8,128)(2,1)S(1)}, bf16[128,640]{1,0:T(8,128)(2,1)S(1)}, u32[]{:S(2)}, u32[]{:S(2)}) collective-permute-start(bf16[128,640]{1,0:T(8,128)(2,1)S(1)} %add_convert_fusion), channel_id=1, source_target_pairs={{0,96},{1,417},{16,112},{17,433},{32,128},{33,449},{48,144},{49,46... | collective-permute-start | bytes 491528 | tf_op jit(solution)/shard_map/ppermute | solution.py:47

commit v3 on v2

--- a/solution.py
+++ b/solution.py
@@ -11,9 +11,9 @@
 ROW = ("z", "xl", "seq")
 NZ, NX, NSEQ, NT = 16, 2, 2, 8
 
-ELEMENTS = ((0, 0), (-2, 0), (-4, 1), (3, 0), (3, 1), (4, 0), (4, 1))
-FIRST = ((1, 0, (-2, 0)), (3, 0, (3, 0)))
-SECOND = ((2, 1, (-2, 1)), (6, 3, (1, 1)), (5, 3, (1, 0)), (4, 3, (0, 1)))
+ELEMENTS = ((0, 0), (-2, 1), (-4, 1), (3, 0), (3, 1), (4, 0), (4, 1))
+FIRST = ((1, 0, (-2, 1)), (3, 0, (3, 0)))
+SECOND = ((2, 1, (-2, 0)), (6, 3, (1, 1)), (5, 3, (1, 0)), (4, 3, (0, 1)))
 TILES = (
     (0, 0), (0, 1), (0, 3), (0, 4), (0, 5), (0, 6),
     (1, 2), (1, 3), (1, 4), (1, 5), (1, 6),
@@ -63,30 +63,21 @@
     return [b for a, b in TILES if a == left]
 
 
-def teacher_kernel(scale, *refs):
+def gram_kernel(ds, student_scale, teacher_scale, *refs):
     blocks, out = refs[:-1], refs[-1]
+    share = out.shape[1] // len(TILES)
+    n = blocks[0].shape[0]
     k = 0
     for left in sorted({a for a, _ in TILES}):
         rights = rights_of(left)
-        right = jnp.concatenate([blocks[b][...] for b in rights], axis=0)
-        product = tile_dot(blocks[left][...], right) * scale
+        right_s = jnp.concatenate([blocks[b][:, :ds] for b in rights], axis=0)
+        right_t = jnp.concatenate([blocks[b][:, ds:] for b in rights], axis=0)
+        product = (
+            tile_dot(blocks[left][:, :ds], right_s) * student_scale
+            - tile_dot(blocks[left][:, ds:], right_t) * teacher_scale
+        )
         for i in range(len(rights)):
-            n = product.shape[0]
-            out[k] = product[:, i * n : (i + 1) * n]
-            k += 1
-
-
-def student_kernel(scale, *refs):
-    blocks, teacher, out = refs[:-2], refs[-2], refs[-1]
-    share = out.shape[1] // len(TILES)
-    k = 0
-    for left in sorted({a for a, _ in TILES}):
-        rights = rights_of(left)
-        right = jnp.concatenate([blocks[b][...] for b in rights], axis=0)
-        product = tile_dot(blocks[left][...], right) * scale
-        for i in range(len(rights)):
-            n = product.shape[0]
-            tile = (product[:, i * n : (i + 1) * n] - teacher[k]).astype(BF16)
+            tile = product[:, i * n : (i + 1) * n].astype(BF16)
             out[:, k * share : (k + 1) * share, :] = tile.reshape(NT, share, n)
             k += 1
 
@@ -120,7 +111,7 @@
 def gradient_kernel(wanted, *refs):
     tiles, blocks, outs = refs[0], refs[1 : 1 + len(ELEMENTS)], refs[1 + len(ELEMENTS) :]
     share = tiles.shape[1] // len(TILES)
-    n = tiles.shape[2]
+    n, width = tiles.shape[2], outs[0].shape[1]
 
     def tile(k):
         return tiles[:, k * share : (k + 1) * share, :].reshape(NT * share, n)
@@ -131,13 +122,13 @@
         if straight:
             total = jnp.dot(
                 jnp.concatenate([tile(k) for k, _ in straight], axis=1),
-                jnp.concatenate([blocks[b][...] for _, b in straight], axis=0),
+                jnp.concatenate([blocks[b][:, :width] for _, b in straight], axis=0),
                 preferred_element_type=F32,
             )
         if turned:
             more = lax.dot_general(
                 jnp.concatenate([tile(k) for k, _ in turned], axis=0),
-                jnp.concatenate([blocks[b][...] for _, b in turned], axis=0),
+                jnp.concatenate([blocks[b][:, :width] for _, b in turned], axis=0),
                 (((0,), (0,)), ((), ())),
                 preferred_element_type=F32,
             )
@@ -167,21 +158,14 @@
     share = rows // NT
     z, x, s = lax.axis_index("z"), lax.axis_index("xl"), lax.axis_index("seq")
 
-    teachers = gather(teacher)
-    students = gather(student)
-
-    gram_t = call(
-        lambda *refs: teacher_kernel(1.0 / math.sqrt(dt * NT), *refs),
-        jax.ShapeDtypeStruct((count, rows, rows), F32),
-        2 * count * rows * rows * dt,
-        *teachers,
-    )
+    blocks = gather(jnp.concatenate([student, teacher], axis=1))
     partial = call(
-        lambda *refs: student_kernel(1.0 / math.sqrt(ds * NT), *refs),
+        lambda *refs: gram_kernel(
+            ds, 1.0 / math.sqrt(ds * NT), 1.0 / math.sqrt(dt * NT), *refs
+        ),
         jax.ShapeDtypeStruct((NT, count * share, rows), BF16),
-        2 * count * rows * rows * ds,
-        *students,
-        gram_t,
+        2 * count * rows * rows * (ds + dt),
+        *blocks,
     )
 
     ends = jnp.cumsum(counts)
@@ -207,14 +191,14 @@
         [jax.ShapeDtypeStruct((rows, ds), BF16)] * len(far),
         14 * block,
         tiles,
-        *students,
+        *blocks,
     )
     kept = call(
         lambda *refs: gradient_kernel(near, *refs),
         [jax.ShapeDtypeStruct((rows, ds), F32)] * len(near),
         18 * block,
         tiles,
-        *students,
+        *blocks,
     )
     sums = dict(zip(near, kept, strict=True))
     for (_, target, step), value in zip(SECOND, given, strict=True):

time: 146 us -> 136 us (0.932)
  the two profiles are of different devices: /device:TPU:32 before, /device:TPU:2 now
where the time goes in v3:
time: 136 us; the launch traced here: 135 us
  starting transfers between devices  62.6 us (46%)
  waiting for transfers between devices  59.8 us (44%)
  local copies, waits for them, and re-layouts  6.22 us (5%)
  Pallas kernels  5.19 us (4%)
    ppermute x6, waiting for transfers between devices, fetch(): return lax.ppermute(block, ROW, moves(step, False))  30.4 us
    ppermute x6, starting transfers between devices, fetch(): return lax.ppermute(block, ROW, moves(step, False))  28.2 us
    ppermute x6, starting transfers between devices, give(): return lax.ppermute(block, ROW, moves(step, True))  23.9 us
    ppermute x6, waiting for transfers between devices, give(): return lax.ppermute(block, ROW, moves(step, True))  11.3 us
    all_to_all x1, waiting for transfers between devices, on_device(): tiles = lax.all_to_all(copies, TENSOR, 0, 0)  10.5 us
    all_to_all x1, waiting for transfers between devices, on_device(): parts = lax.all_to_all(partial, TENSOR, 0, 0)  7.76 us
    all_to_all x1, starting transfers between devices, on_device(): parts = lax.all_to_all(partial, TENSOR, 0, 0)  6.98 us
    pallas_call x4, Pallas kernels, call(): pl.pallas_call(kernel, out_shape=out_shape, in_specs=specs, out_specs=[vm...  5.19 us
  transfers between devices with their start and end apart: 14, of which 8 were waited for; matrix products, arithmetic and copies ran while one was open for 2% of the time, Pallas kernels for 1%

profile of v3, /device:TPU:2, one launch (start us, length us, event | category | flops | bytes accessed | tf_op | source)
XLA Modules:
  0.0 135.3 jit_solution(267358245756817812)
XLA Ops:
  0.0 0.0 copy-start.3
  0.0 1.0 constant_dynamic-update-slice_fusion.1
  1.0 0.0 copy-done.3
  1.1 12.3 %collective-permute-start.2 = (bf16[128,1664]{1,0:T(8,128)(2,1)S(1)}, bf16[128,1664]{1,0:T(8,128)(2,1)S(1)}, u32[]{:S(2)}, u32[]{:S(2)}) collective-permute-start(bf16[128,1664]{1,0:T(8,128)(2,1)S(1)} %constant_dynamic-update-slice_fusion.refs_0_.refs_1_), channel_id=1, source_target_pairs={{96,0},{417,1},{112,16},{433,17},{128,32},{449,33},{144,48},{465,4... | collective-permute-start | bytes 1277960 | tf_op jit(solution)/shard_map/ppermute | solution.py:43
  13.3 3.4 %collective-permute-start = (bf16[128,1664]{1,0:T(8,128)(2,1)S(1)}, bf16[128,1664]{1,0:T(8,128)(2,1)S(1)}, u32[]{:S(2)}, u32[]{:S(2)}) collective-permute-start(bf16[128,1664]{1,0:T(8,128)(2,1)S(1)} %constant_dynamic-update-slice_fusion.refs_0_.refs_1_), channel_id=1, source_target_pairs={{464,0},{81,1},{448,16},{65,17},{496,32},{113,33},{480,48},{97,49}... | collective-permute-start | bytes 1277960 | tf_op jit(solution)/shard_map/ppermute | solution.py:43
  16.7 20.2 %collective-permute-done.2.refs_3_.refs_4_ = bf16[128,1664]{1,0:T(8,128)(2,1)S(1)} collective-permute-done((bf16[128,1664]{1,0:T(8,128)(2,1)S(1)}, bf16[128,1664]{1,0:T(8,128)(2,1)S(1)}, u32[]{:S(2)}, u32[]{:S(2)}) %collective-permute-start.2) | collective-permute-done | bytes 426016 | tf_op jit(solution)/shard_map/ppermute | solution.py:43
  36.9 3.3 %collective-permute-start.5 = (bf16[128,1664]{1,0:T(8,128)(2,1)S(1)}, bf16[128,1664]{1,0:T(8,128)(2,1)S(1)}, u32[]{:S(2)}, u32[]{:S(2)}) collective-permute-start(bf16[128,1664]{1,0:T(8,128)(2,1)S(1)} %collective-permute-done.2.refs_3_.refs_4_), channel_id=1, source_target_pairs={{48,0},{497,1},{32,16},{481,17},{80,32},{17,33},{64,48},{1,49},{11... | collective-permute-start | bytes 1277960 | tf_op jit(solution)/shard_map/ppermute | solution.py:43
  40.2 3.8 %collective-permute-start.4 = (bf16[128,1664]{1,0:T(8,128)(2,1)S(1)}, bf16[128,1664]{1,0:T(8,128)(2,1)S(1)}, u32[]{:S(2)}, u32[]{:S(2)}) collective-permute-start(bf16[128,1664]{1,0:T(8,128)(2,1)S(1)} %collective-permute-done.2.refs_3_.refs_4_), channel_id=1, source_target_pairs={{32,0},{481,1},{48,16},{497,17},{64,32},{1,33},{80,48},{17,49},{96... | collective-permute-start | bytes 1277960 | tf_op jit(solution)/shard_map/ppermute | solution.py:43
  44.1 1.9 %collective-permute-start.3 = (bf16[128,1664]{1,0:T(8,128)(2,1)S(1)}, bf16[128,1664]{1,0:T(8,128)(2,1)S(1)}, u32[]{:S(2)}, u32[]{:S(2)}) collective-permute-start(bf16[128,1664]{1,0:T(8,128)(2,1)S(1)} %collective-permute-done.2.refs_3_.refs_4_), channel_id=1, source_target_pairs={{16,0},{17,1},{0,16},{1,17},{48,32},{49,33},{32,48},{33,49},{80,64... | collective-permute-start | bytes 1277960 | tf_op jit(solution)/shard_map/ppermute | solution.py:43
  46.0 0.0 collective-permute-done.refs_1_.refs_2_
  46.0 3.5 %collective-permute-start.1 = (bf16[128,1664]{1,0:T(8,128)(2,1)S(1)}, bf16[128,1664]{1,0:T(8,128)(2,1)S(1)}, u32[]{:S(2)}, u32[]{:S(2)}) collective-permute-start(bf16[128,1664]{1,0:T(8,128)(2,1)S(1)} %collective-permute-done.refs_1_.refs_2_), channel_id=1, source_target_pairs={{448,0},{65,1},{464,16},{81,17},{480,32},{97,33},{496,48},{113,49}... | collective-permute-start | bytes 1277960 | tf_op jit(solution)/shard_map/ppermute | solution.py:43
  49.5 3.2 %collective-permute-done.5.refs_6_.refs_7_ = bf16[128,1664]{1,0:T(8,128)(2,1)S(1)} collective-permute-done((bf16[128,1664]{1,0:T(8,128)(2,1)S(1)}, bf16[128,1664]{1,0:T(8,128)(2,1)S(1)}, u32[]{:S(2)}, u32[]{:S(2)}) %collective-permute-start.5) | collective-permute-done | bytes 426016 | tf_op jit(solution)/shard_map/ppermute | solution.py:43
  52.7 6.9 %collective-permute-done.4.refs_5_.refs_6_ = bf16[128,1664]{1,0:T(8,128)(2,1)S(1)} collective-permute-done((bf16[128,1664]{1,0:T(8,128)(2,1)S(1)}, bf16[128,1664]{1,0:T(8,128)(2,1)S(1)}, u32[]{:S(2)}, u32[]{:S(2)}) %collective-permute-start.4) | collective-permute-done | bytes 426016 | tf_op jit(solution)/shard_map/ppermute | solution.py:43
  59.6 0.0 collective-permute-done.3.refs_4_.refs_5_
  59.6 0.1 collective-permute-done.1.refs_2_.refs_3_
  59.7 2.3 %shard_map.37 = bf16[8,288,128]{2,1,0:T(8,128)(2,1)S(1)} custom-call(bf16[128,1664]{1,0:T(8,128)(2,1)S(1)} %constant_dynamic-update-slice_fusion.refs_0_.refs_1_, bf16[128,1664]{1,0:T(8,128)(2,1)S(1)} %collective-permute-done.refs_1_.refs_2_, bf16[128,1664]{1,0:T(8,128)(2,1)S(1)} %collective-permute-done.1.refs_2_.refs_3_, ...), custom_call_target="tpu_custom_call" | custom-call | flops 981467136 | bytes 2981888 | tf_op jit(solution)/shard_map/pallas_call | solution.py:144
  62.0 0.0 copy-start
  62.0 0.8 copy-done
  62.8 0.0 copy-start.2
  62.8 0.8 copy-done.2
  63.6 7.0 %all-to-all-start = ((bf16[8,288,128]{2,1,0:T(8,128)(2,1)}), bf16[8,288,128]{2,1,0:T(8,128)(2,1)S(1)}, u32[]{:S(2)}, u32[]{:S(2)}) async-start(bf16[8,288,128]{2,1,0:T(8,128)(2,1)} %copy-done.2), calls=%async_computation | async-start | bytes 1179648 | tf_op jit(solution)/shard_map/all_to_all | solution.py:175
  70.6 0.7 copy-done.4
  71.2 0.2 reduce-window.4
  71.4 0.6 fusion.1
  72.0 1.4 %stack.35.where_ref = s32[10]{0:T(128)S(1)} concatenate(s32[1]{0:T(128)} %bitcast.1, s32[1]{0:T(128)} %bitcast.2, s32[1]{0:T(128)} %bitcast.3, s32[1]{0:T(128)} %bitcast.4, s32[1]{0:T(128)} %bitcast.5, s32[1]{0:T(128)} %bitcast.6, s32[1]{0:T(128)} %bitcast.7, s32[1]{0:T(128)} %bitcast.8, s32[1]{0:T(128)} %bitcast.9, s32[1]{0:T(128)} %bitcast.10), dimensions={0} | concatenate | bytes 80 | tf_op jit(solution)/shard_map/stack | solution.py:174
  73.4 7.8 %all-to-all-done.parts = bf16[8,288,128]{2,1,0:T(8,128)(2,1)S(1)} async-done(((bf16[8,288,128]{2,1,0:T(8,128)(2,1)}), bf16[8,288,128]{2,1,0:T(8,128)(2,1)S(1)}, u32[]{:S(2)}, u32[]{:S(2)}) %all-to-all-start) | async-done | bytes 589856 | tf_op jit(solution)/shard_map/all_to_all | solution.py:175
  81.1 1.5 %shard_map.38 = bf16[8,288,128]{2,1,0:T(8,128)(2,1)} custom-call(s32[10]{0:T(128)S(1)} %stack.35.where_ref, bf16[8,288,128]{2,1,0:T(8,128)(2,1)S(1)} %all-to-all-done.parts), custom_call_target="tpu_custom_call" | custom-call | flops 294912 | bytes 589864 | tf_op jit(solution)/shard_map/pallas_call | solution.py:144
  82.6 3.5 %all-to-all-start.1 = ((bf16[8,288,128]{2,1,0:T(8,128)(2,1)}), bf16[8,288,128]{2,1,0:T(8,128)(2,1)S(1)}, u32[]{:S(2)}, u32[]{:S(2)}) async-start(bf16[8,288,128]{2,1,0:T(8,128)(2,1)} %shard_map.38), calls=%async_computation.1 | async-start | bytes 1179648 | tf_op jit(solution)/shard_map/all_to_all | solution.py:184
  86.2 10.5 %all-to-all-done.1.refs_0_ = bf16[8,288,128]{2,1,0:T(8,128)(2,1)S(1)} async-done(((bf16[8,288,128]{2,1,0:T(8,128)(2,1)}), bf16[8,288,128]{2,1,0:T(8,128)(2,1)S(1)}, u32[]{:S(2)}, u32[]{:S(2)}) %all-to-all-start.1) | async-done | bytes 589856 | tf_op jit(solution)/shard_map/all_to_all | solution.py:184
  96.6 1.0 copy-done.1
  97.6 0.7 shard_map.40
  98.3 6.5 %collective-permute-start.6 = (bf16[128,640]{1,0:T(8,128)(2,1)S(1)}, bf16[128,640]{1,0:T(8,128)(2,1)S(1)}, u32[]{:S(2)}, u32[]{:S(2)}) collective-permute-start(bf16[128,640]{1,0:T(8,128)(2,1)S(1)} %get-tuple-element.14), channel_id=1, source_target_pairs={{0,448},{1,65},{16,464},{17,81},{32,480},{33,97},{48,496},{49,113}... | collective-permute-start | bytes 491528 | tf_op jit(solution)/shard_map/ppermute | solution.py:47
  104.8 0.1 fusion
  104.9 0.1 select_reduce_fusion
  105.0 4.4 %collective-permute-start.8 = (bf16[128,640]{1,0:T(8,128)(2,1)S(1)}, bf16[128,640]{1,0:T(8,128)(2,1)S(1)}, u32[]{:S(2)}, u32[]{:S(2)}) collective-permute-start(bf16[128,640]{1,0:T(8,128)(2,1)S(1)} %get-tuple-element.16), channel_id=1, source_target_pairs={{0,48},{1,497},{16,32},{17,481},{32,80},{33,17},{48,64},{49,1},{64... | collective-permute-start | bytes 491528 | tf_op jit(solution)/shard_map/ppermute | solution.py:47
  109.4 1.9 %collective-permute-start.9 = (bf16[128,640]{1,0:T(8,128)(2,1)S(1)}, bf16[128,640]{1,0:T(8,128)(2,1)S(1)}, u32[]{:S(2)}, u32[]{:S(2)}) collective-permute-start(bf16[128,640]{1,0:T(8,128)(2,1)S(1)} %get-tuple-element.17), channel_id=1, source_target_pairs={{0,32},{1,481},{16,48},{17,497},{32,64},{33,1},{48,80},{49,17},{64... | collective-permute-start | bytes 491528 | tf_op jit(solution)/shard_map/ppermute | solution.py:47
  111.3 2.6 %collective-permute-start.10 = (bf16[128,640]{1,0:T(8,128)(2,1)S(1)}, bf16[128,640]{1,0:T(8,128)(2,1)S(1)}, u32[]{:S(2)}, u32[]{:S(2)}) collective-permute-start(bf16[128,640]{1,0:T(8,128)(2,1)S(1)} %get-tuple-element.18), channel_id=1, source_target_pairs={{0,16},{1,17},{16,0},{17,1},{32,48},{33,49},{48,32},{49,33},{64,80... | collective-permute-start | bytes 491528 | tf_op jit(solution)/shard_map/ppermute | solution.py:47
  113.9 0.7 shard_map.39
  114.7 0.0 collective-permute-done.6
  114.7 5.5 %collective-permute-start.7 = (bf16[128,640]{1,0:T(8,128)(2,1)S(1)}, bf16[128,640]{1,0:T(8,128)(2,1)S(1)}, u32[]{:S(2)}, u32[]{:S(2)}) collective-permute-start(bf16[128,640]{1,0:T(8,128)(2,1)S(1)} %add_convert_fusion.1), channel_id=1, source_target_pairs={{0,464},{1,81},{16,448},{17,65},{32,496},{33,113},{48,480},{49,97}... | collective-permute-start | bytes 491528 | tf_op jit(solution)/shard_map/ppermute | solution.py:47
  120.3 0.0 collective-permute-done.8
  120.3 0.0 collective-permute-done.9
  120.3 0.0 collective-permute-done.10
  120.3 0.1 add_convert_fusion
  120.4 2.9 %collective-permute-start.11 = (bf16[128,640]{1,0:T(8,128)(2,1)S(1)}, bf16[128,640]{1,0:T(8,128)(2,1)S(1)}, u32[]{:S(2)}, u32[]{:S(2)}) collective-permute-start(bf16[128,640]{1,0:T(8,128)(2,1)S(1)} %add_convert_fusion), channel_id=1, source_target_pairs={{0,96},{1,417},{16,112},{17,433},{32,128},{33,449},{48,144},{49,46... | collective-permute-start | bytes 491528 | tf_op jit(solution)/shard_map/ppermute | solution.py:47
  123.3 6.1 %collective-permute-done.7 = bf16[128,640]{1,0:T(8,128)(2,1)S(1)} collective-permute-done((bf16[128,640]{1,0:T(8,128)(2,1)S(1)}, bf16[128,640]{1,0:T(8,128)(2,1)S(1)}, u32[]{:S(2)}, u32[]{:S(2)}) %collective-permute-start.7) | collective-permute-done | bytes 163872 | tf_op jit(solution)/shard_map/ppermute | solution.py:47
  129.4 5.2 %collective-permute-done.11 = bf16[128,640]{1,0:T(8,128)(2,1)S(1)} collective-permute-done((bf16[128,640]{1,0:T(8,128)(2,1)S(1)}, bf16[128,640]{1,0:T(8,128)(2,1)S(1)}, u32[]{:S(2)}, u32[]{:S(2)}) %collective-permute-start.11) | collective-permute-done | bytes 163872 | tf_op jit(solution)/shard_map/ppermute | solution.py:47
  134.6 0.8 multiply_convert_fusion
  (7 shorter events, 0.1 us)
Async XLA Ops:
  0.0 1.0 copy-start.3
  1.1 35.9 %collective-permute-start.2 = (bf16[128,1664]{1,0:T(8,128)(2,1)S(1)}, bf16[128,1664]{1,0:T(8,128)(2,1)S(1)}, u32[]{:S(2)}, u32[]{:S(2)}) collective-permute-start(bf16[128,1664]{1,0:T(8,128)(2,1)S(1)} %constant_dynamic-update-slice_fusion.refs_0_.refs_1_), channel_id=1, source_target_pairs={{96,0},{417,1},{112,16},{433,17},{128,32},{449,33},{144,48},{465,4... | collective-permute-start | bytes 1277960 | tf_op jit(solution)/shard_map/ppermute | solution.py:43
  13.3 32.7 %collective-permute-start = (bf16[128,1664]{1,0:T(8,128)(2,1)S(1)}, bf16[128,1664]{1,0:T(8,128)(2,1)S(1)}, u32[]{:S(2)}, u32[]{:S(2)}) collective-permute-start(bf16[128,1664]{1,0:T(8,128)(2,1)S(1)} %constant_dynamic-update-slice_fusion.refs_0_.refs_1_), channel_id=1, source_target_pairs={{464,0},{81,1},{448,16},{65,17},{496,32},{113,33},{480,48},{97,49}... | collective-permute-start | bytes 1277960 | tf_op jit(solution)/shard_map/ppermute | solution.py:43
  36.9 15.8 %collective-permute-start.5 = (bf16[128,1664]{1,0:T(8,128)(2,1)S(1)}, bf16[128,1664]{1,0:T(8,128)(2,1)S(1)}, u32[]{:S(2)}, u32[]{:S(2)}) collective-permute-start(bf16[128,1664]{1,0:T(8,128)(2,1)S(1)} %collective-permute-done.2.refs_3_.refs_4_), channel_id=1, source_target_pairs={{48,0},{497,1},{32,16},{481,17},{80,32},{17,33},{64,48},{1,49},{11... | collective-permute-start | bytes 1277960 | tf_op jit(solution)/shard_map/ppermute | solution.py:43
  40.2 19.4 %collective-permute-start.4 = (bf16[128,1664]{1,0:T(8,128)(2,1)S(1)}, bf16[128,1664]{1,0:T(8,128)(2,1)S(1)}, u32[]{:S(2)}, u32[]{:S(2)}) collective-permute-start(bf16[128,1664]{1,0:T(8,128)(2,1)S(1)} %collective-permute-done.2.refs_3_.refs_4_), channel_id=1, source_target_pairs={{32,0},{481,1},{48,16},{497,17},{64,32},{1,33},{80,48},{17,49},{96... | collective-permute-start | bytes 1277960 | tf_op jit(solution)/shard_map/ppermute | solution.py:43
  44.1 15.6 %collective-permute-start.3 = (bf16[128,1664]{1,0:T(8,128)(2,1)S(1)}, bf16[128,1664]{1,0:T(8,128)(2,1)S(1)}, u32[]{:S(2)}, u32[]{:S(2)}) collective-permute-start(bf16[128,1664]{1,0:T(8,128)(2,1)S(1)} %collective-permute-done.2.refs_3_.refs_4_), channel_id=1, source_target_pairs={{16,0},{17,1},{0,16},{1,17},{48,32},{49,33},{32,48},{33,49},{80,64... | collective-permute-start | bytes 1277960 | tf_op jit(solution)/shard_map/ppermute | solution.py:43
  46.0 13.7 %collective-permute-start.1 = (bf16[128,1664]{1,0:T(8,128)(2,1)S(1)}, bf16[128,1664]{1,0:T(8,128)(2,1)S(1)}, u32[]{:S(2)}, u32[]{:S(2)}) collective-permute-start(bf16[128,1664]{1,0:T(8,128)(2,1)S(1)} %collective-permute-done.refs_1_.refs_2_), channel_id=1, source_target_pairs={{448,0},{65,1},{464,16},{81,17},{480,32},{97,33},{496,48},{113,49}... | collective-permute-start | bytes 1277960 | tf_op jit(solution)/shard_map/ppermute | solution.py:43
  62.0 0.8 copy-start
  62.8 0.8 copy-start.2
  63.6 17.5 %all-to-all-start = ((bf16[8,288,128]{2,1,0:T(8,128)(2,1)}), bf16[8,288,128]{2,1,0:T(8,128)(2,1)S(1)}, u32[]{:S(2)}, u32[]{:S(2)}) async-start(bf16[8,288,128]{2,1,0:T(8,128)(2,1)} %copy-done.2), calls=%async_computation | async-start | bytes 1179648 | tf_op jit(solution)/shard_map/all_to_all | solution.py:175
  70.6 0.7 copy-start.4
  82.6 14.0 %all-to-all-start.1 = ((bf16[8,288,128]{2,1,0:T(8,128)(2,1)}), bf16[8,288,128]{2,1,0:T(8,128)(2,1)S(1)}, u32[]{:S(2)}, u32[]{:S(2)}) async-start(bf16[8,288,128]{2,1,0:T(8,128)(2,1)} %shard_map.38), calls=%async_computation.1 | async-start | bytes 1179648 | tf_op jit(solution)/shard_map/all_to_all | solution.py:184
  96.6 1.0 copy-start.1
  98.3 16.4 %collective-permute-start.6 = (bf16[128,640]{1,0:T(8,128)(2,1)S(1)}, bf16[128,640]{1,0:T(8,128)(2,1)S(1)}, u32[]{:S(2)}, u32[]{:S(2)}) collective-permute-start(bf16[128,640]{1,0:T(8,128)(2,1)S(1)} %get-tuple-element.14), channel_id=1, source_target_pairs={{0,448},{1,65},{16,464},{17,81},{32,480},{33,97},{48,496},{49,113}... | collective-permute-start | bytes 491528 | tf_op jit(solution)/shard_map/ppermute | solution.py:47
  105.0 15.3 %collective-permute-start.8 = (bf16[128,640]{1,0:T(8,128)(2,1)S(1)}, bf16[128,640]{1,0:T(8,128)(2,1)S(1)}, u32[]{:S(2)}, u32[]{:S(2)}) collective-permute-start(bf16[128,640]{1,0:T(8,128)(2,1)S(1)} %get-tuple-element.16), channel_id=1, source_target_pairs={{0,48},{1,497},{16,32},{17,481},{32,80},{33,17},{48,64},{49,1},{64... | collective-permute-start | bytes 491528 | tf_op jit(solution)/shard_map/ppermute | solution.py:47
  109.4 10.9 %collective-permute-start.9 = (bf16[128,640]{1,0:T(8,128)(2,1)S(1)}, bf16[128,640]{1,0:T(8,128)(2,1)S(1)}, u32[]{:S(2)}, u32[]{:S(2)}) collective-permute-start(bf16[128,640]{1,0:T(8,128)(2,1)S(1)} %get-tuple-element.17), channel_id=1, source_target_pairs={{0,32},{1,481},{16,48},{17,497},{32,64},{33,1},{48,80},{49,17},{64... | collective-permute-start | bytes 491528 | tf_op jit(solution)/shard_map/ppermute | solution.py:47
  111.3 9.0 %collective-permute-start.10 = (bf16[128,640]{1,0:T(8,128)(2,1)S(1)}, bf16[128,640]{1,0:T(8,128)(2,1)S(1)}, u32[]{:S(2)}, u32[]{:S(2)}) collective-permute-start(bf16[128,640]{1,0:T(8,128)(2,1)S(1)} %get-tuple-element.18), channel_id=1, source_target_pairs={{0,16},{1,17},{16,0},{17,1},{32,48},{33,49},{48,32},{49,33},{64,80... | collective-permute-start | bytes 491528 | tf_op jit(solution)/shard_map/ppermute | solution.py:47
  114.7 14.6 %collective-permute-start.7 = (bf16[128,640]{1,0:T(8,128)(2,1)S(1)}, bf16[128,640]{1,0:T(8,128)(2,1)S(1)}, u32[]{:S(2)}, u32[]{:S(2)}) collective-permute-start(bf16[128,640]{1,0:T(8,128)(2,1)S(1)} %add_convert_fusion.1), channel_id=1, source_target_pairs={{0,464},{1,81},{16,448},{17,65},{32,496},{33,113},{48,480},{49,97}... | collective-permute-start | bytes 491528 | tf_op jit(solution)/shard_map/ppermute | solution.py:47
  120.4 14.2 %collective-permute-start.11 = (bf16[128,640]{1,0:T(8,128)(2,1)S(1)}, bf16[128,640]{1,0:T(8,128)(2,1)S(1)}, u32[]{:S(2)}, u32[]{:S(2)}) collective-permute-start(bf16[128,640]{1,0:T(8,128)(2,1)S(1)} %add_convert_fusion), channel_id=1, source_target_pairs={{0,96},{1,417},{16,112},{17,433},{32,128},{33,449},{48,144},{49,46... | collective-permute-start | bytes 491528 | tf_op jit(solution)/shard_map/ppermute | solution.py:47

commit v4 on v3

--- a/solution.py
+++ b/solution.py
@@ -11,16 +11,16 @@
 ROW = ("z", "xl", "seq")
 NZ, NX, NSEQ, NT = 16, 2, 2, 8
 
-ELEMENTS = ((0, 0), (-2, 1), (-4, 1), (3, 0), (3, 1), (4, 0), (4, 1))
-FIRST = ((1, 0, (-2, 1)), (3, 0, (3, 0)))
-SECOND = ((2, 1, (-2, 0)), (6, 3, (1, 1)), (5, 3, (1, 0)), (4, 3, (0, 1)))
+ELEMENTS = ((0, 0), (1, 0), (0, 1), (-3, 0), (1, 1), (2, 0), (2, 1), (-6, 0))
+FIRST = ((3, 0, (-3, 0)), (1, 0, (1, 0)), (2, 0, (0, 1)))
+SECOND = ((7, 3, (-3, 0)), (5, 1, (1, 0)), (6, 1, (1, 1)), (4, 1, (0, 1)))
 TILES = (
-    (0, 0), (0, 1), (0, 3), (0, 4), (0, 5), (0, 6),
-    (1, 2), (1, 3), (1, 4), (1, 5), (1, 6),
-    (2, 3), (2, 4), (2, 5), (2, 6),
-    (3, 4), (3, 5), (3, 6),
+    (0, 0), (0, 1), (0, 2), (0, 3), (0, 5), (0, 6),
+    (1, 2),
+    (3, 1), (3, 2), (3, 4), (3, 5), (3, 6),
+    (7, 0), (7, 1), (7, 2), (7, 4), (7, 5), (7, 6),
 )
-ONE_SIDED = ((0, 0), (2, 5), (2, 6), (3, 4))
+ONE_SIDED = ((0, 0), (0, 2), (7, 5), (7, 6))
 F32, BF16 = jnp.float32, jnp.bfloat16
 
 
@@ -183,34 +183,30 @@
     )
     tiles = lax.all_to_all(copies, TENSOR, 0, 0)
 
-    far = [e for e, _, _ in SECOND]
-    near = [0] + [e for e, _, _ in FIRST]
+    far = [7, 3, 6, 5, 4, 1, 2]
     block = 2 * rows * rows * ds
     given = call(
         lambda *refs: gradient_kernel(far, *refs),
         [jax.ShapeDtypeStruct((rows, ds), BF16)] * len(far),
-        14 * block,
+        26 * block,
         tiles,
         *blocks,
     )
-    kept = call(
-        lambda *refs: gradient_kernel(near, *refs),
-        [jax.ShapeDtypeStruct((rows, ds), F32)] * len(near),
-        18 * block,
+    total = call(
+        lambda *refs: gradient_kernel([0], *refs),
+        jax.ShapeDtypeStruct((rows, ds), F32),
+        6 * block,
         tiles,
         *blocks,
     )
-    sums = dict(zip(near, kept, strict=True))
-    for (_, target, step), value in zip(SECOND, given, strict=True):
-        sums[target] = sums[target] + give(value, step).astype(F32)
-    for element, target, step in FIRST:
-        sums[target] = sums[target] + give(sums[element].astype(BF16), step).astype(F32)
+    for e, value in zip(far, given, strict=True):
+        total = total + give(value, ELEMENTS[e]).astype(F32)
 
     r = starts[0] + jnp.arange(rows, dtype=jnp.int32)
     segment = jnp.sum((r[:, None] >= ends[None, :-1]).astype(jnp.int32), axis=1)
     index = jnp.arange(counts.shape[0], dtype=jnp.int32)
     length = jnp.sum(jnp.where(segment[:, None] == index[None, :], counts[None, :], 0), axis=1)
-    return (sums[0] * lax.rsqrt(length.astype(F32))[:, None]).astype(BF16)
+    return (total * lax.rsqrt(length.astype(F32))[:, None]).astype(BF16)
 
 
 def solution(mesh):

time: 136 us -> 143 us (1.051)
  the two profiles are of different devices: /device:TPU:2 before, /device:TPU:1 now
where the time goes in v4:
time: 143 us; the launch traced here: 142 us
  starting transfers between devices  70.5 us (49%)
  waiting for transfers between devices  57.3 us (40%)
  local copies, waits for them, and re-layouts  8.89 us (6%)
  Pallas kernels  4.32 us (3%)
    ppermute x7, starting transfers between devices, fetch(): return lax.ppermute(block, ROW, moves(step, False))  32.7 us
    ppermute x7, waiting for transfers between devices, fetch(): return lax.ppermute(block, ROW, moves(step, False))  28.4 us
    ppermute x7, starting transfers between devices, give(): return lax.ppermute(block, ROW, moves(step, True))  27.8 us
    ppermute x7, waiting for transfers between devices, give(): return lax.ppermute(block, ROW, moves(step, True))  10.7 us
    all_to_all x1, waiting for transfers between devices, on_device(): tiles = lax.all_to_all(copies, TENSOR, 0, 0)  9.83 us
    all_to_all x1, waiting for transfers between devices, on_device(): parts = lax.all_to_all(partial, TENSOR, 0, 0)  8.31 us
    unnamed x17, local copies, waits for them, and re-layouts  6.88 us
    all_to_all x1, starting transfers between devices, on_device(): parts = lax.all_to_all(partial, TENSOR, 0, 0)  6.45 us
  transfers between devices with their start and end apart: 16, of which 9 were waited for; matrix products, arithmetic and copies ran while one was open for 2% of the time, Pallas kernels for 0%

profile of v4, /device:TPU:1, one launch (start us, length us, event | category | flops | bytes accessed | tf_op | source)
XLA Modules:
  0.0 142.4 jit_solution(935282670288077154)
XLA Ops:
  0.0 1.0 constant_dynamic-update-slice_fusion.1
  1.0 0.0 copy-done.6
  1.1 12.8 %collective-permute-start.2 = (bf16[128,1664]{1,0:T(8,128)(2,1)S(1)}, bf16[128,1664]{1,0:T(8,128)(2,1)S(1)}, u32[]{:S(2)}, u32[]{:S(2)}) collective-permute-start(bf16[128,1664]{1,0:T(8,128)(2,1)S(1)} %constant_dynamic-update-slice_fusion.refs_0_.refs_1_), channel_id=1, source_target_pairs={{416,0},{97,1},{432,16},{113,17},{448,32},{129,33},{464,48},{145,4... | collective-permute-start | bytes 1277960 | tf_op jit(solution)/shard_map/ppermute | solution.py:43
  13.9 2.6 %collective-permute-start = (bf16[128,1664]{1,0:T(8,128)(2,1)S(1)}, bf16[128,1664]{1,0:T(8,128)(2,1)S(1)}, u32[]{:S(2)}, u32[]{:S(2)}) collective-permute-start(bf16[128,1664]{1,0:T(8,128)(2,1)S(1)} %constant_dynamic-update-slice_fusion.refs_0_.refs_1_), channel_id=1, source_target_pairs={{32,0},{481,1},{48,16},{497,17},{64,32},{1,33},{80,48},{17,49},{96... | collective-permute-start | bytes 1277960 | tf_op jit(solution)/shard_map/ppermute | solution.py:43
  16.6 3.1 %collective-permute-start.1 = (bf16[128,1664]{1,0:T(8,128)(2,1)S(1)}, bf16[128,1664]{1,0:T(8,128)(2,1)S(1)}, u32[]{:S(2)}, u32[]{:S(2)}) collective-permute-start(bf16[128,1664]{1,0:T(8,128)(2,1)S(1)} %constant_dynamic-update-slice_fusion.refs_0_.refs_1_), channel_id=1, source_target_pairs={{16,0},{17,1},{0,16},{1,17},{48,32},{49,33},{32,48},{33,49},{80,64... | collective-permute-start | bytes 1277960 | tf_op jit(solution)/shard_map/ppermute | solution.py:43
  19.7 11.4 %collective-permute-done.2.refs_3_.refs_4_ = bf16[128,1664]{1,0:T(8,128)(2,1)S(1)} collective-permute-done((bf16[128,1664]{1,0:T(8,128)(2,1)S(1)}, bf16[128,1664]{1,0:T(8,128)(2,1)S(1)}, u32[]{:S(2)}, u32[]{:S(2)}) %collective-permute-start.2) | collective-permute-done | bytes 426016 | tf_op jit(solution)/shard_map/ppermute | solution.py:43
  31.0 7.1 %collective-permute-start.6 = (bf16[128,1664]{1,0:T(8,128)(2,1)S(1)}, bf16[128,1664]{1,0:T(8,128)(2,1)S(1)}, u32[]{:S(2)}, u32[]{:S(2)}) collective-permute-start(bf16[128,1664]{1,0:T(8,128)(2,1)S(1)} %collective-permute-done.2.refs_3_.refs_4_), channel_id=1, source_target_pairs={{416,0},{97,1},{432,16},{113,17},{448,32},{129,33},{464,48},{145,4... | collective-permute-start | bytes 1277960 | tf_op jit(solution)/shard_map/ppermute | solution.py:43
  38.2 0.0 collective-permute-done.refs_1_.refs_2_
  38.2 1.9 %collective-permute-start.5 = (bf16[128,1664]{1,0:T(8,128)(2,1)S(1)}, bf16[128,1664]{1,0:T(8,128)(2,1)S(1)}, u32[]{:S(2)}, u32[]{:S(2)}) collective-permute-start(bf16[128,1664]{1,0:T(8,128)(2,1)S(1)} %collective-permute-done.refs_1_.refs_2_), channel_id=1, source_target_pairs={{48,0},{497,1},{32,16},{481,17},{80,32},{17,33},{64,48},{1,49},{11... | collective-permute-start | bytes 1277960 | tf_op jit(solution)/shard_map/ppermute | solution.py:43
  40.1 1.9 %collective-permute-start.4 = (bf16[128,1664]{1,0:T(8,128)(2,1)S(1)}, bf16[128,1664]{1,0:T(8,128)(2,1)S(1)}, u32[]{:S(2)}, u32[]{:S(2)}) collective-permute-start(bf16[128,1664]{1,0:T(8,128)(2,1)S(1)} %collective-permute-done.refs_1_.refs_2_), channel_id=1, source_target_pairs={{32,0},{481,1},{48,16},{497,17},{64,32},{1,33},{80,48},{17,49},{96... | collective-permute-start | bytes 1277960 | tf_op jit(solution)/shard_map/ppermute | solution.py:43
  42.0 3.1 %collective-permute-start.3 = (bf16[128,1664]{1,0:T(8,128)(2,1)S(1)}, bf16[128,1664]{1,0:T(8,128)(2,1)S(1)}, u32[]{:S(2)}, u32[]{:S(2)}) collective-permute-start(bf16[128,1664]{1,0:T(8,128)(2,1)S(1)} %collective-permute-done.refs_1_.refs_2_), channel_id=1, source_target_pairs={{16,0},{17,1},{0,16},{1,17},{48,32},{49,33},{32,48},{33,49},{80,64... | collective-permute-start | bytes 1277960 | tf_op jit(solution)/shard_map/ppermute | solution.py:43
  45.2 7.6 %collective-permute-done.6.refs_7_.refs_8_ = bf16[128,1664]{1,0:T(8,128)(2,1)S(1)} collective-permute-done((bf16[128,1664]{1,0:T(8,128)(2,1)S(1)}, bf16[128,1664]{1,0:T(8,128)(2,1)S(1)}, u32[]{:S(2)}, u32[]{:S(2)}) %collective-permute-start.6) | collective-permute-done | bytes 426016 | tf_op jit(solution)/shard_map/ppermute | solution.py:43
  52.8 0.2 collective-permute-done.5.refs_6_.refs_7_
  52.9 9.2 %collective-permute-done.4.refs_5_.refs_6_ = bf16[128,1664]{1,0:T(8,128)(2,1)S(1)} collective-permute-done((bf16[128,1664]{1,0:T(8,128)(2,1)S(1)}, bf16[128,1664]{1,0:T(8,128)(2,1)S(1)}, u32[]{:S(2)}, u32[]{:S(2)}) %collective-permute-start.4) | collective-permute-done | bytes 426016 | tf_op jit(solution)/shard_map/ppermute | solution.py:43
  62.2 0.0 collective-permute-done.3.refs_4_.refs_5_
  62.2 2.3 %shard_map.37 = bf16[8,288,128]{2,1,0:T(8,128)(2,1)S(1)} custom-call(bf16[128,1664]{1,0:T(8,128)(2,1)S(1)} %constant_dynamic-update-slice_fusion.refs_0_.refs_1_, bf16[128,1664]{1,0:T(8,128)(2,1)S(1)} %collective-permute-done.refs_1_.refs_2_, bf16[128,1664]{1,0:T(8,128)(2,1)S(1)} %collective-permute-done.1.refs_2_.refs_3_, ...), custom_call_target="tpu_custom_call" | custom-call | flops 981467136 | bytes 3407872 | tf_op jit(solution)/shard_map/pallas_call | solution.py:144
  64.5 0.8 copy-done
  65.3 0.8 copy-done.2
  66.1 0.8 copy-done.5
  66.9 6.5 %all-to-all-start = ((bf16[8,288,128]{2,1,0:T(8,128)(2,1)}), bf16[8,288,128]{2,1,0:T(8,128)(2,1)S(1)}, u32[]{:S(2)}, u32[]{:S(2)}) async-start(bf16[8,288,128]{2,1,0:T(8,128)(2,1)} %copy-done.5), calls=%async_computation | async-start | bytes 1179648 | tf_op jit(solution)/shard_map/all_to_all | solution.py:175
  73.4 0.7 copy-done.7
  74.0 0.2 reduce-window.4
  74.2 0.6 fusion.1
  74.8 1.4 stack.39.where_ref
  76.2 8.3 %all-to-all-done.parts = bf16[8,288,128]{2,1,0:T(8,128)(2,1)S(1)} async-done(((bf16[8,288,128]{2,1,0:T(8,128)(2,1)}), bf16[8,288,128]{2,1,0:T(8,128)(2,1)S(1)}, u32[]{:S(2)}, u32[]{:S(2)}) %all-to-all-start) | async-done | bytes 589856 | tf_op jit(solution)/shard_map/all_to_all | solution.py:175
  84.5 0.6 shard_map.38
  85.2 0.8 copy-done.4
  86.0 3.5 %all-to-all-start.1 = ((bf16[8,288,128]{2,1,0:T(8,128)(2,1)}), bf16[8,288,128]{2,1,0:T(8,128)(2,1)S(1)}, u32[]{:S(2)}, u32[]{:S(2)}) async-start(bf16[8,288,128]{2,1,0:T(8,128)(2,1)} %copy-done.4), calls=%async_computation.1 | async-start | bytes 1179648 | tf_op jit(solution)/shard_map/all_to_all | solution.py:184
  89.5 9.8 %all-to-all-done.1.refs_0_ = bf16[8,288,128]{2,1,0:T(8,128)(2,1)S(1)} async-done(((bf16[8,288,128]{2,1,0:T(8,128)(2,1)}), bf16[8,288,128]{2,1,0:T(8,128)(2,1)S(1)}, u32[]{:S(2)}, u32[]{:S(2)}) %all-to-all-start.1) | async-done | bytes 589856 | tf_op jit(solution)/shard_map/all_to_all | solution.py:184
  99.4 1.0 copy-done.1
  100.4 1.0 copy-done.3
  101.4 0.9 shard_map.40
  102.3 7.3 %collective-permute-start.7 = (bf16[128,640]{1,0:T(8,128)(2,1)S(1)}, bf16[128,640]{1,0:T(8,128)(2,1)S(1)}, u32[]{:S(2)}, u32[]{:S(2)}) collective-permute-start(bf16[128,640]{1,0:T(8,128)(2,1)S(1)} %get-tuple-element.12), channel_id=1, source_target_pairs={{0,320},{1,193},{16,336},{17,209},{32,352},{33,225},{48,368},{49,2... | collective-permute-start | bytes 491528 | tf_op jit(solution)/shard_map/ppermute | solution.py:47
  109.7 2.3 %collective-permute-start.8 = (bf16[128,640]{1,0:T(8,128)(2,1)S(1)}, bf16[128,640]{1,0:T(8,128)(2,1)S(1)}, u32[]{:S(2)}, u32[]{:S(2)}) collective-permute-start(bf16[128,640]{1,0:T(8,128)(2,1)S(1)} %get-tuple-element.13), channel_id=1, source_target_pairs={{0,416},{1,97},{16,432},{17,113},{32,448},{33,129},{48,464},{49,14... | collective-permute-start | bytes 491528 | tf_op jit(solution)/shard_map/ppermute | solution.py:47
  112.0 0.1 fusion
  112.0 0.1 select_reduce_fusion
  112.1 5.5 %collective-permute-start.9 = (bf16[128,640]{1,0:T(8,128)(2,1)S(1)}, bf16[128,640]{1,0:T(8,128)(2,1)S(1)}, u32[]{:S(2)}, u32[]{:S(2)}) collective-permute-start(bf16[128,640]{1,0:T(8,128)(2,1)S(1)} %get-tuple-element.14), channel_id=1, source_target_pairs={{0,80},{1,465},{16,64},{17,449},{32,112},{33,497},{48,96},{49,481}... | collective-permute-start | bytes 491528 | tf_op jit(solution)/shard_map/ppermute | solution.py:47
  117.6 3.0 %collective-permute-start.10 = (bf16[128,640]{1,0:T(8,128)(2,1)S(1)}, bf16[128,640]{1,0:T(8,128)(2,1)S(1)}, u32[]{:S(2)}, u32[]{:S(2)}) collective-permute-start(bf16[128,640]{1,0:T(8,128)(2,1)S(1)} %get-tuple-element.15), channel_id=1, source_target_pairs={{0,64},{1,449},{16,80},{17,465},{32,96},{33,481},{48,112},{49,497}... | collective-permute-start | bytes 491528 | tf_op jit(solution)/shard_map/ppermute | solution.py:47
  120.7 5.2 %collective-permute-start.11 = (bf16[128,640]{1,0:T(8,128)(2,1)S(1)}, bf16[128,640]{1,0:T(8,128)(2,1)S(1)}, u32[]{:S(2)}, u32[]{:S(2)}) collective-permute-start(bf16[128,640]{1,0:T(8,128)(2,1)S(1)} %get-tuple-element.16), channel_id=1, source_target_pairs={{0,48},{1,497},{16,32},{17,481},{32,80},{33,17},{48,64},{49,1},{64... | collective-permute-start | bytes 491528 | tf_op jit(solution)/shard_map/ppermute | solution.py:47
  125.9 0.0 collective-permute-done.7
  125.9 1.9 %collective-permute-start.12 = (bf16[128,640]{1,0:T(8,128)(2,1)S(1)}, bf16[128,640]{1,0:T(8,128)(2,1)S(1)}, u32[]{:S(2)}, u32[]{:S(2)}) collective-permute-start(bf16[128,640]{1,0:T(8,128)(2,1)S(1)} %get-tuple-element.17), channel_id=1, source_target_pairs={{0,32},{1,481},{16,48},{17,497},{32,64},{33,1},{48,80},{49,17},{64... | collective-permute-start | bytes 491528 | tf_op jit(solution)/shard_map/ppermute | solution.py:47
  127.8 2.6 %collective-permute-start.13 = (bf16[128,640]{1,0:T(8,128)(2,1)S(1)}, bf16[128,640]{1,0:T(8,128)(2,1)S(1)}, u32[]{:S(2)}, u32[]{:S(2)}) collective-permute-start(bf16[128,640]{1,0:T(8,128)(2,1)S(1)} %get-tuple-element.18), channel_id=1, source_target_pairs={{0,16},{1,17},{16,0},{17,1},{32,48},{33,49},{48,32},{49,33},{64,80... | collective-permute-start | bytes 491528 | tf_op jit(solution)/shard_map/ppermute | solution.py:47
  130.4 0.4 shard_map.39
  130.8 6.1 %collective-permute-done.10 = bf16[128,640]{1,0:T(8,128)(2,1)S(1)} collective-permute-done((bf16[128,640]{1,0:T(8,128)(2,1)S(1)}, bf16[128,640]{1,0:T(8,128)(2,1)S(1)}, u32[]{:S(2)}, u32[]{:S(2)}) %collective-permute-start.10) | collective-permute-done | bytes 163872 | tf_op jit(solution)/shard_map/ppermute | solution.py:47
  137.0 2.9 %collective-permute-done.11 = bf16[128,640]{1,0:T(8,128)(2,1)S(1)} collective-permute-done((bf16[128,640]{1,0:T(8,128)(2,1)S(1)}, bf16[128,640]{1,0:T(8,128)(2,1)S(1)}, u32[]{:S(2)}, u32[]{:S(2)}) %collective-permute-start.11) | collective-permute-done | bytes 163872 | tf_op jit(solution)/shard_map/ppermute | solution.py:47
  139.9 1.6 %collective-permute-done.12 = bf16[128,640]{1,0:T(8,128)(2,1)S(1)} collective-permute-done((bf16[128,640]{1,0:T(8,128)(2,1)S(1)}, bf16[128,640]{1,0:T(8,128)(2,1)S(1)}, u32[]{:S(2)}, u32[]{:S(2)}) %collective-permute-start.12) | collective-permute-done | bytes 163872 | tf_op jit(solution)/shard_map/ppermute | solution.py:47
  141.6 0.0 collective-permute-done.13
  141.6 0.8 multiply_convert_fusion
  (15 shorter events, 0.1 us)
Async XLA Ops:
  0.0 1.0 copy-start.6
  1.1 30.0 %collective-permute-start.2 = (bf16[128,1664]{1,0:T(8,128)(2,1)S(1)}, bf16[128,1664]{1,0:T(8,128)(2,1)S(1)}, u32[]{:S(2)}, u32[]{:S(2)}) collective-permute-start(bf16[128,1664]{1,0:T(8,128)(2,1)S(1)} %constant_dynamic-update-slice_fusion.refs_0_.refs_1_), channel_id=1, source_target_pairs={{416,0},{97,1},{432,16},{113,17},{448,32},{129,33},{464,48},{145,4... | collective-permute-start | bytes 1277960 | tf_op jit(solution)/shard_map/ppermute | solution.py:43
  13.9 24.3 %collective-permute-start = (bf16[128,1664]{1,0:T(8,128)(2,1)S(1)}, bf16[128,1664]{1,0:T(8,128)(2,1)S(1)}, u32[]{:S(2)}, u32[]{:S(2)}) collective-permute-start(bf16[128,1664]{1,0:T(8,128)(2,1)S(1)} %constant_dynamic-update-slice_fusion.refs_0_.refs_1_), channel_id=1, source_target_pairs={{32,0},{481,1},{48,16},{497,17},{64,32},{1,33},{80,48},{17,49},{96... | collective-permute-start | bytes 1277960 | tf_op jit(solution)/shard_map/ppermute | solution.py:43
  16.6 28.6 %collective-permute-start.1 = (bf16[128,1664]{1,0:T(8,128)(2,1)S(1)}, bf16[128,1664]{1,0:T(8,128)(2,1)S(1)}, u32[]{:S(2)}, u32[]{:S(2)}) collective-permute-start(bf16[128,1664]{1,0:T(8,128)(2,1)S(1)} %constant_dynamic-update-slice_fusion.refs_0_.refs_1_), channel_id=1, source_target_pairs={{16,0},{17,1},{0,16},{1,17},{48,32},{49,33},{32,48},{33,49},{80,64... | collective-permute-start | bytes 1277960 | tf_op jit(solution)/shard_map/ppermute | solution.py:43
  31.0 21.7 %collective-permute-start.6 = (bf16[128,1664]{1,0:T(8,128)(2,1)S(1)}, bf16[128,1664]{1,0:T(8,128)(2,1)S(1)}, u32[]{:S(2)}, u32[]{:S(2)}) collective-permute-start(bf16[128,1664]{1,0:T(8,128)(2,1)S(1)} %collective-permute-done.2.refs_3_.refs_4_), channel_id=1, source_target_pairs={{416,0},{97,1},{432,16},{113,17},{448,32},{129,33},{464,48},{145,4... | collective-permute-start | bytes 1277960 | tf_op jit(solution)/shard_map/ppermute | solution.py:43
  38.2 14.8 %collective-permute-start.5 = (bf16[128,1664]{1,0:T(8,128)(2,1)S(1)}, bf16[128,1664]{1,0:T(8,128)(2,1)S(1)}, u32[]{:S(2)}, u32[]{:S(2)}) collective-permute-start(bf16[128,1664]{1,0:T(8,128)(2,1)S(1)} %collective-permute-done.refs_1_.refs_2_), channel_id=1, source_target_pairs={{48,0},{497,1},{32,16},{481,17},{80,32},{17,33},{64,48},{1,49},{11... | collective-permute-start | bytes 1277960 | tf_op jit(solution)/shard_map/ppermute | solution.py:43
  40.1 22.1 %collective-permute-start.4 = (bf16[128,1664]{1,0:T(8,128)(2,1)S(1)}, bf16[128,1664]{1,0:T(8,128)(2,1)S(1)}, u32[]{:S(2)}, u32[]{:S(2)}) collective-permute-start(bf16[128,1664]{1,0:T(8,128)(2,1)S(1)} %collective-permute-done.refs_1_.refs_2_), channel_id=1, source_target_pairs={{32,0},{481,1},{48,16},{497,17},{64,32},{1,33},{80,48},{17,49},{96... | collective-permute-start | bytes 1277960 | tf_op jit(solution)/shard_map/ppermute | solution.py:43
  42.0 20.2 %collective-permute-start.3 = (bf16[128,1664]{1,0:T(8,128)(2,1)S(1)}, bf16[128,1664]{1,0:T(8,128)(2,1)S(1)}, u32[]{:S(2)}, u32[]{:S(2)}) collective-permute-start(bf16[128,1664]{1,0:T(8,128)(2,1)S(1)} %collective-permute-done.refs_1_.refs_2_), channel_id=1, source_target_pairs={{16,0},{17,1},{0,16},{1,17},{48,32},{49,33},{32,48},{33,49},{80,64... | collective-permute-start | bytes 1277960 | tf_op jit(solution)/shard_map/ppermute | solution.py:43
  64.5 0.8 copy-start
  65.3 0.8 copy-start.2
  66.1 0.8 copy-start.5
  66.9 17.6 %all-to-all-start = ((bf16[8,288,128]{2,1,0:T(8,128)(2,1)}), bf16[8,288,128]{2,1,0:T(8,128)(2,1)S(1)}, u32[]{:S(2)}, u32[]{:S(2)}) async-start(bf16[8,288,128]{2,1,0:T(8,128)(2,1)} %copy-done.5), calls=%async_computation | async-start | bytes 1179648 | tf_op jit(solution)/shard_map/all_to_all | solution.py:175
  73.4 0.7 copy-start.7
  85.2 0.8 copy-start.4
  86.0 13.4 %all-to-all-start.1 = ((bf16[8,288,128]{2,1,0:T(8,128)(2,1)}), bf16[8,288,128]{2,1,0:T(8,128)(2,1)S(1)}, u32[]{:S(2)}, u32[]{:S(2)}) async-start(bf16[8,288,128]{2,1,0:T(8,128)(2,1)} %copy-done.4), calls=%async_computation.1 | async-start | bytes 1179648 | tf_op jit(solution)/shard_map/all_to_all | solution.py:184
  99.4 1.0 copy-start.1
  100.4 1.0 copy-start.3
  102.3 23.5 %collective-permute-start.7 = (bf16[128,640]{1,0:T(8,128)(2,1)S(1)}, bf16[128,640]{1,0:T(8,128)(2,1)S(1)}, u32[]{:S(2)}, u32[]{:S(2)}) collective-permute-start(bf16[128,640]{1,0:T(8,128)(2,1)S(1)} %get-tuple-element.12), channel_id=1, source_target_pairs={{0,320},{1,193},{16,336},{17,209},{32,352},{33,225},{48,368},{49,2... | collective-permute-start | bytes 491528 | tf_op jit(solution)/shard_map/ppermute | solution.py:47
  109.7 18.2 %collective-permute-start.8 = (bf16[128,640]{1,0:T(8,128)(2,1)S(1)}, bf16[128,640]{1,0:T(8,128)(2,1)S(1)}, u32[]{:S(2)}, u32[]{:S(2)}) collective-permute-start(bf16[128,640]{1,0:T(8,128)(2,1)S(1)} %get-tuple-element.13), channel_id=1, source_target_pairs={{0,416},{1,97},{16,432},{17,113},{32,448},{33,129},{48,464},{49,14... | collective-permute-start | bytes 491528 | tf_op jit(solution)/shard_map/ppermute | solution.py:47
  112.1 18.7 %collective-permute-start.9 = (bf16[128,640]{1,0:T(8,128)(2,1)S(1)}, bf16[128,640]{1,0:T(8,128)(2,1)S(1)}, u32[]{:S(2)}, u32[]{:S(2)}) collective-permute-start(bf16[128,640]{1,0:T(8,128)(2,1)S(1)} %get-tuple-element.14), channel_id=1, source_target_pairs={{0,80},{1,465},{16,64},{17,449},{32,112},{33,497},{48,96},{49,481}... | collective-permute-start | bytes 491528 | tf_op jit(solution)/shard_map/ppermute | solution.py:47
  117.6 19.4 %collective-permute-start.10 = (bf16[128,640]{1,0:T(8,128)(2,1)S(1)}, bf16[128,640]{1,0:T(8,128)(2,1)S(1)}, u32[]{:S(2)}, u32[]{:S(2)}) collective-permute-start(bf16[128,640]{1,0:T(8,128)(2,1)S(1)} %get-tuple-element.15), channel_id=1, source_target_pairs={{0,64},{1,449},{16,80},{17,465},{32,96},{33,481},{48,112},{49,497}... | collective-permute-start | bytes 491528 | tf_op jit(solution)/shard_map/ppermute | solution.py:47
  120.7 19.3 %collective-permute-start.11 = (bf16[128,640]{1,0:T(8,128)(2,1)S(1)}, bf16[128,640]{1,0:T(8,128)(2,1)S(1)}, u32[]{:S(2)}, u32[]{:S(2)}) collective-permute-start(bf16[128,640]{1,0:T(8,128)(2,1)S(1)} %get-tuple-element.16), channel_id=1, source_target_pairs={{0,48},{1,497},{16,32},{17,481},{32,80},{33,17},{48,64},{49,1},{64... | collective-permute-start | bytes 491528 | tf_op jit(solution)/shard_map/ppermute | solution.py:47
  125.9 15.7 %collective-permute-start.12 = (bf16[128,640]{1,0:T(8,128)(2,1)S(1)}, bf16[128,640]{1,0:T(8,128)(2,1)S(1)}, u32[]{:S(2)}, u32[]{:S(2)}) collective-permute-start(bf16[128,640]{1,0:T(8,128)(2,1)S(1)} %get-tuple-element.17), channel_id=1, source_target_pairs={{0,32},{1,481},{16,48},{17,497},{32,64},{33,1},{48,80},{49,17},{64... | collective-permute-start | bytes 491528 | tf_op jit(solution)/shard_map/ppermute | solution.py:47
  127.8 13.8 %collective-permute-start.13 = (bf16[128,640]{1,0:T(8,128)(2,1)S(1)}, bf16[128,640]{1,0:T(8,128)(2,1)S(1)}, u32[]{:S(2)}, u32[]{:S(2)}) collective-permute-start(bf16[128,640]{1,0:T(8,128)(2,1)S(1)} %get-tuple-element.18), channel_id=1, source_target_pairs={{0,16},{1,17},{16,0},{17,1},{32,48},{33,49},{48,32},{49,33},{64,80... | collective-permute-start | bytes 491528 | tf_op jit(solution)/shard_map/ppermute | solution.py:47

commit v5 on v3

--- a/solution.py
+++ b/solution.py
@@ -146,7 +146,7 @@
         out_shape=out_shape,
         in_specs=specs,
         out_specs=[vmem] * len(out_shape) if several else vmem,
-        compiler_params=pltpu.CompilerParams(vmem_limit_bytes=40 * 1024 * 1024),
+        compiler_params=pltpu.CompilerParams(vmem_limit_bytes=16 * 1024 * 1024),
         cost_estimate=pl.CostEstimate(flops=flops, bytes_accessed=moved, transcendentals=0),
     )(*operands)
 
@@ -191,14 +191,16 @@
         [jax.ShapeDtypeStruct((rows, ds), BF16)] * len(far),
         14 * block,
         tiles,
-        *blocks,
+        student,
+        *blocks[1:],
     )
     kept = call(
         lambda *refs: gradient_kernel(near, *refs),
         [jax.ShapeDtypeStruct((rows, ds), F32)] * len(near),
         18 * block,
         tiles,
-        *blocks,
+        student,
+        *blocks[1:],
     )
     sums = dict(zip(near, kept, strict=True))
     for (_, target, step), value in zip(SECOND, given, strict=True):

time: 136 us -> 134 us (0.985)
  local copies, waits for them, and re-layouts: 6.22 us -> 4.45 us
    unnamed x11 -> x9, local copies, waits for them, and re-layouts: 4.25 us -> 2.5 us
where the time goes in v5:
time: 134 us
  starting transfers between devices  62.7 us (47%)
  waiting for transfers between devices  59.9 us (45%)
  Pallas kernels  5.19 us (4%)
  local copies, waits for them, and re-layouts  4.45 us (3%)
    ppermute x6, waiting for transfers between devices, fetch(): return lax.ppermute(block, ROW, moves(step, False))  30.4 us
    ppermute x6, starting transfers between devices, fetch(): return lax.ppermute(block, ROW, moves(step, False))  28.2 us
    ppermute x6, starting transfers between devices, give(): return lax.ppermute(block, ROW, moves(step, True))  23.9 us
    ppermute x6, waiting for transfers between devices, give(): return lax.ppermute(block, ROW, moves(step, True))  11.3 us
    all_to_all x1, waiting for transfers between devices, on_device(): tiles = lax.all_to_all(copies, TENSOR, 0, 0)  10.5 us
    all_to_all x1, waiting for transfers between devices, on_device(): parts = lax.all_to_all(partial, TENSOR, 0, 0)  7.77 us
    all_to_all x1, starting transfers between devices, on_device(): parts = lax.all_to_all(partial, TENSOR, 0, 0)  6.98 us
    pallas_call x4, Pallas kernels, call(): pl.pallas_call(kernel, out_shape=out_shape, in_specs=specs, out_specs=[vm...  5.19 us
  transfers between devices with their start and end apart: 14, of which 8 were waited for; matrix products, arithmetic and copies ran while one was open for 2% of the time, Pallas kernels for 1%

profile of v5, /device:TPU:2, one launch (start us, length us, event | category | flops | bytes accessed | tf_op | source)
XLA Modules:
  0.0 133.7 jit_solution(5726794697562523329)
XLA Ops:
  0.0 0.0 copy-start.2
  0.0 1.0 constant_dynamic-update-slice_fusion.1
  1.0 0.0 copy-done.2
  1.1 12.3 %collective-permute-start.2 = (bf16[128,1664]{1,0:T(8,128)(2,1)S(1)}, bf16[128,1664]{1,0:T(8,128)(2,1)S(1)}, u32[]{:S(2)}, u32[]{:S(2)}) collective-permute-start(bf16[128,1664]{1,0:T(8,128)(2,1)S(1)} %constant_dynamic-update-slice_fusion.refs_0_), channel_id=1, source_target_pairs={{96,0},{417,1},{112,16},{433,17},{128,32},{449,33},{144,48},{465,4... | collective-permute-start | bytes 1277960 | tf_op jit(solution)/shard_map/ppermute | solution.py:43
  13.3 3.4 %collective-permute-start = (bf16[128,1664]{1,0:T(8,128)(2,1)S(1)}, bf16[128,1664]{1,0:T(8,128)(2,1)S(1)}, u32[]{:S(2)}, u32[]{:S(2)}) collective-permute-start(bf16[128,1664]{1,0:T(8,128)(2,1)S(1)} %constant_dynamic-update-slice_fusion.refs_0_), channel_id=1, source_target_pairs={{464,0},{81,1},{448,16},{65,17},{496,32},{113,33},{480,48},{97,49}... | collective-permute-start | bytes 1277960 | tf_op jit(solution)/shard_map/ppermute | solution.py:43
  16.7 20.2 %collective-permute-done.2.refs_3_.refs_4_ = bf16[128,1664]{1,0:T(8,128)(2,1)S(1)} collective-permute-done((bf16[128,1664]{1,0:T(8,128)(2,1)S(1)}, bf16[128,1664]{1,0:T(8,128)(2,1)S(1)}, u32[]{:S(2)}, u32[]{:S(2)}) %collective-permute-start.2) | collective-permute-done | bytes 426016 | tf_op jit(solution)/shard_map/ppermute | solution.py:43
  36.9 3.3 %collective-permute-start.5 = (bf16[128,1664]{1,0:T(8,128)(2,1)S(1)}, bf16[128,1664]{1,0:T(8,128)(2,1)S(1)}, u32[]{:S(2)}, u32[]{:S(2)}) collective-permute-start(bf16[128,1664]{1,0:T(8,128)(2,1)S(1)} %collective-permute-done.2.refs_3_.refs_4_), channel_id=1, source_target_pairs={{48,0},{497,1},{32,16},{481,17},{80,32},{17,33},{64,48},{1,49},{11... | collective-permute-start | bytes 1277960 | tf_op jit(solution)/shard_map/ppermute | solution.py:43
  40.2 3.8 %collective-permute-start.4 = (bf16[128,1664]{1,0:T(8,128)(2,1)S(1)}, bf16[128,1664]{1,0:T(8,128)(2,1)S(1)}, u32[]{:S(2)}, u32[]{:S(2)}) collective-permute-start(bf16[128,1664]{1,0:T(8,128)(2,1)S(1)} %collective-permute-done.2.refs_3_.refs_4_), channel_id=1, source_target_pairs={{32,0},{481,1},{48,16},{497,17},{64,32},{1,33},{80,48},{17,49},{96... | collective-permute-start | bytes 1277960 | tf_op jit(solution)/shard_map/ppermute | solution.py:43
  44.1 1.9 %collective-permute-start.3 = (bf16[128,1664]{1,0:T(8,128)(2,1)S(1)}, bf16[128,1664]{1,0:T(8,128)(2,1)S(1)}, u32[]{:S(2)}, u32[]{:S(2)}) collective-permute-start(bf16[128,1664]{1,0:T(8,128)(2,1)S(1)} %collective-permute-done.2.refs_3_.refs_4_), channel_id=1, source_target_pairs={{16,0},{17,1},{0,16},{1,17},{48,32},{49,33},{32,48},{33,49},{80,64... | collective-permute-start | bytes 1277960 | tf_op jit(solution)/shard_map/ppermute | solution.py:43
  46.0 0.0 collective-permute-done.refs_1_.refs_2_
  46.0 3.5 %collective-permute-start.1 = (bf16[128,1664]{1,0:T(8,128)(2,1)S(1)}, bf16[128,1664]{1,0:T(8,128)(2,1)S(1)}, u32[]{:S(2)}, u32[]{:S(2)}) collective-permute-start(bf16[128,1664]{1,0:T(8,128)(2,1)S(1)} %collective-permute-done.refs_1_.refs_2_), channel_id=1, source_target_pairs={{448,0},{65,1},{464,16},{81,17},{480,32},{97,33},{496,48},{113,49}... | collective-permute-start | bytes 1277960 | tf_op jit(solution)/shard_map/ppermute | solution.py:43
  49.5 3.2 %collective-permute-done.5.refs_6_.refs_7_ = bf16[128,1664]{1,0:T(8,128)(2,1)S(1)} collective-permute-done((bf16[128,1664]{1,0:T(8,128)(2,1)S(1)}, bf16[128,1664]{1,0:T(8,128)(2,1)S(1)}, u32[]{:S(2)}, u32[]{:S(2)}) %collective-permute-start.5) | collective-permute-done | bytes 426016 | tf_op jit(solution)/shard_map/ppermute | solution.py:43
  52.7 6.9 %collective-permute-done.4.refs_5_.refs_6_ = bf16[128,1664]{1,0:T(8,128)(2,1)S(1)} collective-permute-done((bf16[128,1664]{1,0:T(8,128)(2,1)S(1)}, bf16[128,1664]{1,0:T(8,128)(2,1)S(1)}, u32[]{:S(2)}, u32[]{:S(2)}) %collective-permute-start.4) | collective-permute-done | bytes 426016 | tf_op jit(solution)/shard_map/ppermute | solution.py:43
  59.6 0.0 collective-permute-done.3.refs_4_.refs_5_
  59.6 0.1 collective-permute-done.1.refs_2_.refs_3_
  59.7 2.3 %shard_map.37 = bf16[8,288,128]{2,1,0:T(8,128)(2,1)S(1)} custom-call(bf16[128,1664]{1,0:T(8,128)(2,1)S(1)} %constant_dynamic-update-slice_fusion.refs_0_, bf16[128,1664]{1,0:T(8,128)(2,1)S(1)} %collective-permute-done.refs_1_.refs_2_, bf16[128,1664]{1,0:T(8,128)(2,1)S(1)} %collective-permute-done.1.refs_2_.refs_3_, ...), custom_call_target="tpu_custom_call" | custom-call | flops 981467136 | bytes 2981888 | tf_op jit(solution)/shard_map/pallas_call | solution.py:144
  62.0 0.0 copy-start.1
  62.0 0.8 copy-done.1
  62.8 7.0 %all-to-all-start = ((bf16[8,288,128]{2,1,0:T(8,128)(2,1)}), bf16[8,288,128]{2,1,0:T(8,128)(2,1)S(1)}, u32[]{:S(2)}, u32[]{:S(2)}) async-start(bf16[8,288,128]{2,1,0:T(8,128)(2,1)} %copy-done.1), calls=%async_computation | async-start | bytes 1179648 | tf_op jit(solution)/shard_map/all_to_all | solution.py:175
  69.8 0.0 copy-start.3
  69.8 0.7 copy-done.3
  70.5 0.2 reduce-window.4
  70.7 0.6 fusion.1
  71.2 1.4 %stack.35.where_ref = s32[10]{0:T(128)S(1)} concatenate(s32[1]{0:T(128)} %bitcast.1, s32[1]{0:T(128)} %bitcast.2, s32[1]{0:T(128)} %bitcast.3, s32[1]{0:T(128)} %bitcast.4, s32[1]{0:T(128)} %bitcast.5, s32[1]{0:T(128)} %bitcast.6, s32[1]{0:T(128)} %bitcast.7, s32[1]{0:T(128)} %bitcast.8, s32[1]{0:T(128)} %bitcast.9, s32[1]{0:T(128)} %bitcast.10), dimensions={0} | concatenate | bytes 80 | tf_op jit(solution)/shard_map/stack | solution.py:174
  72.6 7.8 %all-to-all-done.parts = bf16[8,288,128]{2,1,0:T(8,128)(2,1)S(1)} async-done(((bf16[8,288,128]{2,1,0:T(8,128)(2,1)}), bf16[8,288,128]{2,1,0:T(8,128)(2,1)S(1)}, u32[]{:S(2)}, u32[]{:S(2)}) %all-to-all-start) | async-done | bytes 589856 | tf_op jit(solution)/shard_map/all_to_all | solution.py:175
  80.4 1.5 %shard_map.38 = bf16[8,288,128]{2,1,0:T(8,128)(2,1)} custom-call(s32[10]{0:T(128)S(1)} %stack.35.where_ref, bf16[8,288,128]{2,1,0:T(8,128)(2,1)S(1)} %all-to-all-done.parts), custom_call_target="tpu_custom_call" | custom-call | flops 294912 | bytes 589864 | tf_op jit(solution)/shard_map/pallas_call | solution.py:144
  81.8 0.0 copy-start
  81.8 3.7 %all-to-all-start.1 = ((bf16[8,288,128]{2,1,0:T(8,128)(2,1)}), bf16[8,288,128]{2,1,0:T(8,128)(2,1)S(1)}, u32[]{:S(2)}, u32[]{:S(2)}) async-start(bf16[8,288,128]{2,1,0:T(8,128)(2,1)} %shard_map.38), calls=%async_computation.1 | async-start | bytes 1179648 | tf_op jit(solution)/shard_map/all_to_all | solution.py:184
  85.5 10.5 %all-to-all-done.1.refs_0_ = bf16[8,288,128]{2,1,0:T(8,128)(2,1)S(1)} async-done(((bf16[8,288,128]{2,1,0:T(8,128)(2,1)}), bf16[8,288,128]{2,1,0:T(8,128)(2,1)S(1)}, u32[]{:S(2)}, u32[]{:S(2)}) %all-to-all-start.1) | async-done | bytes 589856 | tf_op jit(solution)/shard_map/all_to_all | solution.py:184
  96.0 0.0 copy-done
  96.0 0.7 shard_map.40
  96.7 6.5 %collective-permute-start.6 = (bf16[128,640]{1,0:T(8,128)(2,1)S(1)}, bf16[128,640]{1,0:T(8,128)(2,1)S(1)}, u32[]{:S(2)}, u32[]{:S(2)}) collective-permute-start(bf16[128,640]{1,0:T(8,128)(2,1)S(1)} %get-tuple-element.14), channel_id=1, source_target_pairs={{0,448},{1,65},{16,464},{17,81},{32,480},{33,97},{48,496},{49,113}... | collective-permute-start | bytes 491528 | tf_op jit(solution)/shard_map/ppermute | solution.py:47
  103.2 0.1 fusion
  103.2 0.1 select_reduce_fusion
  103.3 4.4 %collective-permute-start.8 = (bf16[128,640]{1,0:T(8,128)(2,1)S(1)}, bf16[128,640]{1,0:T(8,128)(2,1)S(1)}, u32[]{:S(2)}, u32[]{:S(2)}) collective-permute-start(bf16[128,640]{1,0:T(8,128)(2,1)S(1)} %get-tuple-element.16), channel_id=1, source_target_pairs={{0,48},{1,497},{16,32},{17,481},{32,80},{33,17},{48,64},{49,1},{64... | collective-permute-start | bytes 491528 | tf_op jit(solution)/shard_map/ppermute | solution.py:47
  107.7 1.9 %collective-permute-start.9 = (bf16[128,640]{1,0:T(8,128)(2,1)S(1)}, bf16[128,640]{1,0:T(8,128)(2,1)S(1)}, u32[]{:S(2)}, u32[]{:S(2)}) collective-permute-start(bf16[128,640]{1,0:T(8,128)(2,1)S(1)} %get-tuple-element.17), channel_id=1, source_target_pairs={{0,32},{1,481},{16,48},{17,497},{32,64},{33,1},{48,80},{49,17},{64... | collective-permute-start | bytes 491528 | tf_op jit(solution)/shard_map/ppermute | solution.py:47
  109.7 2.6 %collective-permute-start.10 = (bf16[128,640]{1,0:T(8,128)(2,1)S(1)}, bf16[128,640]{1,0:T(8,128)(2,1)S(1)}, u32[]{:S(2)}, u32[]{:S(2)}) collective-permute-start(bf16[128,640]{1,0:T(8,128)(2,1)S(1)} %get-tuple-element.18), channel_id=1, source_target_pairs={{0,16},{1,17},{16,0},{17,1},{32,48},{33,49},{48,32},{49,33},{64,80... | collective-permute-start | bytes 491528 | tf_op jit(solution)/shard_map/ppermute | solution.py:47
  112.3 0.7 shard_map.39
  113.0 0.0 collective-permute-done.6
  113.1 5.6 %collective-permute-start.7 = (bf16[128,640]{1,0:T(8,128)(2,1)S(1)}, bf16[128,640]{1,0:T(8,128)(2,1)S(1)}, u32[]{:S(2)}, u32[]{:S(2)}) collective-permute-start(bf16[128,640]{1,0:T(8,128)(2,1)S(1)} %add_convert_fusion.1), channel_id=1, source_target_pairs={{0,464},{1,81},{16,448},{17,65},{32,496},{33,113},{48,480},{49,97}... | collective-permute-start | bytes 491528 | tf_op jit(solution)/shard_map/ppermute | solution.py:47
  118.7 0.0 collective-permute-done.8
  118.7 0.0 collective-permute-done.9
  118.7 0.0 collective-permute-done.10
  118.7 0.1 add_convert_fusion
  118.8 2.9 %collective-permute-start.11 = (bf16[128,640]{1,0:T(8,128)(2,1)S(1)}, bf16[128,640]{1,0:T(8,128)(2,1)S(1)}, u32[]{:S(2)}, u32[]{:S(2)}) collective-permute-start(bf16[128,640]{1,0:T(8,128)(2,1)S(1)} %add_convert_fusion), channel_id=1, source_target_pairs={{0,96},{1,417},{16,112},{17,433},{32,128},{33,449},{48,144},{49,46... | collective-permute-start | bytes 491528 | tf_op jit(solution)/shard_map/ppermute | solution.py:47
  121.7 6.1 %collective-permute-done.7 = bf16[128,640]{1,0:T(8,128)(2,1)S(1)} collective-permute-done((bf16[128,640]{1,0:T(8,128)(2,1)S(1)}, bf16[128,640]{1,0:T(8,128)(2,1)S(1)}, u32[]{:S(2)}, u32[]{:S(2)}) %collective-permute-start.7) | collective-permute-done | bytes 163872 | tf_op jit(solution)/shard_map/ppermute | solution.py:47
  127.7 5.2 %collective-permute-done.11 = bf16[128,640]{1,0:T(8,128)(2,1)S(1)} collective-permute-done((bf16[128,640]{1,0:T(8,128)(2,1)S(1)}, bf16[128,640]{1,0:T(8,128)(2,1)S(1)}, u32[]{:S(2)}, u32[]{:S(2)}) %collective-permute-start.11) | collective-permute-done | bytes 163872 | tf_op jit(solution)/shard_map/ppermute | solution.py:47
  132.9 0.8 multiply_convert_fusion
  (5 shorter events, 0.1 us)
Async XLA Ops:
  0.0 1.0 copy-start.2
  1.1 35.9 %collective-permute-start.2 = (bf16[128,1664]{1,0:T(8,128)(2,1)S(1)}, bf16[128,1664]{1,0:T(8,128)(2,1)S(1)}, u32[]{:S(2)}, u32[]{:S(2)}) collective-permute-start(bf16[128,1664]{1,0:T(8,128)(2,1)S(1)} %constant_dynamic-update-slice_fusion.refs_0_), channel_id=1, source_target_pairs={{96,0},{417,1},{112,16},{433,17},{128,32},{449,33},{144,48},{465,4... | collective-permute-start | bytes 1277960 | tf_op jit(solution)/shard_map/ppermute | solution.py:43
  13.3 32.7 %collective-permute-start = (bf16[128,1664]{1,0:T(8,128)(2,1)S(1)}, bf16[128,1664]{1,0:T(8,128)(2,1)S(1)}, u32[]{:S(2)}, u32[]{:S(2)}) collective-permute-start(bf16[128,1664]{1,0:T(8,128)(2,1)S(1)} %constant_dynamic-update-slice_fusion.refs_0_), channel_id=1, source_target_pairs={{464,0},{81,1},{448,16},{65,17},{496,32},{113,33},{480,48},{97,49}... | collective-permute-start | bytes 1277960 | tf_op jit(solution)/shard_map/ppermute | solution.py:43
  36.9 15.8 %collective-permute-start.5 = (bf16[128,1664]{1,0:T(8,128)(2,1)S(1)}, bf16[128,1664]{1,0:T(8,128)(2,1)S(1)}, u32[]{:S(2)}, u32[]{:S(2)}) collective-permute-start(bf16[128,1664]{1,0:T(8,128)(2,1)S(1)} %collective-permute-done.2.refs_3_.refs_4_), channel_id=1, source_target_pairs={{48,0},{497,1},{32,16},{481,17},{80,32},{17,33},{64,48},{1,49},{11... | collective-permute-start | bytes 1277960 | tf_op jit(solution)/shard_map/ppermute | solution.py:43
  40.2 19.4 %collective-permute-start.4 = (bf16[128,1664]{1,0:T(8,128)(2,1)S(1)}, bf16[128,1664]{1,0:T(8,128)(2,1)S(1)}, u32[]{:S(2)}, u32[]{:S(2)}) collective-permute-start(bf16[128,1664]{1,0:T(8,128)(2,1)S(1)} %collective-permute-done.2.refs_3_.refs_4_), channel_id=1, source_target_pairs={{32,0},{481,1},{48,16},{497,17},{64,32},{1,33},{80,48},{17,49},{96... | collective-permute-start | bytes 1277960 | tf_op jit(solution)/shard_map/ppermute | solution.py:43
  44.1 15.6 %collective-permute-start.3 = (bf16[128,1664]{1,0:T(8,128)(2,1)S(1)}, bf16[128,1664]{1,0:T(8,128)(2,1)S(1)}, u32[]{:S(2)}, u32[]{:S(2)}) collective-permute-start(bf16[128,1664]{1,0:T(8,128)(2,1)S(1)} %collective-permute-done.2.refs_3_.refs_4_), channel_id=1, source_target_pairs={{16,0},{17,1},{0,16},{1,17},{48,32},{49,33},{32,48},{33,49},{80,64... | collective-permute-start | bytes 1277960 | tf_op jit(solution)/shard_map/ppermute | solution.py:43
  46.0 13.7 %collective-permute-start.1 = (bf16[128,1664]{1,0:T(8,128)(2,1)S(1)}, bf16[128,1664]{1,0:T(8,128)(2,1)S(1)}, u32[]{:S(2)}, u32[]{:S(2)}) collective-permute-start(bf16[128,1664]{1,0:T(8,128)(2,1)S(1)} %collective-permute-done.refs_1_.refs_2_), channel_id=1, source_target_pairs={{448,0},{65,1},{464,16},{81,17},{480,32},{97,33},{496,48},{113,49}... | collective-permute-start | bytes 1277960 | tf_op jit(solution)/shard_map/ppermute | solution.py:43
  62.0 0.8 copy-start.1
  62.8 17.5 %all-to-all-start = ((bf16[8,288,128]{2,1,0:T(8,128)(2,1)}), bf16[8,288,128]{2,1,0:T(8,128)(2,1)S(1)}, u32[]{:S(2)}, u32[]{:S(2)}) async-start(bf16[8,288,128]{2,1,0:T(8,128)(2,1)} %copy-done.1), calls=%async_computation | async-start | bytes 1179648 | tf_op jit(solution)/shard_map/all_to_all | solution.py:175
  69.8 0.7 copy-start.3
  81.8 14.2 %copy-start = (bf16[128,640]{1,0:T(8,128)(2,1)S(1)}, bf16[128,640]{1,0:T(8,128)(2,1)}, u32[]{:S(2)}) copy-start(bf16[128,640]{1,0:T(8,128)(2,1)} %refs_1_.3) | copy-start | bytes 491524
  81.8 14.2 %all-to-all-start.1 = ((bf16[8,288,128]{2,1,0:T(8,128)(2,1)}), bf16[8,288,128]{2,1,0:T(8,128)(2,1)S(1)}, u32[]{:S(2)}, u32[]{:S(2)}) async-start(bf16[8,288,128]{2,1,0:T(8,128)(2,1)} %shard_map.38), calls=%async_computation.1 | async-start | bytes 1179648 | tf_op jit(solution)/shard_map/all_to_all | solution.py:184
  96.7 16.4 %collective-permute-start.6 = (bf16[128,640]{1,0:T(8,128)(2,1)S(1)}, bf16[128,640]{1,0:T(8,128)(2,1)S(1)}, u32[]{:S(2)}, u32[]{:S(2)}) collective-permute-start(bf16[128,640]{1,0:T(8,128)(2,1)S(1)} %get-tuple-element.14), channel_id=1, source_target_pairs={{0,448},{1,65},{16,464},{17,81},{32,480},{33,97},{48,496},{49,113}... | collective-permute-start | bytes 491528 | tf_op jit(solution)/shard_map/ppermute | solution.py:47
  103.3 15.3 %collective-permute-start.8 = (bf16[128,640]{1,0:T(8,128)(2,1)S(1)}, bf16[128,640]{1,0:T(8,128)(2,1)S(1)}, u32[]{:S(2)}, u32[]{:S(2)}) collective-permute-start(bf16[128,640]{1,0:T(8,128)(2,1)S(1)} %get-tuple-element.16), channel_id=1, source_target_pairs={{0,48},{1,497},{16,32},{17,481},{32,80},{33,17},{48,64},{49,1},{64... | collective-permute-start | bytes 491528 | tf_op jit(solution)/shard_map/ppermute | solution.py:47
  107.7 10.9 %collective-permute-start.9 = (bf16[128,640]{1,0:T(8,128)(2,1)S(1)}, bf16[128,640]{1,0:T(8,128)(2,1)S(1)}, u32[]{:S(2)}, u32[]{:S(2)}) collective-permute-start(bf16[128,640]{1,0:T(8,128)(2,1)S(1)} %get-tuple-element.17), channel_id=1, source_target_pairs={{0,32},{1,481},{16,48},{17,497},{32,64},{33,1},{48,80},{49,17},{64... | collective-permute-start | bytes 491528 | tf_op jit(solution)/shard_map/ppermute | solution.py:47
  109.7 9.0 %collective-permute-start.10 = (bf16[128,640]{1,0:T(8,128)(2,1)S(1)}, bf16[128,640]{1,0:T(8,128)(2,1)S(1)}, u32[]{:S(2)}, u32[]{:S(2)}) collective-permute-start(bf16[128,640]{1,0:T(8,128)(2,1)S(1)} %get-tuple-element.18), channel_id=1, source_target_pairs={{0,16},{1,17},{16,0},{17,1},{32,48},{33,49},{48,32},{49,33},{64,80... | collective-permute-start | bytes 491528 | tf_op jit(solution)/shard_map/ppermute | solution.py:47
  113.1 14.6 %collective-permute-start.7 = (bf16[128,640]{1,0:T(8,128)(2,1)S(1)}, bf16[128,640]{1,0:T(8,128)(2,1)S(1)}, u32[]{:S(2)}, u32[]{:S(2)}) collective-permute-start(bf16[128,640]{1,0:T(8,128)(2,1)S(1)} %add_convert_fusion.1), channel_id=1, source_target_pairs={{0,464},{1,81},{16,448},{17,65},{32,496},{33,113},{48,480},{49,97}... | collective-permute-start | bytes 491528 | tf_op jit(solution)/shard_map/ppermute | solution.py:47
  118.8 14.2 %collective-permute-start.11 = (bf16[128,640]{1,0:T(8,128)(2,1)S(1)}, bf16[128,640]{1,0:T(8,128)(2,1)S(1)}, u32[]{:S(2)}, u32[]{:S(2)}) collective-permute-start(bf16[128,640]{1,0:T(8,128)(2,1)S(1)} %add_convert_fusion), channel_id=1, source_target_pairs={{0,96},{1,417},{16,112},{17,433},{32,128},{33,449},{48,144},{49,46... | collective-permute-start | bytes 491528 | tf_op jit(solution)/shard_map/ppermute | solution.py:47

commit v6 on v5

--- a/solution.py
+++ b/solution.py
@@ -159,6 +159,16 @@
     z, x, s = lax.axis_index("z"), lax.axis_index("xl"), lax.axis_index("seq")
 
     blocks = gather(jnp.concatenate([student, teacher], axis=1))
+    ends = jnp.cumsum(counts)
+    sign = 1 - 2 * s
+    starts = [(((z + sign * ez) % NZ) * NX + (x ^ ex)) * rows for ez, ex in ELEMENTS]
+    where = jnp.stack([ends[0], ends[1], lax.axis_index(TENSOR)] + starts).astype(jnp.int32)
+    r = starts[0] + jnp.arange(rows, dtype=jnp.int32)
+    segment = jnp.sum((r[:, None] >= ends[None, :-1]).astype(jnp.int32), axis=1)
+    index = jnp.arange(counts.shape[0], dtype=jnp.int32)
+    length = jnp.sum(jnp.where(segment[:, None] == index[None, :], counts[None, :], 0), axis=1)
+    scale = lax.rsqrt(length.astype(F32))
+    where, scale, *blocks = lax.optimization_barrier((where, scale, *blocks))
     partial = call(
         lambda *refs: gram_kernel(
             ds, 1.0 / math.sqrt(ds * NT), 1.0 / math.sqrt(dt * NT), *refs
@@ -168,10 +178,6 @@
         *blocks,
     )
 
-    ends = jnp.cumsum(counts)
-    sign = 1 - 2 * s
-    starts = [(((z + sign * ez) % NZ) * NX + (x ^ ex)) * rows for ez, ex in ELEMENTS]
-    where = jnp.stack([ends[0], ends[1], lax.axis_index(TENSOR)] + starts).astype(jnp.int32)
     parts = lax.all_to_all(partial, TENSOR, 0, 0)
     copies = call(
         mask_kernel,
@@ -208,11 +214,7 @@
     for element, target, step in FIRST:
         sums[target] = sums[target] + give(sums[element].astype(BF16), step).astype(F32)
 
-    r = starts[0] + jnp.arange(rows, dtype=jnp.int32)
-    segment = jnp.sum((r[:, None] >= ends[None, :-1]).astype(jnp.int32), axis=1)
-    index = jnp.arange(counts.shape[0], dtype=jnp.int32)
-    length = jnp.sum(jnp.where(segment[:, None] == index[None, :], counts[None, :], 0), axis=1)
-    return (sums[0] * lax.rsqrt(length.astype(F32))[:, None]).astype(BF16)
+    return (sums[0] * scale[:, None]).astype(BF16)
 
 
 def solution(mesh):

time: 134 us -> 131 us (0.978)
  blocking collectives: 0 us -> 30.6 us
  waiting for transfers between devices: 59.9 us -> 38.5 us
  starting transfers between devices: 62.7 us -> 52 us
    all_to_all x0 -> x2, blocking collectives: none -> 30.6 us  [the longest x1 17.4 us: on_device(): parts = lax.all_to_all(partial, TENSOR, 0, 0)]
    all_to_all x2 -> x0, waiting for transfers between devices: 18.2 us -> none  [the longest x1 10.5 us: on_device(): tiles = lax.all_to_all(copies, TENSOR, 0, 0)]
    all_to_all x2 -> x0, starting transfers between devices: 10.6 us -> none  [the longest x1 6.98 us: on_device(): parts = lax.all_to_all(partial, TENSOR, 0, 0)]
    ppermute x6, waiting for transfers between devices: 30.4 us -> 27.3 us  [fetch(): return lax.ppermute(block, ROW, moves(step, False))]
  transfers between devices with their start and end apart: 14 -> 12, of which waited for: 8 -> 6; matrix products, arithmetic and copies ran while one was open for 2% -> 2% of each run, Pallas kernels for 1% -> 1%
where the time goes in v6:
time: 131 us
  starting transfers between devices  52 us (40%)
  waiting for transfers between devices  38.5 us (29%)
  blocking collectives  30.6 us (23%)
  Pallas kernels  4.37 us (3%)
  local copies, waits for them, and re-layouts  3.65 us (3%)
    ppermute x6, starting transfers between devices, fetch(): return lax.ppermute(block, ROW, moves(step, False))  28.2 us
    ppermute x6, waiting for transfers between devices, fetch(): return lax.ppermute(block, ROW, moves(step, False))  27.3 us
    ppermute x6, starting transfers between devices, give(): return lax.ppermute(block, ROW, moves(step, True))  23.8 us
    all_to_all x1, blocking collectives, on_device(): parts = lax.all_to_all(partial, TENSOR, 0, 0)  17.4 us
    all_to_all x1, blocking collectives, on_device(): tiles = lax.all_to_all(copies, TENSOR, 0, 0)  13.2 us
    ppermute x6, waiting for transfers between devices, give(): return lax.ppermute(block, ROW, moves(step, True))  11.2 us
    pallas_call x4, Pallas kernels, call(): pl.pallas_call(kernel, out_shape=out_shape, in_specs=specs, out_specs=[vm...  4.37 us
  transfers between devices with their start and end apart: 12, of which 6 were waited for; matrix products, arithmetic and copies ran while one was open for 2% of the time, Pallas kernels for 1%

profile of v6, /device:TPU:2, one launch (start us, length us, event | category | flops | bytes accessed | tf_op | source)
XLA Modules:
  0.0 130.8 jit_solution(12912882161805093558)
XLA Ops:
  0.0 0.0 copy-start.1
  0.0 1.0 constant_dynamic-update-slice_fusion.1
  1.0 0.0 copy-done.1
  1.1 12.3 %collective-permute-start.2 = (bf16[128,1664]{1,0:T(8,128)(2,1)S(1)}, bf16[128,1664]{1,0:T(8,128)(2,1)S(1)}, u32[]{:S(2)}, u32[]{:S(2)}) collective-permute-start(bf16[128,1664]{1,0:T(8,128)(2,1)S(1)} %constant_dynamic-update-slice_fusion.refs_0_), channel_id=1, source_target_pairs={{96,0},{417,1},{112,16},{433,17},{128,32},{449,33},{144,48},{465,4... | collective-permute-start | bytes 1277960 | tf_op jit(solution)/shard_map/ppermute | solution.py:43
  13.3 3.4 %collective-permute-start = (bf16[128,1664]{1,0:T(8,128)(2,1)S(1)}, bf16[128,1664]{1,0:T(8,128)(2,1)S(1)}, u32[]{:S(2)}, u32[]{:S(2)}) collective-permute-start(bf16[128,1664]{1,0:T(8,128)(2,1)S(1)} %constant_dynamic-update-slice_fusion.refs_0_), channel_id=1, source_target_pairs={{464,0},{81,1},{448,16},{65,17},{496,32},{113,33},{480,48},{97,49}... | collective-permute-start | bytes 1277960 | tf_op jit(solution)/shard_map/ppermute | solution.py:43
  16.8 0.0 copy-start.2
  16.8 0.6 copy-done.2
  17.5 0.2 reduce-window.4
  17.6 0.6 fusion.1
  18.2 1.4 %stack.35.where_ref = s32[10]{0:T(128)S(1)} concatenate(s32[1]{0:T(128)} %bitcast.1, s32[1]{0:T(128)} %bitcast.2, s32[1]{0:T(128)} %bitcast.3, s32[1]{0:T(128)} %bitcast.4, s32[1]{0:T(128)} %bitcast.5, s32[1]{0:T(128)} %bitcast.6, s32[1]{0:T(128)} %bitcast.7, s32[1]{0:T(128)} %bitcast.8, s32[1]{0:T(128)} %bitcast.9, s32[1]{0:T(128)} %bitcast.10), dimensions={0} | concatenate | bytes 80 | tf_op jit(solution)/shard_map/stack | solution.py:165
  19.6 17.3 %collective-permute-done.2.refs_3_.refs_4_ = bf16[128,1664]{1,0:T(8,128)(2,1)S(1)} collective-permute-done((bf16[128,1664]{1,0:T(8,128)(2,1)S(1)}, bf16[128,1664]{1,0:T(8,128)(2,1)S(1)}, u32[]{:S(2)}, u32[]{:S(2)}) %collective-permute-start.2) | collective-permute-done | bytes 426016 | tf_op jit(solution)/shard_map/ppermute | solution.py:43
  36.9 3.3 %collective-permute-start.5 = (bf16[128,1664]{1,0:T(8,128)(2,1)S(1)}, bf16[128,1664]{1,0:T(8,128)(2,1)S(1)}, u32[]{:S(2)}, u32[]{:S(2)}) collective-permute-start(bf16[128,1664]{1,0:T(8,128)(2,1)S(1)} %collective-permute-done.2.refs_3_.refs_4_), channel_id=1, source_target_pairs={{48,0},{497,1},{32,16},{481,17},{80,32},{17,33},{64,48},{1,49},{11... | collective-permute-start | bytes 1277960 | tf_op jit(solution)/shard_map/ppermute | solution.py:43
  40.2 3.8 %collective-permute-start.4 = (bf16[128,1664]{1,0:T(8,128)(2,1)S(1)}, bf16[128,1664]{1,0:T(8,128)(2,1)S(1)}, u32[]{:S(2)}, u32[]{:S(2)}) collective-permute-start(bf16[128,1664]{1,0:T(8,128)(2,1)S(1)} %collective-permute-done.2.refs_3_.refs_4_), channel_id=1, source_target_pairs={{32,0},{481,1},{48,16},{497,17},{64,32},{1,33},{80,48},{17,49},{96... | collective-permute-start | bytes 1277960 | tf_op jit(solution)/shard_map/ppermute | solution.py:43
  44.1 1.9 %collective-permute-start.3 = (bf16[128,1664]{1,0:T(8,128)(2,1)S(1)}, bf16[128,1664]{1,0:T(8,128)(2,1)S(1)}, u32[]{:S(2)}, u32[]{:S(2)}) collective-permute-start(bf16[128,1664]{1,0:T(8,128)(2,1)S(1)} %collective-permute-done.2.refs_3_.refs_4_), channel_id=1, source_target_pairs={{16,0},{17,1},{0,16},{1,17},{48,32},{49,33},{32,48},{33,49},{80,64... | collective-permute-start | bytes 1277960 | tf_op jit(solution)/shard_map/ppermute | solution.py:43
  46.0 0.0 collective-permute-done.refs_1_.refs_2_
  46.0 3.5 %collective-permute-start.1 = (bf16[128,1664]{1,0:T(8,128)(2,1)S(1)}, bf16[128,1664]{1,0:T(8,128)(2,1)S(1)}, u32[]{:S(2)}, u32[]{:S(2)}) collective-permute-start(bf16[128,1664]{1,0:T(8,128)(2,1)S(1)} %collective-permute-done.refs_1_.refs_2_), channel_id=1, source_target_pairs={{448,0},{65,1},{464,16},{81,17},{480,32},{97,33},{496,48},{113,49}... | collective-permute-start | bytes 1277960 | tf_op jit(solution)/shard_map/ppermute | solution.py:43
  49.5 0.1 fusion
  49.6 0.1 select_reduce_fusion
  49.7 3.0 %collective-permute-done.5.refs_6_.refs_7_ = bf16[128,1664]{1,0:T(8,128)(2,1)S(1)} collective-permute-done((bf16[128,1664]{1,0:T(8,128)(2,1)S(1)}, bf16[128,1664]{1,0:T(8,128)(2,1)S(1)}, u32[]{:S(2)}, u32[]{:S(2)}) %collective-permute-start.5) | collective-permute-done | bytes 426016 | tf_op jit(solution)/shard_map/ppermute | solution.py:43
  52.7 6.9 %collective-permute-done.4.refs_5_.refs_6_ = bf16[128,1664]{1,0:T(8,128)(2,1)S(1)} collective-permute-done((bf16[128,1664]{1,0:T(8,128)(2,1)S(1)}, bf16[128,1664]{1,0:T(8,128)(2,1)S(1)}, u32[]{:S(2)}, u32[]{:S(2)}) %collective-permute-start.4) | collective-permute-done | bytes 426016 | tf_op jit(solution)/shard_map/ppermute | solution.py:43
  59.6 0.0 collective-permute-done.3.refs_4_.refs_5_
  59.6 0.1 collective-permute-done.1.refs_2_.refs_3_
  59.7 2.3 %shard_map.37 = bf16[8,288,128]{2,1,0:T(8,128)(2,1)S(1)} custom-call(bf16[128,1664]{1,0:T(8,128)(2,1)S(1)} %constant_dynamic-update-slice_fusion.refs_0_, bf16[128,1664]{1,0:T(8,128)(2,1)S(1)} %collective-permute-done.refs_1_.refs_2_, bf16[128,1664]{1,0:T(8,128)(2,1)S(1)} %collective-permute-done.1.refs_2_.refs_3_, ...), custom_call_target="tpu_custom_call" | custom-call | flops 981467136 | bytes 2981888 | tf_op jit(solution)/shard_map/pallas_call | solution.py:144
  62.0 17.4 %all_to_all.10.parts = bf16[8,288,128]{2,1,0:T(8,128)(2,1)S(1)} all-to-all(bf16[8,288,128]{2,1,0:T(8,128)(2,1)S(1)} %shard_map.37), channel_id=1, replica_groups=mesh['z'=16,'xl'=2,'y'=4,'xh'=2,'seq'=2] {'y','xh'}, dimensions={0} | all-to-all | bytes 1179648 | tf_op jit(solution)/shard_map/all_to_all | solution.py:181
  79.5 0.7 shard_map.38
  80.1 0.0 copy-start
  80.1 13.2 %all_to_all.11.refs_0_ = bf16[8,288,128]{2,1,0:T(8,128)(2,1)S(1)} all-to-all(bf16[8,288,128]{2,1,0:T(8,128)(2,1)S(1)} %shard_map.38), channel_id=1, replica_groups=mesh['z'=16,'xl'=2,'y'=4,'xh'=2,'seq'=2] {'y','xh'}, dimensions={0} | all-to-all | bytes 1179648 | tf_op jit(solution)/shard_map/all_to_all | solution.py:190
  93.3 0.0 copy-done
  93.3 0.7 shard_map.40
  94.0 6.5 %collective-permute-start.6 = (bf16[128,640]{1,0:T(8,128)(2,1)S(1)}, bf16[128,640]{1,0:T(8,128)(2,1)S(1)}, u32[]{:S(2)}, u32[]{:S(2)}) collective-permute-start(bf16[128,640]{1,0:T(8,128)(2,1)S(1)} %get-tuple-element.31), channel_id=1, source_target_pairs={{0,448},{1,65},{16,464},{17,81},{32,480},{33,97},{48,496},{49,113}... | collective-permute-start | bytes 491528 | tf_op jit(solution)/shard_map/ppermute | solution.py:47
  100.5 4.4 %collective-permute-start.8 = (bf16[128,640]{1,0:T(8,128)(2,1)S(1)}, bf16[128,640]{1,0:T(8,128)(2,1)S(1)}, u32[]{:S(2)}, u32[]{:S(2)}) collective-permute-start(bf16[128,640]{1,0:T(8,128)(2,1)S(1)} %get-tuple-element.33), channel_id=1, source_target_pairs={{0,48},{1,497},{16,32},{17,481},{32,80},{33,17},{48,64},{49,1},{64... | collective-permute-start | bytes 491528 | tf_op jit(solution)/shard_map/ppermute | solution.py:47
  104.9 1.9 %collective-permute-start.9 = (bf16[128,640]{1,0:T(8,128)(2,1)S(1)}, bf16[128,640]{1,0:T(8,128)(2,1)S(1)}, u32[]{:S(2)}, u32[]{:S(2)}) collective-permute-start(bf16[128,640]{1,0:T(8,128)(2,1)S(1)} %get-tuple-element.34), channel_id=1, source_target_pairs={{0,32},{1,481},{16,48},{17,497},{32,64},{33,1},{48,80},{49,17},{64... | collective-permute-start | bytes 491528 | tf_op jit(solution)/shard_map/ppermute | solution.py:47
  106.8 2.6 %collective-permute-start.10 = (bf16[128,640]{1,0:T(8,128)(2,1)S(1)}, bf16[128,640]{1,0:T(8,128)(2,1)S(1)}, u32[]{:S(2)}, u32[]{:S(2)}) collective-permute-start(bf16[128,640]{1,0:T(8,128)(2,1)S(1)} %get-tuple-element.35), channel_id=1, source_target_pairs={{0,16},{1,17},{16,0},{17,1},{32,48},{33,49},{48,32},{49,33},{64,80... | collective-permute-start | bytes 491528 | tf_op jit(solution)/shard_map/ppermute | solution.py:47
  109.5 0.7 shard_map.39
  110.2 0.0 collective-permute-done.6
  110.3 5.5 %collective-permute-start.7 = (bf16[128,640]{1,0:T(8,128)(2,1)S(1)}, bf16[128,640]{1,0:T(8,128)(2,1)S(1)}, u32[]{:S(2)}, u32[]{:S(2)}) collective-permute-start(bf16[128,640]{1,0:T(8,128)(2,1)S(1)} %add_convert_fusion.1), channel_id=1, source_target_pairs={{0,464},{1,81},{16,448},{17,65},{32,496},{33,113},{48,480},{49,97}... | collective-permute-start | bytes 491528 | tf_op jit(solution)/shard_map/ppermute | solution.py:47
  115.8 0.0 collective-permute-done.8
  115.8 0.0 collective-permute-done.9
  115.9 0.0 collective-permute-done.10
  115.9 0.1 add_convert_fusion
  115.9 2.8 %collective-permute-start.11 = (bf16[128,640]{1,0:T(8,128)(2,1)S(1)}, bf16[128,640]{1,0:T(8,128)(2,1)S(1)}, u32[]{:S(2)}, u32[]{:S(2)}) collective-permute-start(bf16[128,640]{1,0:T(8,128)(2,1)S(1)} %add_convert_fusion), channel_id=1, source_target_pairs={{0,96},{1,417},{16,112},{17,433},{32,128},{33,449},{48,144},{49,46... | collective-permute-start | bytes 491528 | tf_op jit(solution)/shard_map/ppermute | solution.py:47
  118.8 6.2 %collective-permute-done.7 = bf16[128,640]{1,0:T(8,128)(2,1)S(1)} collective-permute-done((bf16[128,640]{1,0:T(8,128)(2,1)S(1)}, bf16[128,640]{1,0:T(8,128)(2,1)S(1)}, u32[]{:S(2)}, u32[]{:S(2)}) %collective-permute-start.7) | collective-permute-done | bytes 163872 | tf_op jit(solution)/shard_map/ppermute | solution.py:47
  125.0 5.0 %collective-permute-done.11 = bf16[128,640]{1,0:T(8,128)(2,1)S(1)} collective-permute-done((bf16[128,640]{1,0:T(8,128)(2,1)S(1)}, bf16[128,640]{1,0:T(8,128)(2,1)S(1)}, u32[]{:S(2)}, u32[]{:S(2)}) %collective-permute-start.11) | collective-permute-done | bytes 163872 | tf_op jit(solution)/shard_map/ppermute | solution.py:47
  130.0 0.8 multiply_convert_fusion
  (5 shorter events, 0.1 us)
Async XLA Ops:
  0.0 1.0 copy-start.1
  1.1 35.9 %collective-permute-start.2 = (bf16[128,1664]{1,0:T(8,128)(2,1)S(1)}, bf16[128,1664]{1,0:T(8,128)(2,1)S(1)}, u32[]{:S(2)}, u32[]{:S(2)}) collective-permute-start(bf16[128,1664]{1,0:T(8,128)(2,1)S(1)} %constant_dynamic-update-slice_fusion.refs_0_), channel_id=1, source_target_pairs={{96,0},{417,1},{112,16},{433,17},{128,32},{449,33},{144,48},{465,4... | collective-permute-start | bytes 1277960 | tf_op jit(solution)/shard_map/ppermute | solution.py:43
  13.3 32.7 %collective-permute-start = (bf16[128,1664]{1,0:T(8,128)(2,1)S(1)}, bf16[128,1664]{1,0:T(8,128)(2,1)S(1)}, u32[]{:S(2)}, u32[]{:S(2)}) collective-permute-start(bf16[128,1664]{1,0:T(8,128)(2,1)S(1)} %constant_dynamic-update-slice_fusion.refs_0_), channel_id=1, source_target_pairs={{464,0},{81,1},{448,16},{65,17},{496,32},{113,33},{480,48},{97,49}... | collective-permute-start | bytes 1277960 | tf_op jit(solution)/shard_map/ppermute | solution.py:43
  16.8 0.7 copy-start.2
  36.9 15.8 %collective-permute-start.5 = (bf16[128,1664]{1,0:T(8,128)(2,1)S(1)}, bf16[128,1664]{1,0:T(8,128)(2,1)S(1)}, u32[]{:S(2)}, u32[]{:S(2)}) collective-permute-start(bf16[128,1664]{1,0:T(8,128)(2,1)S(1)} %collective-permute-done.2.refs_3_.refs_4_), channel_id=1, source_target_pairs={{48,0},{497,1},{32,16},{481,17},{80,32},{17,33},{64,48},{1,49},{11... | collective-permute-start | bytes 1277960 | tf_op jit(solution)/shard_map/ppermute | solution.py:43
  40.2 19.4 %collective-permute-start.4 = (bf16[128,1664]{1,0:T(8,128)(2,1)S(1)}, bf16[128,1664]{1,0:T(8,128)(2,1)S(1)}, u32[]{:S(2)}, u32[]{:S(2)}) collective-permute-start(bf16[128,1664]{1,0:T(8,128)(2,1)S(1)} %collective-permute-done.2.refs_3_.refs_4_), channel_id=1, source_target_pairs={{32,0},{481,1},{48,16},{497,17},{64,32},{1,33},{80,48},{17,49},{96... | collective-permute-start | bytes 1277960 | tf_op jit(solution)/shard_map/ppermute | solution.py:43
  44.1 15.6 %collective-permute-start.3 = (bf16[128,1664]{1,0:T(8,128)(2,1)S(1)}, bf16[128,1664]{1,0:T(8,128)(2,1)S(1)}, u32[]{:S(2)}, u32[]{:S(2)}) collective-permute-start(bf16[128,1664]{1,0:T(8,128)(2,1)S(1)} %collective-permute-done.2.refs_3_.refs_4_), channel_id=1, source_target_pairs={{16,0},{17,1},{0,16},{1,17},{48,32},{49,33},{32,48},{33,49},{80,64... | collective-permute-start | bytes 1277960 | tf_op jit(solution)/shard_map/ppermute | solution.py:43
  46.0 13.7 %collective-permute-start.1 = (bf16[128,1664]{1,0:T(8,128)(2,1)S(1)}, bf16[128,1664]{1,0:T(8,128)(2,1)S(1)}, u32[]{:S(2)}, u32[]{:S(2)}) collective-permute-start(bf16[128,1664]{1,0:T(8,128)(2,1)S(1)} %collective-permute-done.refs_1_.refs_2_), channel_id=1, source_target_pairs={{448,0},{65,1},{464,16},{81,17},{480,32},{97,33},{496,48},{113,49}... | collective-permute-start | bytes 1277960 | tf_op jit(solution)/shard_map/ppermute | solution.py:43
  80.1 13.2 %copy-start = (bf16[128,640]{1,0:T(8,128)(2,1)S(1)}, bf16[128,640]{1,0:T(8,128)(2,1)}, u32[]{:S(2)}) copy-start(bf16[128,640]{1,0:T(8,128)(2,1)} %refs_1_.3) | copy-start | bytes 491524
  94.0 16.2 %collective-permute-start.6 = (bf16[128,640]{1,0:T(8,128)(2,1)S(1)}, bf16[128,640]{1,0:T(8,128)(2,1)S(1)}, u32[]{:S(2)}, u32[]{:S(2)}) collective-permute-start(bf16[128,640]{1,0:T(8,128)(2,1)S(1)} %get-tuple-element.31), channel_id=1, source_target_pairs={{0,448},{1,65},{16,464},{17,81},{32,480},{33,97},{48,496},{49,113}... | collective-permute-start | bytes 491528 | tf_op jit(solution)/shard_map/ppermute | solution.py:47
  100.5 15.4 %collective-permute-start.8 = (bf16[128,640]{1,0:T(8,128)(2,1)S(1)}, bf16[128,640]{1,0:T(8,128)(2,1)S(1)}, u32[]{:S(2)}, u32[]{:S(2)}) collective-permute-start(bf16[128,640]{1,0:T(8,128)(2,1)S(1)} %get-tuple-element.33), channel_id=1, source_target_pairs={{0,48},{1,497},{16,32},{17,481},{32,80},{33,17},{48,64},{49,1},{64... | collective-permute-start | bytes 491528 | tf_op jit(solution)/shard_map/ppermute | solution.py:47
  104.9 10.9 %collective-permute-start.9 = (bf16[128,640]{1,0:T(8,128)(2,1)S(1)}, bf16[128,640]{1,0:T(8,128)(2,1)S(1)}, u32[]{:S(2)}, u32[]{:S(2)}) collective-permute-start(bf16[128,640]{1,0:T(8,128)(2,1)S(1)} %get-tuple-element.34), channel_id=1, source_target_pairs={{0,32},{1,481},{16,48},{17,497},{32,64},{33,1},{48,80},{49,17},{64... | collective-permute-start | bytes 491528 | tf_op jit(solution)/shard_map/ppermute | solution.py:47
  106.8 9.0 %collective-permute-start.10 = (bf16[128,640]{1,0:T(8,128)(2,1)S(1)}, bf16[128,640]{1,0:T(8,128)(2,1)S(1)}, u32[]{:S(2)}, u32[]{:S(2)}) collective-permute-start(bf16[128,640]{1,0:T(8,128)(2,1)S(1)} %get-tuple-element.35), channel_id=1, source_target_pairs={{0,16},{1,17},{16,0},{17,1},{32,48},{33,49},{48,32},{49,33},{64,80... | collective-permute-start | bytes 491528 | tf_op jit(solution)/shard_map/ppermute | solution.py:47
  110.3 14.7 %collective-permute-start.7 = (bf16[128,640]{1,0:T(8,128)(2,1)S(1)}, bf16[128,640]{1,0:T(8,128)(2,1)S(1)}, u32[]{:S(2)}, u32[]{:S(2)}) collective-permute-start(bf16[128,640]{1,0:T(8,128)(2,1)S(1)} %add_convert_fusion.1), channel_id=1, source_target_pairs={{0,464},{1,81},{16,448},{17,65},{32,496},{33,113},{48,480},{49,97}... | collective-permute-start | bytes 491528 | tf_op jit(solution)/shard_map/ppermute | solution.py:47
  115.9 14.0 %collective-permute-start.11 = (bf16[128,640]{1,0:T(8,128)(2,1)S(1)}, bf16[128,640]{1,0:T(8,128)(2,1)S(1)}, u32[]{:S(2)}, u32[]{:S(2)}) collective-permute-start(bf16[128,640]{1,0:T(8,128)(2,1)S(1)} %add_convert_fusion), channel_id=1, source_target_pairs={{0,96},{1,417},{16,112},{17,433},{32,128},{33,449},{48,144},{49,46... | collective-permute-start | bytes 491528 | tf_op jit(solution)/shard_map/ppermute | solution.py:47

commit v7 on v6

--- a/solution.py
+++ b/solution.py
@@ -20,6 +20,7 @@
     (2, 3), (2, 4), (2, 5), (2, 6),
     (3, 4), (3, 5), (3, 6),
 )
+BATCHES = (((0, 1, 2), (3, 4, 5, 6)), ((3,), (4, 5, 6)), ((0,), (0, 1)), ((1,), (2,)))
 ONE_SIDED = ((0, 0), (2, 5), (2, 6), (3, 4))
 F32, BF16 = jnp.float32, jnp.bfloat16
 
@@ -59,27 +60,25 @@
     return lax.dot_general(left, right, (((1,), (1,)), ((), ())), preferred_element_type=F32)
 
 
-def rights_of(left):
-    return [b for a, b in TILES if a == left]
-
-
 def gram_kernel(ds, student_scale, teacher_scale, *refs):
     blocks, out = refs[:-1], refs[-1]
     share = out.shape[1] // len(TILES)
     n = blocks[0].shape[0]
-    k = 0
-    for left in sorted({a for a, _ in TILES}):
-        rights = rights_of(left)
-        right_s = jnp.concatenate([blocks[b][:, :ds] for b in rights], axis=0)
-        right_t = jnp.concatenate([blocks[b][:, ds:] for b in rights], axis=0)
+
+    def rows_of(elements, columns):
+        return jnp.concatenate([blocks[e][:, columns] for e in elements], axis=0)
+
+    for lefts, rights in BATCHES:
         product = (
-            tile_dot(blocks[left][:, :ds], right_s) * student_scale
-            - tile_dot(blocks[left][:, ds:], right_t) * teacher_scale
+            tile_dot(rows_of(lefts, slice(0, ds)), rows_of(rights, slice(0, ds))) * student_scale
+            - tile_dot(rows_of(lefts, slice(ds, None)), rows_of(rights, slice(ds, None)))
+            * teacher_scale
         )
-        for i in range(len(rights)):
-            tile = product[:, i * n : (i + 1) * n].astype(BF16)
-            out[:, k * share : (k + 1) * share, :] = tile.reshape(NT, share, n)
-            k += 1
+        for i, a in enumerate(lefts):
+            for j, b in enumerate(rights):
+                k = TILES.index((a, b))
+                tile = product[i * n : (i + 1) * n, j * n : (j + 1) * n].astype(BF16)
+                out[:, k * share : (k + 1) * share, :] = tile.reshape(NT, share, n)
 
 
 def mask_kernel(where_ref, parts, out):

time: 131 us -> 131 us (level)
  no operation moved by 1% of the time
where the time goes in v7:
time: 131 us; the launch traced here: 130 us
  starting transfers between devices  52 us (40%)
  waiting for transfers between devices  38.5 us (29%)
  blocking collectives  30.6 us (23%)
  Pallas kernels  3.66 us (3%)
  local copies, waits for them, and re-layouts  3.65 us (3%)
    ppermute x6, starting transfers between devices, fetch(): return lax.ppermute(block, ROW, moves(step, False))  28.2 us
    ppermute x6, waiting for transfers between devices, fetch(): return lax.ppermute(block, ROW, moves(step, False))  27.3 us
    ppermute x6, starting transfers between devices, give(): return lax.ppermute(block, ROW, moves(step, True))  23.8 us
    all_to_all x1, blocking collectives, on_device(): parts = lax.all_to_all(partial, TENSOR, 0, 0)  17.4 us
    all_to_all x1, blocking collectives, on_device(): tiles = lax.all_to_all(copies, TENSOR, 0, 0)  13.2 us
    ppermute x6, waiting for transfers between devices, give(): return lax.ppermute(block, ROW, moves(step, True))  11.2 us
    pallas_call x4, Pallas kernels, call(): pl.pallas_call(kernel, out_shape=out_shape, in_specs=specs, out_specs=[vm...  3.66 us
  transfers between devices with their start and end apart: 12, of which 6 were waited for; matrix products, arithmetic and copies ran while one was open for 2% of the time, Pallas kernels for 1%

profile of v7, /device:TPU:2, one launch (start us, length us, event | category | flops | bytes accessed | tf_op | source)
XLA Modules:
  0.0 130.0 jit_solution(17109030022093394510)
XLA Ops:
  0.0 0.0 copy-start.1
  0.0 1.0 constant_dynamic-update-slice_fusion.1
  1.0 0.0 copy-done.1
  1.1 12.3 %collective-permute-start.2 = (bf16[128,1664]{1,0:T(8,128)(2,1)S(1)}, bf16[128,1664]{1,0:T(8,128)(2,1)S(1)}, u32[]{:S(2)}, u32[]{:S(2)}) collective-permute-start(bf16[128,1664]{1,0:T(8,128)(2,1)S(1)} %constant_dynamic-update-slice_fusion.refs_0_), channel_id=1, source_target_pairs={{96,0},{417,1},{112,16},{433,17},{128,32},{449,33},{144,48},{465,4... | collective-permute-start | bytes 1277960 | tf_op jit(solution)/shard_map/ppermute | solution.py:44
  13.3 3.4 %collective-permute-start = (bf16[128,1664]{1,0:T(8,128)(2,1)S(1)}, bf16[128,1664]{1,0:T(8,128)(2,1)S(1)}, u32[]{:S(2)}, u32[]{:S(2)}) collective-permute-start(bf16[128,1664]{1,0:T(8,128)(2,1)S(1)} %constant_dynamic-update-slice_fusion.refs_0_), channel_id=1, source_target_pairs={{464,0},{81,1},{448,16},{65,17},{496,32},{113,33},{480,48},{97,49}... | collective-permute-start | bytes 1277960 | tf_op jit(solution)/shard_map/ppermute | solution.py:44
  16.8 0.0 copy-start.2
  16.8 0.6 copy-done.2
  17.5 0.2 reduce-window.4
  17.6 0.6 fusion.1
  18.2 1.4 %stack.35.where_ref = s32[10]{0:T(128)S(1)} concatenate(s32[1]{0:T(128)} %bitcast.1, s32[1]{0:T(128)} %bitcast.2, s32[1]{0:T(128)} %bitcast.3, s32[1]{0:T(128)} %bitcast.4, s32[1]{0:T(128)} %bitcast.5, s32[1]{0:T(128)} %bitcast.6, s32[1]{0:T(128)} %bitcast.7, s32[1]{0:T(128)} %bitcast.8, s32[1]{0:T(128)} %bitcast.9, s32[1]{0:T(128)} %bitcast.10), dimensions={0} | concatenate | bytes 80 | tf_op jit(solution)/shard_map/stack | solution.py:164
  19.6 17.3 %collective-permute-done.2.refs_3_.refs_4_ = bf16[128,1664]{1,0:T(8,128)(2,1)S(1)} collective-permute-done((bf16[128,1664]{1,0:T(8,128)(2,1)S(1)}, bf16[128,1664]{1,0:T(8,128)(2,1)S(1)}, u32[]{:S(2)}, u32[]{:S(2)}) %collective-permute-start.2) | collective-permute-done | bytes 426016 | tf_op jit(solution)/shard_map/ppermute | solution.py:44
  36.9 3.3 %collective-permute-start.5 = (bf16[128,1664]{1,0:T(8,128)(2,1)S(1)}, bf16[128,1664]{1,0:T(8,128)(2,1)S(1)}, u32[]{:S(2)}, u32[]{:S(2)}) collective-permute-start(bf16[128,1664]{1,0:T(8,128)(2,1)S(1)} %collective-permute-done.2.refs_3_.refs_4_), channel_id=1, source_target_pairs={{48,0},{497,1},{32,16},{481,17},{80,32},{17,33},{64,48},{1,49},{11... | collective-permute-start | bytes 1277960 | tf_op jit(solution)/shard_map/ppermute | solution.py:44
  40.2 3.8 %collective-permute-start.4 = (bf16[128,1664]{1,0:T(8,128)(2,1)S(1)}, bf16[128,1664]{1,0:T(8,128)(2,1)S(1)}, u32[]{:S(2)}, u32[]{:S(2)}) collective-permute-start(bf16[128,1664]{1,0:T(8,128)(2,1)S(1)} %collective-permute-done.2.refs_3_.refs_4_), channel_id=1, source_target_pairs={{32,0},{481,1},{48,16},{497,17},{64,32},{1,33},{80,48},{17,49},{96... | collective-permute-start | bytes 1277960 | tf_op jit(solution)/shard_map/ppermute | solution.py:44
  44.1 1.9 %collective-permute-start.3 = (bf16[128,1664]{1,0:T(8,128)(2,1)S(1)}, bf16[128,1664]{1,0:T(8,128)(2,1)S(1)}, u32[]{:S(2)}, u32[]{:S(2)}) collective-permute-start(bf16[128,1664]{1,0:T(8,128)(2,1)S(1)} %collective-permute-done.2.refs_3_.refs_4_), channel_id=1, source_target_pairs={{16,0},{17,1},{0,16},{1,17},{48,32},{49,33},{32,48},{33,49},{80,64... | collective-permute-start | bytes 1277960 | tf_op jit(solution)/shard_map/ppermute | solution.py:44
  46.0 0.0 collective-permute-done.refs_1_.refs_2_
  46.0 3.5 %collective-permute-start.1 = (bf16[128,1664]{1,0:T(8,128)(2,1)S(1)}, bf16[128,1664]{1,0:T(8,128)(2,1)S(1)}, u32[]{:S(2)}, u32[]{:S(2)}) collective-permute-start(bf16[128,1664]{1,0:T(8,128)(2,1)S(1)} %collective-permute-done.refs_1_.refs_2_), channel_id=1, source_target_pairs={{448,0},{65,1},{464,16},{81,17},{480,32},{97,33},{496,48},{113,49}... | collective-permute-start | bytes 1277960 | tf_op jit(solution)/shard_map/ppermute | solution.py:44
  49.5 0.1 fusion
  49.6 0.1 select_reduce_fusion
  49.7 3.0 %collective-permute-done.5.refs_6_.refs_7_ = bf16[128,1664]{1,0:T(8,128)(2,1)S(1)} collective-permute-done((bf16[128,1664]{1,0:T(8,128)(2,1)S(1)}, bf16[128,1664]{1,0:T(8,128)(2,1)S(1)}, u32[]{:S(2)}, u32[]{:S(2)}) %collective-permute-start.5) | collective-permute-done | bytes 426016 | tf_op jit(solution)/shard_map/ppermute | solution.py:44
  52.7 6.9 %collective-permute-done.4.refs_5_.refs_6_ = bf16[128,1664]{1,0:T(8,128)(2,1)S(1)} collective-permute-done((bf16[128,1664]{1,0:T(8,128)(2,1)S(1)}, bf16[128,1664]{1,0:T(8,128)(2,1)S(1)}, u32[]{:S(2)}, u32[]{:S(2)}) %collective-permute-start.4) | collective-permute-done | bytes 426016 | tf_op jit(solution)/shard_map/ppermute | solution.py:44
  59.6 0.0 collective-permute-done.3.refs_4_.refs_5_
  59.6 0.1 collective-permute-done.1.refs_2_.refs_3_
  59.7 1.6 %shard_map.37 = bf16[8,288,128]{2,1,0:T(8,128)(2,1)S(1)} custom-call(bf16[128,1664]{1,0:T(8,128)(2,1)S(1)} %constant_dynamic-update-slice_fusion.refs_0_, bf16[128,1664]{1,0:T(8,128)(2,1)S(1)} %collective-permute-done.refs_1_.refs_2_, bf16[128,1664]{1,0:T(8,128)(2,1)S(1)} %collective-permute-done.1.refs_2_.refs_3_, ...), custom_call_target="tpu_custom_call" | custom-call | flops 981467136 | bytes 2981888 | tf_op jit(solution)/shard_map/pallas_call | solution.py:143
  61.3 17.4 %all_to_all.10.parts = bf16[8,288,128]{2,1,0:T(8,128)(2,1)S(1)} all-to-all(bf16[8,288,128]{2,1,0:T(8,128)(2,1)S(1)} %shard_map.37), channel_id=1, replica_groups=mesh['z'=16,'xl'=2,'y'=4,'xh'=2,'seq'=2] {'y','xh'}, dimensions={0} | all-to-all | bytes 1179648 | tf_op jit(solution)/shard_map/all_to_all | solution.py:180
  78.7 0.7 shard_map.38
  79.4 0.0 copy-start
  79.4 13.2 %all_to_all.11.refs_0_ = bf16[8,288,128]{2,1,0:T(8,128)(2,1)S(1)} all-to-all(bf16[8,288,128]{2,1,0:T(8,128)(2,1)S(1)} %shard_map.38), channel_id=1, replica_groups=mesh['z'=16,'xl'=2,'y'=4,'xh'=2,'seq'=2] {'y','xh'}, dimensions={0} | all-to-all | bytes 1179648 | tf_op jit(solution)/shard_map/all_to_all | solution.py:189
  92.6 0.0 copy-done
  92.6 0.7 shard_map.40
  93.3 6.5 %collective-permute-start.6 = (bf16[128,640]{1,0:T(8,128)(2,1)S(1)}, bf16[128,640]{1,0:T(8,128)(2,1)S(1)}, u32[]{:S(2)}, u32[]{:S(2)}) collective-permute-start(bf16[128,640]{1,0:T(8,128)(2,1)S(1)} %get-tuple-element.31), channel_id=1, source_target_pairs={{0,448},{1,65},{16,464},{17,81},{32,480},{33,97},{48,496},{49,113}... | collective-permute-start | bytes 491528 | tf_op jit(solution)/shard_map/ppermute | solution.py:48
  99.8 4.4 %collective-permute-start.8 = (bf16[128,640]{1,0:T(8,128)(2,1)S(1)}, bf16[128,640]{1,0:T(8,128)(2,1)S(1)}, u32[]{:S(2)}, u32[]{:S(2)}) collective-permute-start(bf16[128,640]{1,0:T(8,128)(2,1)S(1)} %get-tuple-element.33), channel_id=1, source_target_pairs={{0,48},{1,497},{16,32},{17,481},{32,80},{33,17},{48,64},{49,1},{64... | collective-permute-start | bytes 491528 | tf_op jit(solution)/shard_map/ppermute | solution.py:48
  104.2 1.9 %collective-permute-start.9 = (bf16[128,640]{1,0:T(8,128)(2,1)S(1)}, bf16[128,640]{1,0:T(8,128)(2,1)S(1)}, u32[]{:S(2)}, u32[]{:S(2)}) collective-permute-start(bf16[128,640]{1,0:T(8,128)(2,1)S(1)} %get-tuple-element.34), channel_id=1, source_target_pairs={{0,32},{1,481},{16,48},{17,497},{32,64},{33,1},{48,80},{49,17},{64... | collective-permute-start | bytes 491528 | tf_op jit(solution)/shard_map/ppermute | solution.py:48
  106.1 2.6 %collective-permute-start.10 = (bf16[128,640]{1,0:T(8,128)(2,1)S(1)}, bf16[128,640]{1,0:T(8,128)(2,1)S(1)}, u32[]{:S(2)}, u32[]{:S(2)}) collective-permute-start(bf16[128,640]{1,0:T(8,128)(2,1)S(1)} %get-tuple-element.35), channel_id=1, source_target_pairs={{0,16},{1,17},{16,0},{17,1},{32,48},{33,49},{48,32},{49,33},{64,80... | collective-permute-start | bytes 491528 | tf_op jit(solution)/shard_map/ppermute | solution.py:48
  108.8 0.7 shard_map.39
  109.5 0.0 collective-permute-done.6
  109.6 5.6 %collective-permute-start.7 = (bf16[128,640]{1,0:T(8,128)(2,1)S(1)}, bf16[128,640]{1,0:T(8,128)(2,1)S(1)}, u32[]{:S(2)}, u32[]{:S(2)}) collective-permute-start(bf16[128,640]{1,0:T(8,128)(2,1)S(1)} %add_convert_fusion.1), channel_id=1, source_target_pairs={{0,464},{1,81},{16,448},{17,65},{32,496},{33,113},{48,480},{49,97}... | collective-permute-start | bytes 491528 | tf_op jit(solution)/shard_map/ppermute | solution.py:48
  115.1 0.0 collective-permute-done.8
  115.1 0.0 collective-permute-done.9
  115.1 0.0 collective-permute-done.10
  115.2 0.1 add_convert_fusion
  115.2 2.8 %collective-permute-start.11 = (bf16[128,640]{1,0:T(8,128)(2,1)S(1)}, bf16[128,640]{1,0:T(8,128)(2,1)S(1)}, u32[]{:S(2)}, u32[]{:S(2)}) collective-permute-start(bf16[128,640]{1,0:T(8,128)(2,1)S(1)} %add_convert_fusion), channel_id=1, source_target_pairs={{0,96},{1,417},{16,112},{17,433},{32,128},{33,449},{48,144},{49,46... | collective-permute-start | bytes 491528 | tf_op jit(solution)/shard_map/ppermute | solution.py:48
  118.1 6.2 %collective-permute-done.7 = bf16[128,640]{1,0:T(8,128)(2,1)S(1)} collective-permute-done((bf16[128,640]{1,0:T(8,128)(2,1)S(1)}, bf16[128,640]{1,0:T(8,128)(2,1)S(1)}, u32[]{:S(2)}, u32[]{:S(2)}) %collective-permute-start.7) | collective-permute-done | bytes 163872 | tf_op jit(solution)/shard_map/ppermute | solution.py:48
  124.2 5.1 %collective-permute-done.11 = bf16[128,640]{1,0:T(8,128)(2,1)S(1)} collective-permute-done((bf16[128,640]{1,0:T(8,128)(2,1)S(1)}, bf16[128,640]{1,0:T(8,128)(2,1)S(1)}, u32[]{:S(2)}, u32[]{:S(2)}) %collective-permute-start.11) | collective-permute-done | bytes 163872 | tf_op jit(solution)/shard_map/ppermute | solution.py:48
  129.3 0.8 multiply_convert_fusion
  (5 shorter events, 0.1 us)
Async XLA Ops:
  0.0 1.0 copy-start.1
  1.1 35.9 %collective-permute-start.2 = (bf16[128,1664]{1,0:T(8,128)(2,1)S(1)}, bf16[128,1664]{1,0:T(8,128)(2,1)S(1)}, u32[]{:S(2)}, u32[]{:S(2)}) collective-permute-start(bf16[128,1664]{1,0:T(8,128)(2,1)S(1)} %constant_dynamic-update-slice_fusion.refs_0_), channel_id=1, source_target_pairs={{96,0},{417,1},{112,16},{433,17},{128,32},{449,33},{144,48},{465,4... | collective-permute-start | bytes 1277960 | tf_op jit(solution)/shard_map/ppermute | solution.py:44
  13.3 32.7 %collective-permute-start = (bf16[128,1664]{1,0:T(8,128)(2,1)S(1)}, bf16[128,1664]{1,0:T(8,128)(2,1)S(1)}, u32[]{:S(2)}, u32[]{:S(2)}) collective-permute-start(bf16[128,1664]{1,0:T(8,128)(2,1)S(1)} %constant_dynamic-update-slice_fusion.refs_0_), channel_id=1, source_target_pairs={{464,0},{81,1},{448,16},{65,17},{496,32},{113,33},{480,48},{97,49}... | collective-permute-start | bytes 1277960 | tf_op jit(solution)/shard_map/ppermute | solution.py:44
  16.8 0.7 copy-start.2
  36.9 15.8 %collective-permute-start.5 = (bf16[128,1664]{1,0:T(8,128)(2,1)S(1)}, bf16[128,1664]{1,0:T(8,128)(2,1)S(1)}, u32[]{:S(2)}, u32[]{:S(2)}) collective-permute-start(bf16[128,1664]{1,0:T(8,128)(2,1)S(1)} %collective-permute-done.2.refs_3_.refs_4_), channel_id=1, source_target_pairs={{48,0},{497,1},{32,16},{481,17},{80,32},{17,33},{64,48},{1,49},{11... | collective-permute-start | bytes 1277960 | tf_op jit(solution)/shard_map/ppermute | solution.py:44
  40.2 19.4 %collective-permute-start.4 = (bf16[128,1664]{1,0:T(8,128)(2,1)S(1)}, bf16[128,1664]{1,0:T(8,128)(2,1)S(1)}, u32[]{:S(2)}, u32[]{:S(2)}) collective-permute-start(bf16[128,1664]{1,0:T(8,128)(2,1)S(1)} %collective-permute-done.2.refs_3_.refs_4_), channel_id=1, source_target_pairs={{32,0},{481,1},{48,16},{497,17},{64,32},{1,33},{80,48},{17,49},{96... | collective-permute-start | bytes 1277960 | tf_op jit(solution)/shard_map/ppermute | solution.py:44
  44.1 15.6 %collective-permute-start.3 = (bf16[128,1664]{1,0:T(8,128)(2,1)S(1)}, bf16[128,1664]{1,0:T(8,128)(2,1)S(1)}, u32[]{:S(2)}, u32[]{:S(2)}) collective-permute-start(bf16[128,1664]{1,0:T(8,128)(2,1)S(1)} %collective-permute-done.2.refs_3_.refs_4_), channel_id=1, source_target_pairs={{16,0},{17,1},{0,16},{1,17},{48,32},{49,33},{32,48},{33,49},{80,64... | collective-permute-start | bytes 1277960 | tf_op jit(solution)/shard_map/ppermute | solution.py:44
  46.0 13.7 %collective-permute-start.1 = (bf16[128,1664]{1,0:T(8,128)(2,1)S(1)}, bf16[128,1664]{1,0:T(8,128)(2,1)S(1)}, u32[]{:S(2)}, u32[]{:S(2)}) collective-permute-start(bf16[128,1664]{1,0:T(8,128)(2,1)S(1)} %collective-permute-done.refs_1_.refs_2_), channel_id=1, source_target_pairs={{448,0},{65,1},{464,16},{81,17},{480,32},{97,33},{496,48},{113,49}... | collective-permute-start | bytes 1277960 | tf_op jit(solution)/shard_map/ppermute | solution.py:44
  79.4 13.2 %copy-start = (bf16[128,640]{1,0:T(8,128)(2,1)S(1)}, bf16[128,640]{1,0:T(8,128)(2,1)}, u32[]{:S(2)}) copy-start(bf16[128,640]{1,0:T(8,128)(2,1)} %refs_1_.3) | copy-start | bytes 491524
  93.3 16.2 %collective-permute-start.6 = (bf16[128,640]{1,0:T(8,128)(2,1)S(1)}, bf16[128,640]{1,0:T(8,128)(2,1)S(1)}, u32[]{:S(2)}, u32[]{:S(2)}) collective-permute-start(bf16[128,640]{1,0:T(8,128)(2,1)S(1)} %get-tuple-element.31), channel_id=1, source_target_pairs={{0,448},{1,65},{16,464},{17,81},{32,480},{33,97},{48,496},{49,113}... | collective-permute-start | bytes 491528 | tf_op jit(solution)/shard_map/ppermute | solution.py:48
  99.8 15.4 %collective-permute-start.8 = (bf16[128,640]{1,0:T(8,128)(2,1)S(1)}, bf16[128,640]{1,0:T(8,128)(2,1)S(1)}, u32[]{:S(2)}, u32[]{:S(2)}) collective-permute-start(bf16[128,640]{1,0:T(8,128)(2,1)S(1)} %get-tuple-element.33), channel_id=1, source_target_pairs={{0,48},{1,497},{16,32},{17,481},{32,80},{33,17},{48,64},{49,1},{64... | collective-permute-start | bytes 491528 | tf_op jit(solution)/shard_map/ppermute | solution.py:48
  104.2 10.9 %collective-permute-start.9 = (bf16[128,640]{1,0:T(8,128)(2,1)S(1)}, bf16[128,640]{1,0:T(8,128)(2,1)S(1)}, u32[]{:S(2)}, u32[]{:S(2)}) collective-permute-start(bf16[128,640]{1,0:T(8,128)(2,1)S(1)} %get-tuple-element.34), channel_id=1, source_target_pairs={{0,32},{1,481},{16,48},{17,497},{32,64},{33,1},{48,80},{49,17},{64... | collective-permute-start | bytes 491528 | tf_op jit(solution)/shard_map/ppermute | solution.py:48
  106.1 9.0 %collective-permute-start.10 = (bf16[128,640]{1,0:T(8,128)(2,1)S(1)}, bf16[128,640]{1,0:T(8,128)(2,1)S(1)}, u32[]{:S(2)}, u32[]{:S(2)}) collective-permute-start(bf16[128,640]{1,0:T(8,128)(2,1)S(1)} %get-tuple-element.35), channel_id=1, source_target_pairs={{0,16},{1,17},{16,0},{17,1},{32,48},{33,49},{48,32},{49,33},{64,80... | collective-permute-start | bytes 491528 | tf_op jit(solution)/shard_map/ppermute | solution.py:48
  109.6 14.7 %collective-permute-start.7 = (bf16[128,640]{1,0:T(8,128)(2,1)S(1)}, bf16[128,640]{1,0:T(8,128)(2,1)S(1)}, u32[]{:S(2)}, u32[]{:S(2)}) collective-permute-start(bf16[128,640]{1,0:T(8,128)(2,1)S(1)} %add_convert_fusion.1), channel_id=1, source_target_pairs={{0,464},{1,81},{16,448},{17,65},{32,496},{33,113},{48,480},{49,97}... | collective-permute-start | bytes 491528 | tf_op jit(solution)/shard_map/ppermute | solution.py:48
  115.2 14.0 %collective-permute-start.11 = (bf16[128,640]{1,0:T(8,128)(2,1)S(1)}, bf16[128,640]{1,0:T(8,128)(2,1)S(1)}, u32[]{:S(2)}, u32[]{:S(2)}) collective-permute-start(bf16[128,640]{1,0:T(8,128)(2,1)S(1)} %add_convert_fusion), channel_id=1, source_target_pairs={{0,96},{1,417},{16,112},{17,433},{32,128},{33,449},{48,144},{49,46... | collective-permute-start | bytes 491528 | tf_op jit(solution)/shard_map/ppermute | solution.py:48

commit v8 on v7

--- a/solution.py
+++ b/solution.py
@@ -21,7 +21,14 @@
     (3, 4), (3, 5), (3, 6),
 )
 BATCHES = (((0, 1, 2), (3, 4, 5, 6)), ((3,), (4, 5, 6)), ((0,), (0, 1)), ((1,), (2,)))
-ONE_SIDED = ((0, 0), (2, 5), (2, 6), (3, 4))
+FAR = (
+    (((2,), (3, 4, 5, 6)),),
+    (((0, 1), (4, 5, 6)), ((2,), (4,)), ((3,), (5, 6)), ((1,), (2,))),
+)
+NEAR = (
+    (((0, 1), (3, 4, 5, 6)), ((0,), (0, 1)), ((1,), (2,)), ((3,), (4, 5, 6))),
+    (((0, 1, 2), (3,)), ((0,), (1,))),
+)
 F32, BF16 = jnp.float32, jnp.bfloat16
 
 
@@ -101,38 +108,42 @@
             out[s, rows, :] = kept
 
 
-def terms_of(a):
-    straight = [(k, b) for k, (p, b) in enumerate(TILES) if p == a]
-    turned = [(k, p) for k, (p, b) in enumerate(TILES) if b == a and (p, b) not in ONE_SIDED]
-    return straight, turned
-
-
-def gradient_kernel(wanted, *refs):
+def gradient_kernel(wanted, straight, turned, *refs):
     tiles, blocks, outs = refs[0], refs[1 : 1 + len(ELEMENTS)], refs[1 + len(ELEMENTS) :]
     share = tiles.shape[1] // len(TILES)
     n, width = tiles.shape[2], outs[0].shape[1]
 
-    def tile(k):
+    def tile(a, b):
+        k = TILES.index((a, b))
         return tiles[:, k * share : (k + 1) * share, :].reshape(NT * share, n)
 
-    for out, a in zip(outs, wanted, strict=True):
-        straight, turned = terms_of(a)
-        total = None
-        if straight:
-            total = jnp.dot(
-                jnp.concatenate([tile(k) for k, _ in straight], axis=1),
-                jnp.concatenate([blocks[b][:, :width] for _, b in straight], axis=0),
-                preferred_element_type=F32,
-            )
-        if turned:
-            more = lax.dot_general(
-                jnp.concatenate([tile(k) for k, _ in turned], axis=0),
-                jnp.concatenate([blocks[b][:, :width] for _, b in turned], axis=0),
-                (((0,), (0,)), ((), ())),
-                preferred_element_type=F32,
-            )
-            total = more if total is None else total + more
-        out[...] = total.astype(out.dtype)
+    def grid_of(lefts, rights):
+        return jnp.concatenate(
+            [jnp.concatenate([tile(a, b) for b in rights], axis=1) for a in lefts], axis=0
+        )
+
+    def students(elements):
+        return jnp.concatenate([blocks[e][:, :width] for e in elements], axis=0)
+
+    sums = {}
+
+    def add(elements, product):
+        for i, e in enumerate(elements):
+            part = product[i * n : (i + 1) * n, :]
+            sums[e] = sums[e] + part if e in sums else part
+
+    for lefts, rights in straight:
+        add(lefts, jnp.dot(grid_of(lefts, rights), students(rights), preferred_element_type=F32))
+    for lefts, rights in turned:
+        product = lax.dot_general(
+            grid_of(lefts, rights),
+            students(lefts),
+            (((0,), (0,)), ((), ())),
+            preferred_element_type=F32,
+        )
+        add(rights, product)
+    for out, e in zip(outs, wanted, strict=True):
+        out[...] = sums[e].astype(out.dtype)
 
 
 def call(kernel, out_shape, flops, *operands, smem=0):
@@ -192,7 +203,7 @@
     near = [0] + [e for e, _, _ in FIRST]
     block = 2 * rows * rows * ds
     given = call(
-        lambda *refs: gradient_kernel(far, *refs),
+        lambda *refs: gradient_kernel(far, *FAR, *refs),
         [jax.ShapeDtypeStruct((rows, ds), BF16)] * len(far),
         14 * block,
         tiles,
@@ -200,7 +211,7 @@
         *blocks[1:],
     )
     kept = call(
-        lambda *refs: gradient_kernel(near, *refs),
+        lambda *refs: gradient_kernel(near, *NEAR, *refs),
         [jax.ShapeDtypeStruct((rows, ds), F32)] * len(near),
         18 * block,
         tiles,

time: 131 us -> 131 us (level)
  no operation moved by 1% of the time
where the time goes in v8:
time: 131 us; the launch traced here: 130 us
  starting transfers between devices  52.1 us (40%)
  waiting for transfers between devices  38.5 us (29%)
  blocking collectives  30.6 us (23%)
  local copies, waits for them, and re-layouts  3.65 us (3%)
  Pallas kernels  3.6 us (3%)
    ppermute x6, starting transfers between devices, fetch(): return lax.ppermute(block, ROW, moves(step, False))  28.2 us
    ppermute x6, waiting for transfers between devices, fetch(): return lax.ppermute(block, ROW, moves(step, False))  27.3 us
    ppermute x6, starting transfers between devices, give(): return lax.ppermute(block, ROW, moves(step, True))  23.8 us
    all_to_all x1, blocking collectives, on_device(): parts = lax.all_to_all(partial, TENSOR, 0, 0)  17.4 us
    all_to_all x1, blocking collectives, on_device(): tiles = lax.all_to_all(copies, TENSOR, 0, 0)  13.2 us
    ppermute x6, waiting for transfers between devices, give(): return lax.ppermute(block, ROW, moves(step, True))  11.2 us
    pallas_call x4, Pallas kernels, call(): pl.pallas_call(kernel, out_shape=out_shape, in_specs=specs, out_specs=[vm...  3.6 us
  transfers between devices with their start and end apart: 12, of which 6 were waited for; matrix products, arithmetic and copies ran while one was open for 2% of the time, Pallas kernels for 1%

profile of v8, /device:TPU:2, one launch (start us, length us, event | category | flops | bytes accessed | tf_op | source)
XLA Modules:
  0.0 130.0 jit_solution(10770488996230670937)
XLA Ops:
  0.0 0.0 copy-start.1
  0.0 1.0 constant_dynamic-update-slice_fusion.1
  1.0 0.0 copy-done.1
  1.1 12.3 %collective-permute-start.2 = (bf16[128,1664]{1,0:T(8,128)(2,1)S(1)}, bf16[128,1664]{1,0:T(8,128)(2,1)S(1)}, u32[]{:S(2)}, u32[]{:S(2)}) collective-permute-start(bf16[128,1664]{1,0:T(8,128)(2,1)S(1)} %constant_dynamic-update-slice_fusion.refs_0_), channel_id=1, source_target_pairs={{96,0},{417,1},{112,16},{433,17},{128,32},{449,33},{144,48},{465,4... | collective-permute-start | bytes 1277960 | tf_op jit(solution)/shard_map/ppermute | solution.py:51
  13.3 3.4 %collective-permute-start = (bf16[128,1664]{1,0:T(8,128)(2,1)S(1)}, bf16[128,1664]{1,0:T(8,128)(2,1)S(1)}, u32[]{:S(2)}, u32[]{:S(2)}) collective-permute-start(bf16[128,1664]{1,0:T(8,128)(2,1)S(1)} %constant_dynamic-update-slice_fusion.refs_0_), channel_id=1, source_target_pairs={{464,0},{81,1},{448,16},{65,17},{496,32},{113,33},{480,48},{97,49}... | collective-permute-start | bytes 1277960 | tf_op jit(solution)/shard_map/ppermute | solution.py:51
  16.8 0.0 copy-start.2
  16.8 0.6 copy-done.2
  17.5 0.2 reduce-window.4
  17.6 0.6 fusion.1
  18.2 1.4 %stack.35.where_ref = s32[10]{0:T(128)S(1)} concatenate(s32[1]{0:T(128)} %bitcast.1, s32[1]{0:T(128)} %bitcast.2, s32[1]{0:T(128)} %bitcast.3, s32[1]{0:T(128)} %bitcast.4, s32[1]{0:T(128)} %bitcast.5, s32[1]{0:T(128)} %bitcast.6, s32[1]{0:T(128)} %bitcast.7, s32[1]{0:T(128)} %bitcast.8, s32[1]{0:T(128)} %bitcast.9, s32[1]{0:T(128)} %bitcast.10), dimensions={0} | concatenate | bytes 80 | tf_op jit(solution)/shard_map/stack | solution.py:175
  19.6 17.3 %collective-permute-done.2.refs_3_.refs_4_ = bf16[128,1664]{1,0:T(8,128)(2,1)S(1)} collective-permute-done((bf16[128,1664]{1,0:T(8,128)(2,1)S(1)}, bf16[128,1664]{1,0:T(8,128)(2,1)S(1)}, u32[]{:S(2)}, u32[]{:S(2)}) %collective-permute-start.2) | collective-permute-done | bytes 426016 | tf_op jit(solution)/shard_map/ppermute | solution.py:51
  36.9 3.3 %collective-permute-start.5 = (bf16[128,1664]{1,0:T(8,128)(2,1)S(1)}, bf16[128,1664]{1,0:T(8,128)(2,1)S(1)}, u32[]{:S(2)}, u32[]{:S(2)}) collective-permute-start(bf16[128,1664]{1,0:T(8,128)(2,1)S(1)} %collective-permute-done.2.refs_3_.refs_4_), channel_id=1, source_target_pairs={{48,0},{497,1},{32,16},{481,17},{80,32},{17,33},{64,48},{1,49},{11... | collective-permute-start | bytes 1277960 | tf_op jit(solution)/shard_map/ppermute | solution.py:51
  40.2 3.8 %collective-permute-start.4 = (bf16[128,1664]{1,0:T(8,128)(2,1)S(1)}, bf16[128,1664]{1,0:T(8,128)(2,1)S(1)}, u32[]{:S(2)}, u32[]{:S(2)}) collective-permute-start(bf16[128,1664]{1,0:T(8,128)(2,1)S(1)} %collective-permute-done.2.refs_3_.refs_4_), channel_id=1, source_target_pairs={{32,0},{481,1},{48,16},{497,17},{64,32},{1,33},{80,48},{17,49},{96... | collective-permute-start | bytes 1277960 | tf_op jit(solution)/shard_map/ppermute | solution.py:51
  44.1 1.9 %collective-permute-start.3 = (bf16[128,1664]{1,0:T(8,128)(2,1)S(1)}, bf16[128,1664]{1,0:T(8,128)(2,1)S(1)}, u32[]{:S(2)}, u32[]{:S(2)}) collective-permute-start(bf16[128,1664]{1,0:T(8,128)(2,1)S(1)} %collective-permute-done.2.refs_3_.refs_4_), channel_id=1, source_target_pairs={{16,0},{17,1},{0,16},{1,17},{48,32},{49,33},{32,48},{33,49},{80,64... | collective-permute-start | bytes 1277960 | tf_op jit(solution)/shard_map/ppermute | solution.py:51
  46.0 0.0 collective-permute-done.refs_1_.refs_2_
  46.0 3.5 %collective-permute-start.1 = (bf16[128,1664]{1,0:T(8,128)(2,1)S(1)}, bf16[128,1664]{1,0:T(8,128)(2,1)S(1)}, u32[]{:S(2)}, u32[]{:S(2)}) collective-permute-start(bf16[128,1664]{1,0:T(8,128)(2,1)S(1)} %collective-permute-done.refs_1_.refs_2_), channel_id=1, source_target_pairs={{448,0},{65,1},{464,16},{81,17},{480,32},{97,33},{496,48},{113,49}... | collective-permute-start | bytes 1277960 | tf_op jit(solution)/shard_map/ppermute | solution.py:51
  49.5 0.1 fusion
  49.6 0.1 select_reduce_fusion
  49.7 3.0 %collective-permute-done.5.refs_6_.refs_7_ = bf16[128,1664]{1,0:T(8,128)(2,1)S(1)} collective-permute-done((bf16[128,1664]{1,0:T(8,128)(2,1)S(1)}, bf16[128,1664]{1,0:T(8,128)(2,1)S(1)}, u32[]{:S(2)}, u32[]{:S(2)}) %collective-permute-start.5) | collective-permute-done | bytes 426016 | tf_op jit(solution)/shard_map/ppermute | solution.py:51
  52.7 6.9 %collective-permute-done.4.refs_5_.refs_6_ = bf16[128,1664]{1,0:T(8,128)(2,1)S(1)} collective-permute-done((bf16[128,1664]{1,0:T(8,128)(2,1)S(1)}, bf16[128,1664]{1,0:T(8,128)(2,1)S(1)}, u32[]{:S(2)}, u32[]{:S(2)}) %collective-permute-start.4) | collective-permute-done | bytes 426016 | tf_op jit(solution)/shard_map/ppermute | solution.py:51
  59.6 0.0 collective-permute-done.3.refs_4_.refs_5_
  59.6 0.1 collective-permute-done.1.refs_2_.refs_3_
  59.7 1.6 %shard_map.37 = bf16[8,288,128]{2,1,0:T(8,128)(2,1)S(1)} custom-call(bf16[128,1664]{1,0:T(8,128)(2,1)S(1)} %constant_dynamic-update-slice_fusion.refs_0_, bf16[128,1664]{1,0:T(8,128)(2,1)S(1)} %collective-permute-done.refs_1_.refs_2_, bf16[128,1664]{1,0:T(8,128)(2,1)S(1)} %collective-permute-done.1.refs_2_.refs_3_, ...), custom_call_target="tpu_custom_call" | custom-call | flops 981467136 | bytes 2981888 | tf_op jit(solution)/shard_map/pallas_call | solution.py:154
  61.3 17.4 %all_to_all.10.parts = bf16[8,288,128]{2,1,0:T(8,128)(2,1)S(1)} all-to-all(bf16[8,288,128]{2,1,0:T(8,128)(2,1)S(1)} %shard_map.37), channel_id=1, replica_groups=mesh['z'=16,'xl'=2,'y'=4,'xh'=2,'seq'=2] {'y','xh'}, dimensions={0} | all-to-all | bytes 1179648 | tf_op jit(solution)/shard_map/all_to_all | solution.py:191
  78.7 0.7 shard_map.38
  79.4 0.0 copy-start
  79.4 13.2 %all_to_all.11.refs_0_ = bf16[8,288,128]{2,1,0:T(8,128)(2,1)S(1)} all-to-all(bf16[8,288,128]{2,1,0:T(8,128)(2,1)S(1)} %shard_map.38), channel_id=1, replica_groups=mesh['z'=16,'xl'=2,'y'=4,'xh'=2,'seq'=2] {'y','xh'}, dimensions={0} | all-to-all | bytes 1179648 | tf_op jit(solution)/shard_map/all_to_all | solution.py:200
  92.6 0.0 copy-done
  92.6 0.6 shard_map.40
  93.3 6.4 %collective-permute-start.6 = (bf16[128,640]{1,0:T(8,128)(2,1)S(1)}, bf16[128,640]{1,0:T(8,128)(2,1)S(1)}, u32[]{:S(2)}, u32[]{:S(2)}) collective-permute-start(bf16[128,640]{1,0:T(8,128)(2,1)S(1)} %get-tuple-element.31), channel_id=1, source_target_pairs={{0,448},{1,65},{16,464},{17,81},{32,480},{33,97},{48,496},{49,113}... | collective-permute-start | bytes 491528 | tf_op jit(solution)/shard_map/ppermute | solution.py:55
  99.7 4.4 %collective-permute-start.8 = (bf16[128,640]{1,0:T(8,128)(2,1)S(1)}, bf16[128,640]{1,0:T(8,128)(2,1)S(1)}, u32[]{:S(2)}, u32[]{:S(2)}) collective-permute-start(bf16[128,640]{1,0:T(8,128)(2,1)S(1)} %get-tuple-element.33), channel_id=1, source_target_pairs={{0,48},{1,497},{16,32},{17,481},{32,80},{33,17},{48,64},{49,1},{64... | collective-permute-start | bytes 491528 | tf_op jit(solution)/shard_map/ppermute | solution.py:55
  104.2 1.9 %collective-permute-start.9 = (bf16[128,640]{1,0:T(8,128)(2,1)S(1)}, bf16[128,640]{1,0:T(8,128)(2,1)S(1)}, u32[]{:S(2)}, u32[]{:S(2)}) collective-permute-start(bf16[128,640]{1,0:T(8,128)(2,1)S(1)} %get-tuple-element.34), channel_id=1, source_target_pairs={{0,32},{1,481},{16,48},{17,497},{32,64},{33,1},{48,80},{49,17},{64... | collective-permute-start | bytes 491528 | tf_op jit(solution)/shard_map/ppermute | solution.py:55
  106.1 2.6 %collective-permute-start.10 = (bf16[128,640]{1,0:T(8,128)(2,1)S(1)}, bf16[128,640]{1,0:T(8,128)(2,1)S(1)}, u32[]{:S(2)}, u32[]{:S(2)}) collective-permute-start(bf16[128,640]{1,0:T(8,128)(2,1)S(1)} %get-tuple-element.35), channel_id=1, source_target_pairs={{0,16},{1,17},{16,0},{17,1},{32,48},{33,49},{48,32},{49,33},{64,80... | collective-permute-start | bytes 491528 | tf_op jit(solution)/shard_map/ppermute | solution.py:55
  108.7 0.7 shard_map.39
  109.4 0.0 collective-permute-done.6
  109.5 5.6 %collective-permute-start.7 = (bf16[128,640]{1,0:T(8,128)(2,1)S(1)}, bf16[128,640]{1,0:T(8,128)(2,1)S(1)}, u32[]{:S(2)}, u32[]{:S(2)}) collective-permute-start(bf16[128,640]{1,0:T(8,128)(2,1)S(1)} %add_convert_fusion.1), channel_id=1, source_target_pairs={{0,464},{1,81},{16,448},{17,65},{32,496},{33,113},{48,480},{49,97}... | collective-permute-start | bytes 491528 | tf_op jit(solution)/shard_map/ppermute | solution.py:55
  115.1 0.0 collective-permute-done.8
  115.1 0.0 collective-permute-done.9
  115.1 0.0 collective-permute-done.10
  115.1 0.1 add_convert_fusion
  115.2 2.8 %collective-permute-start.11 = (bf16[128,640]{1,0:T(8,128)(2,1)S(1)}, bf16[128,640]{1,0:T(8,128)(2,1)S(1)}, u32[]{:S(2)}, u32[]{:S(2)}) collective-permute-start(bf16[128,640]{1,0:T(8,128)(2,1)S(1)} %add_convert_fusion), channel_id=1, source_target_pairs={{0,96},{1,417},{16,112},{17,433},{32,128},{33,449},{48,144},{49,46... | collective-permute-start | bytes 491528 | tf_op jit(solution)/shard_map/ppermute | solution.py:55
  118.0 6.2 %collective-permute-done.7 = bf16[128,640]{1,0:T(8,128)(2,1)S(1)} collective-permute-done((bf16[128,640]{1,0:T(8,128)(2,1)S(1)}, bf16[128,640]{1,0:T(8,128)(2,1)S(1)}, u32[]{:S(2)}, u32[]{:S(2)}) %collective-permute-start.7) | collective-permute-done | bytes 163872 | tf_op jit(solution)/shard_map/ppermute | solution.py:55
  124.2 5.0 %collective-permute-done.11 = bf16[128,640]{1,0:T(8,128)(2,1)S(1)} collective-permute-done((bf16[128,640]{1,0:T(8,128)(2,1)S(1)}, bf16[128,640]{1,0:T(8,128)(2,1)S(1)}, u32[]{:S(2)}, u32[]{:S(2)}) %collective-permute-start.11) | collective-permute-done | bytes 163872 | tf_op jit(solution)/shard_map/ppermute | solution.py:55
  129.2 0.8 multiply_convert_fusion
  (5 shorter events, 0.1 us)
Async XLA Ops:
  0.0 1.0 copy-start.1
  1.1 35.9 %collective-permute-start.2 = (bf16[128,1664]{1,0:T(8,128)(2,1)S(1)}, bf16[128,1664]{1,0:T(8,128)(2,1)S(1)}, u32[]{:S(2)}, u32[]{:S(2)}) collective-permute-start(bf16[128,1664]{1,0:T(8,128)(2,1)S(1)} %constant_dynamic-update-slice_fusion.refs_0_), channel_id=1, source_target_pairs={{96,0},{417,1},{112,16},{433,17},{128,32},{449,33},{144,48},{465,4... | collective-permute-start | bytes 1277960 | tf_op jit(solution)/shard_map/ppermute | solution.py:51
  13.3 32.7 %collective-permute-start = (bf16[128,1664]{1,0:T(8,128)(2,1)S(1)}, bf16[128,1664]{1,0:T(8,128)(2,1)S(1)}, u32[]{:S(2)}, u32[]{:S(2)}) collective-permute-start(bf16[128,1664]{1,0:T(8,128)(2,1)S(1)} %constant_dynamic-update-slice_fusion.refs_0_), channel_id=1, source_target_pairs={{464,0},{81,1},{448,16},{65,17},{496,32},{113,33},{480,48},{97,49}... | collective-permute-start | bytes 1277960 | tf_op jit(solution)/shard_map/ppermute | solution.py:51
  16.8 0.7 copy-start.2
  36.9 15.8 %collective-permute-start.5 = (bf16[128,1664]{1,0:T(8,128)(2,1)S(1)}, bf16[128,1664]{1,0:T(8,128)(2,1)S(1)}, u32[]{:S(2)}, u32[]{:S(2)}) collective-permute-start(bf16[128,1664]{1,0:T(8,128)(2,1)S(1)} %collective-permute-done.2.refs_3_.refs_4_), channel_id=1, source_target_pairs={{48,0},{497,1},{32,16},{481,17},{80,32},{17,33},{64,48},{1,49},{11... | collective-permute-start | bytes 1277960 | tf_op jit(solution)/shard_map/ppermute | solution.py:51
  40.2 19.4 %collective-permute-start.4 = (bf16[128,1664]{1,0:T(8,128)(2,1)S(1)}, bf16[128,1664]{1,0:T(8,128)(2,1)S(1)}, u32[]{:S(2)}, u32[]{:S(2)}) collective-permute-start(bf16[128,1664]{1,0:T(8,128)(2,1)S(1)} %collective-permute-done.2.refs_3_.refs_4_), channel_id=1, source_target_pairs={{32,0},{481,1},{48,16},{497,17},{64,32},{1,33},{80,48},{17,49},{96... | collective-permute-start | bytes 1277960 | tf_op jit(solution)/shard_map/ppermute | solution.py:51
  44.1 15.6 %collective-permute-start.3 = (bf16[128,1664]{1,0:T(8,128)(2,1)S(1)}, bf16[128,1664]{1,0:T(8,128)(2,1)S(1)}, u32[]{:S(2)}, u32[]{:S(2)}) collective-permute-start(bf16[128,1664]{1,0:T(8,128)(2,1)S(1)} %collective-permute-done.2.refs_3_.refs_4_), channel_id=1, source_target_pairs={{16,0},{17,1},{0,16},{1,17},{48,32},{49,33},{32,48},{33,49},{80,64... | collective-permute-start | bytes 1277960 | tf_op jit(solution)/shard_map/ppermute | solution.py:51
  46.0 13.7 %collective-permute-start.1 = (bf16[128,1664]{1,0:T(8,128)(2,1)S(1)}, bf16[128,1664]{1,0:T(8,128)(2,1)S(1)}, u32[]{:S(2)}, u32[]{:S(2)}) collective-permute-start(bf16[128,1664]{1,0:T(8,128)(2,1)S(1)} %collective-permute-done.refs_1_.refs_2_), channel_id=1, source_target_pairs={{448,0},{65,1},{464,16},{81,17},{480,32},{97,33},{496,48},{113,49}... | collective-permute-start | bytes 1277960 | tf_op jit(solution)/shard_map/ppermute | solution.py:51
  79.4 13.2 %copy-start = (bf16[128,640]{1,0:T(8,128)(2,1)S(1)}, bf16[128,640]{1,0:T(8,128)(2,1)}, u32[]{:S(2)}) copy-start(bf16[128,640]{1,0:T(8,128)(2,1)} %refs_1_.3) | copy-start | bytes 491524
  93.3 16.2 %collective-permute-start.6 = (bf16[128,640]{1,0:T(8,128)(2,1)S(1)}, bf16[128,640]{1,0:T(8,128)(2,1)S(1)}, u32[]{:S(2)}, u32[]{:S(2)}) collective-permute-start(bf16[128,640]{1,0:T(8,128)(2,1)S(1)} %get-tuple-element.31), channel_id=1, source_target_pairs={{0,448},{1,65},{16,464},{17,81},{32,480},{33,97},{48,496},{49,113}... | collective-permute-start | bytes 491528 | tf_op jit(solution)/shard_map/ppermute | solution.py:55
  99.7 15.4 %collective-permute-start.8 = (bf16[128,640]{1,0:T(8,128)(2,1)S(1)}, bf16[128,640]{1,0:T(8,128)(2,1)S(1)}, u32[]{:S(2)}, u32[]{:S(2)}) collective-permute-start(bf16[128,640]{1,0:T(8,128)(2,1)S(1)} %get-tuple-element.33), channel_id=1, source_target_pairs={{0,48},{1,497},{16,32},{17,481},{32,80},{33,17},{48,64},{49,1},{64... | collective-permute-start | bytes 491528 | tf_op jit(solution)/shard_map/ppermute | solution.py:55
  104.2 10.9 %collective-permute-start.9 = (bf16[128,640]{1,0:T(8,128)(2,1)S(1)}, bf16[128,640]{1,0:T(8,128)(2,1)S(1)}, u32[]{:S(2)}, u32[]{:S(2)}) collective-permute-start(bf16[128,640]{1,0:T(8,128)(2,1)S(1)} %get-tuple-element.34), channel_id=1, source_target_pairs={{0,32},{1,481},{16,48},{17,497},{32,64},{33,1},{48,80},{49,17},{64... | collective-permute-start | bytes 491528 | tf_op jit(solution)/shard_map/ppermute | solution.py:55
  106.1 9.0 %collective-permute-start.10 = (bf16[128,640]{1,0:T(8,128)(2,1)S(1)}, bf16[128,640]{1,0:T(8,128)(2,1)S(1)}, u32[]{:S(2)}, u32[]{:S(2)}) collective-permute-start(bf16[128,640]{1,0:T(8,128)(2,1)S(1)} %get-tuple-element.35), channel_id=1, source_target_pairs={{0,16},{1,17},{16,0},{17,1},{32,48},{33,49},{48,32},{49,33},{64,80... | collective-permute-start | bytes 491528 | tf_op jit(solution)/shard_map/ppermute | solution.py:55
  109.5 14.7 %collective-permute-start.7 = (bf16[128,640]{1,0:T(8,128)(2,1)S(1)}, bf16[128,640]{1,0:T(8,128)(2,1)S(1)}, u32[]{:S(2)}, u32[]{:S(2)}) collective-permute-start(bf16[128,640]{1,0:T(8,128)(2,1)S(1)} %add_convert_fusion.1), channel_id=1, source_target_pairs={{0,464},{1,81},{16,448},{17,65},{32,496},{33,113},{48,480},{49,97}... | collective-permute-start | bytes 491528 | tf_op jit(solution)/shard_map/ppermute | solution.py:55
  115.2 14.0 %collective-permute-start.11 = (bf16[128,640]{1,0:T(8,128)(2,1)S(1)}, bf16[128,640]{1,0:T(8,128)(2,1)S(1)}, u32[]{:S(2)}, u32[]{:S(2)}) collective-permute-start(bf16[128,640]{1,0:T(8,128)(2,1)S(1)} %add_convert_fusion), channel_id=1, source_target_pairs={{0,96},{1,417},{16,112},{17,433},{32,128},{33,449},{48,144},{49,46... | collective-permute-start | bytes 491528 | tf_op jit(solution)/shard_map/ppermute | solution.py:55

commit v9 on v7

--- a/solution.py
+++ b/solution.py
@@ -191,22 +191,16 @@
     far = [e for e, _, _ in SECOND]
     near = [0] + [e for e, _, _ in FIRST]
     block = 2 * rows * rows * ds
-    given = call(
-        lambda *refs: gradient_kernel(far, *refs),
-        [jax.ShapeDtypeStruct((rows, ds), BF16)] * len(far),
-        14 * block,
+    both = call(
+        lambda *refs: gradient_kernel(far + near, *refs),
+        [jax.ShapeDtypeStruct((rows, ds), BF16)] * len(far)
+        + [jax.ShapeDtypeStruct((rows, ds), F32)] * len(near),
+        32 * block,
         tiles,
         student,
         *blocks[1:],
     )
-    kept = call(
-        lambda *refs: gradient_kernel(near, *refs),
-        [jax.ShapeDtypeStruct((rows, ds), F32)] * len(near),
-        18 * block,
-        tiles,
-        student,
-        *blocks[1:],
-    )
+    given, kept = both[: len(far)], both[len(far) :]
     sums = dict(zip(near, kept, strict=True))
     for (_, target, step), value in zip(SECOND, given, strict=True):
         sums[target] = sums[target] + give(value, step).astype(F32)

time: 131 us -> 130 us (level)
  waiting for transfers between devices: 38.5 us -> 37.1 us
    ppermute x6, waiting for transfers between devices: 11.2 us -> 9.81 us  [give(): return lax.ppermute(block, ROW, moves(step, True))]
    pallas_call x4 -> x3, Pallas kernels: 3.66 us -> 3.49 us  [call(): pl.pallas_call(kernel, out_shape=out_shape, in_specs=specs, out_specs=[vm...]
  transfers between devices with their start and end apart: 12 -> 12, of which waited for: 6 -> 6; matrix products, arithmetic and copies ran while one was open for 2% -> 2% of each run, Pallas kernels for 1% -> 0%
where the time goes in v9:
time: 130 us; the launch traced here: 129 us
  starting transfers between devices  53 us (41%)
  waiting for transfers between devices  37.1 us (29%)
  blocking collectives  30.6 us (24%)
  local copies, waits for them, and re-layouts  3.64 us (3%)
  Pallas kernels  3.49 us (3%)
    ppermute x6, starting transfers between devices, fetch(): return lax.ppermute(block, ROW, moves(step, False))  28.2 us
    ppermute x6, waiting for transfers between devices, fetch(): return lax.ppermute(block, ROW, moves(step, False))  27.3 us
    ppermute x6, starting transfers between devices, give(): return lax.ppermute(block, ROW, moves(step, True))  24.8 us
    all_to_all x1, blocking collectives, on_device(): parts = lax.all_to_all(partial, TENSOR, 0, 0)  17.4 us
    all_to_all x1, blocking collectives, on_device(): tiles = lax.all_to_all(copies, TENSOR, 0, 0)  13.2 us
    ppermute x6, waiting for transfers between devices, give(): return lax.ppermute(block, ROW, moves(step, True))  9.81 us
    pallas_call x3, Pallas kernels, call(): pl.pallas_call(kernel, out_shape=out_shape, in_specs=specs, out_specs=[vm...  3.49 us
  transfers between devices with their start and end apart: 12, of which 6 were waited for; matrix products, arithmetic and copies ran while one was open for 2% of the time, Pallas kernels for 0%

profile of v9, /device:TPU:2, one launch (start us, length us, event | category | flops | bytes accessed | tf_op | source)
XLA Modules:
  0.0 129.4 jit_solution(16977289692400864388)
XLA Ops:
  0.0 0.0 copy-start.1
  0.0 1.0 constant_dynamic-update-slice_fusion.1
  1.0 0.0 copy-done.1
  1.1 12.3 %collective-permute-start.2 = (bf16[128,1664]{1,0:T(8,128)(2,1)S(1)}, bf16[128,1664]{1,0:T(8,128)(2,1)S(1)}, u32[]{:S(2)}, u32[]{:S(2)}) collective-permute-start(bf16[128,1664]{1,0:T(8,128)(2,1)S(1)} %constant_dynamic-update-slice_fusion.refs_0_), channel_id=1, source_target_pairs={{96,0},{417,1},{112,16},{433,17},{128,32},{449,33},{144,48},{465,4... | collective-permute-start | bytes 1277960 | tf_op jit(solution)/shard_map/ppermute | solution.py:44
  13.3 3.4 %collective-permute-start = (bf16[128,1664]{1,0:T(8,128)(2,1)S(1)}, bf16[128,1664]{1,0:T(8,128)(2,1)S(1)}, u32[]{:S(2)}, u32[]{:S(2)}) collective-permute-start(bf16[128,1664]{1,0:T(8,128)(2,1)S(1)} %constant_dynamic-update-slice_fusion.refs_0_), channel_id=1, source_target_pairs={{464,0},{81,1},{448,16},{65,17},{496,32},{113,33},{480,48},{97,49}... | collective-permute-start | bytes 1277960 | tf_op jit(solution)/shard_map/ppermute | solution.py:44
  16.8 0.0 copy-start.2
  16.8 0.6 copy-done.2
  17.5 0.2 reduce-window.4
  17.6 0.6 fusion.1
  18.2 1.4 %stack.35.where_ref = s32[10]{0:T(128)S(1)} concatenate(s32[1]{0:T(128)} %bitcast.1, s32[1]{0:T(128)} %bitcast.2, s32[1]{0:T(128)} %bitcast.3, s32[1]{0:T(128)} %bitcast.4, s32[1]{0:T(128)} %bitcast.5, s32[1]{0:T(128)} %bitcast.6, s32[1]{0:T(128)} %bitcast.7, s32[1]{0:T(128)} %bitcast.8, s32[1]{0:T(128)} %bitcast.9, s32[1]{0:T(128)} %bitcast.10), dimensions={0} | concatenate | bytes 80 | tf_op jit(solution)/shard_map/stack | solution.py:164
  19.6 17.3 %collective-permute-done.2.refs_3_.refs_4_ = bf16[128,1664]{1,0:T(8,128)(2,1)S(1)} collective-permute-done((bf16[128,1664]{1,0:T(8,128)(2,1)S(1)}, bf16[128,1664]{1,0:T(8,128)(2,1)S(1)}, u32[]{:S(2)}, u32[]{:S(2)}) %collective-permute-start.2) | collective-permute-done | bytes 426016 | tf_op jit(solution)/shard_map/ppermute | solution.py:44
  36.9 3.3 %collective-permute-start.5 = (bf16[128,1664]{1,0:T(8,128)(2,1)S(1)}, bf16[128,1664]{1,0:T(8,128)(2,1)S(1)}, u32[]{:S(2)}, u32[]{:S(2)}) collective-permute-start(bf16[128,1664]{1,0:T(8,128)(2,1)S(1)} %collective-permute-done.2.refs_3_.refs_4_), channel_id=1, source_target_pairs={{48,0},{497,1},{32,16},{481,17},{80,32},{17,33},{64,48},{1,49},{11... | collective-permute-start | bytes 1277960 | tf_op jit(solution)/shard_map/ppermute | solution.py:44
  40.2 3.8 %collective-permute-start.4 = (bf16[128,1664]{1,0:T(8,128)(2,1)S(1)}, bf16[128,1664]{1,0:T(8,128)(2,1)S(1)}, u32[]{:S(2)}, u32[]{:S(2)}) collective-permute-start(bf16[128,1664]{1,0:T(8,128)(2,1)S(1)} %collective-permute-done.2.refs_3_.refs_4_), channel_id=1, source_target_pairs={{32,0},{481,1},{48,16},{497,17},{64,32},{1,33},{80,48},{17,49},{96... | collective-permute-start | bytes 1277960 | tf_op jit(solution)/shard_map/ppermute | solution.py:44
  44.1 1.9 %collective-permute-start.3 = (bf16[128,1664]{1,0:T(8,128)(2,1)S(1)}, bf16[128,1664]{1,0:T(8,128)(2,1)S(1)}, u32[]{:S(2)}, u32[]{:S(2)}) collective-permute-start(bf16[128,1664]{1,0:T(8,128)(2,1)S(1)} %collective-permute-done.2.refs_3_.refs_4_), channel_id=1, source_target_pairs={{16,0},{17,1},{0,16},{1,17},{48,32},{49,33},{32,48},{33,49},{80,64... | collective-permute-start | bytes 1277960 | tf_op jit(solution)/shard_map/ppermute | solution.py:44
  46.0 0.0 collective-permute-done.refs_1_.refs_2_
  46.0 3.5 %collective-permute-start.1 = (bf16[128,1664]{1,0:T(8,128)(2,1)S(1)}, bf16[128,1664]{1,0:T(8,128)(2,1)S(1)}, u32[]{:S(2)}, u32[]{:S(2)}) collective-permute-start(bf16[128,1664]{1,0:T(8,128)(2,1)S(1)} %collective-permute-done.refs_1_.refs_2_), channel_id=1, source_target_pairs={{448,0},{65,1},{464,16},{81,17},{480,32},{97,33},{496,48},{113,49}... | collective-permute-start | bytes 1277960 | tf_op jit(solution)/shard_map/ppermute | solution.py:44
  49.5 0.1 fusion
  49.6 0.1 select_reduce_fusion
  49.7 3.0 %collective-permute-done.5.refs_6_.refs_7_ = bf16[128,1664]{1,0:T(8,128)(2,1)S(1)} collective-permute-done((bf16[128,1664]{1,0:T(8,128)(2,1)S(1)}, bf16[128,1664]{1,0:T(8,128)(2,1)S(1)}, u32[]{:S(2)}, u32[]{:S(2)}) %collective-permute-start.5) | collective-permute-done | bytes 426016 | tf_op jit(solution)/shard_map/ppermute | solution.py:44
  52.7 6.9 %collective-permute-done.4.refs_5_.refs_6_ = bf16[128,1664]{1,0:T(8,128)(2,1)S(1)} collective-permute-done((bf16[128,1664]{1,0:T(8,128)(2,1)S(1)}, bf16[128,1664]{1,0:T(8,128)(2,1)S(1)}, u32[]{:S(2)}, u32[]{:S(2)}) %collective-permute-start.4) | collective-permute-done | bytes 426016 | tf_op jit(solution)/shard_map/ppermute | solution.py:44
  59.6 0.0 collective-permute-done.3.refs_4_.refs_5_
  59.6 0.1 collective-permute-done.1.refs_2_.refs_3_
  59.7 1.6 %shard_map.37 = bf16[8,288,128]{2,1,0:T(8,128)(2,1)S(1)} custom-call(bf16[128,1664]{1,0:T(8,128)(2,1)S(1)} %constant_dynamic-update-slice_fusion.refs_0_, bf16[128,1664]{1,0:T(8,128)(2,1)S(1)} %collective-permute-done.refs_1_.refs_2_, bf16[128,1664]{1,0:T(8,128)(2,1)S(1)} %collective-permute-done.1.refs_2_.refs_3_, ...), custom_call_target="tpu_custom_call" | custom-call | flops 981467136 | bytes 2981888 | tf_op jit(solution)/shard_map/pallas_call | solution.py:143
  61.3 17.4 %all_to_all.10.parts = bf16[8,288,128]{2,1,0:T(8,128)(2,1)S(1)} all-to-all(bf16[8,288,128]{2,1,0:T(8,128)(2,1)S(1)} %shard_map.37), channel_id=1, replica_groups=mesh['z'=16,'xl'=2,'y'=4,'xh'=2,'seq'=2] {'y','xh'}, dimensions={0} | all-to-all | bytes 1179648 | tf_op jit(solution)/shard_map/all_to_all | solution.py:180
  78.7 0.7 shard_map.38
  79.4 0.0 copy-start
  79.4 13.2 %all_to_all.11.refs_0_ = bf16[8,288,128]{2,1,0:T(8,128)(2,1)S(1)} all-to-all(bf16[8,288,128]{2,1,0:T(8,128)(2,1)S(1)} %shard_map.38), channel_id=1, replica_groups=mesh['z'=16,'xl'=2,'y'=4,'xh'=2,'seq'=2] {'y','xh'}, dimensions={0} | all-to-all | bytes 1179648 | tf_op jit(solution)/shard_map/all_to_all | solution.py:189
  92.6 0.0 copy-done
  92.6 1.2 shard_map.39
  93.9 6.5 %collective-permute-start.6 = (bf16[128,640]{1,0:T(8,128)(2,1)S(1)}, bf16[128,640]{1,0:T(8,128)(2,1)S(1)}, u32[]{:S(2)}, u32[]{:S(2)}) collective-permute-start(bf16[128,640]{1,0:T(8,128)(2,1)S(1)} %get-tuple-element.31), channel_id=1, source_target_pairs={{0,448},{1,65},{16,464},{17,81},{32,480},{33,97},{48,496},{49,113}... | collective-permute-start | bytes 491528 | tf_op jit(solution)/shard_map/ppermute | solution.py:48
  100.3 4.4 %collective-permute-start.8 = (bf16[128,640]{1,0:T(8,128)(2,1)S(1)}, bf16[128,640]{1,0:T(8,128)(2,1)S(1)}, u32[]{:S(2)}, u32[]{:S(2)}) collective-permute-start(bf16[128,640]{1,0:T(8,128)(2,1)S(1)} %get-tuple-element.33), channel_id=1, source_target_pairs={{0,48},{1,497},{16,32},{17,481},{32,80},{33,17},{48,64},{49,1},{64... | collective-permute-start | bytes 491528 | tf_op jit(solution)/shard_map/ppermute | solution.py:48
  104.8 1.9 %collective-permute-start.9 = (bf16[128,640]{1,0:T(8,128)(2,1)S(1)}, bf16[128,640]{1,0:T(8,128)(2,1)S(1)}, u32[]{:S(2)}, u32[]{:S(2)}) collective-permute-start(bf16[128,640]{1,0:T(8,128)(2,1)S(1)} %get-tuple-element.34), channel_id=1, source_target_pairs={{0,32},{1,481},{16,48},{17,497},{32,64},{33,1},{48,80},{49,17},{64... | collective-permute-start | bytes 491528 | tf_op jit(solution)/shard_map/ppermute | solution.py:48
  106.7 2.6 %collective-permute-start.10 = (bf16[128,640]{1,0:T(8,128)(2,1)S(1)}, bf16[128,640]{1,0:T(8,128)(2,1)S(1)}, u32[]{:S(2)}, u32[]{:S(2)}) collective-permute-start(bf16[128,640]{1,0:T(8,128)(2,1)S(1)} %get-tuple-element.35), channel_id=1, source_target_pairs={{0,16},{1,17},{16,0},{17,1},{32,48},{33,49},{48,32},{49,33},{64,80... | collective-permute-start | bytes 491528 | tf_op jit(solution)/shard_map/ppermute | solution.py:48
  109.3 0.0 collective-permute-done.6
  109.4 5.6 %collective-permute-start.7 = (bf16[128,640]{1,0:T(8,128)(2,1)S(1)}, bf16[128,640]{1,0:T(8,128)(2,1)S(1)}, u32[]{:S(2)}, u32[]{:S(2)}) collective-permute-start(bf16[128,640]{1,0:T(8,128)(2,1)S(1)} %add_convert_fusion.1), channel_id=1, source_target_pairs={{0,464},{1,81},{16,448},{17,65},{32,496},{33,113},{48,480},{49,97}... | collective-permute-start | bytes 491528 | tf_op jit(solution)/shard_map/ppermute | solution.py:48
  115.0 0.0 collective-permute-done.8
  115.0 0.0 collective-permute-done.9
  115.0 0.0 collective-permute-done.10
  115.0 0.1 add_convert_fusion
  115.1 3.8 %collective-permute-start.11 = (bf16[128,640]{1,0:T(8,128)(2,1)S(1)}, bf16[128,640]{1,0:T(8,128)(2,1)S(1)}, u32[]{:S(2)}, u32[]{:S(2)}) collective-permute-start(bf16[128,640]{1,0:T(8,128)(2,1)S(1)} %add_convert_fusion), channel_id=1, source_target_pairs={{0,96},{1,417},{16,112},{17,433},{32,128},{33,449},{48,144},{49,46... | collective-permute-start | bytes 491528 | tf_op jit(solution)/shard_map/ppermute | solution.py:48
  118.8 5.4 %collective-permute-done.7 = bf16[128,640]{1,0:T(8,128)(2,1)S(1)} collective-permute-done((bf16[128,640]{1,0:T(8,128)(2,1)S(1)}, bf16[128,640]{1,0:T(8,128)(2,1)S(1)}, u32[]{:S(2)}, u32[]{:S(2)}) %collective-permute-start.7) | collective-permute-done | bytes 163872 | tf_op jit(solution)/shard_map/ppermute | solution.py:48
  124.2 4.4 %collective-permute-done.11 = bf16[128,640]{1,0:T(8,128)(2,1)S(1)} collective-permute-done((bf16[128,640]{1,0:T(8,128)(2,1)S(1)}, bf16[128,640]{1,0:T(8,128)(2,1)S(1)}, u32[]{:S(2)}, u32[]{:S(2)}) %collective-permute-start.11) | collective-permute-done | bytes 163872 | tf_op jit(solution)/shard_map/ppermute | solution.py:48
  128.6 0.8 multiply_convert_fusion
  (5 shorter events, 0.1 us)
Async XLA Ops:
  0.0 1.0 copy-start.1
  1.1 35.9 %collective-permute-start.2 = (bf16[128,1664]{1,0:T(8,128)(2,1)S(1)}, bf16[128,1664]{1,0:T(8,128)(2,1)S(1)}, u32[]{:S(2)}, u32[]{:S(2)}) collective-permute-start(bf16[128,1664]{1,0:T(8,128)(2,1)S(1)} %constant_dynamic-update-slice_fusion.refs_0_), channel_id=1, source_target_pairs={{96,0},{417,1},{112,16},{433,17},{128,32},{449,33},{144,48},{465,4... | collective-permute-start | bytes 1277960 | tf_op jit(solution)/shard_map/ppermute | solution.py:44
  13.3 32.7 %collective-permute-start = (bf16[128,1664]{1,0:T(8,128)(2,1)S(1)}, bf16[128,1664]{1,0:T(8,128)(2,1)S(1)}, u32[]{:S(2)}, u32[]{:S(2)}) collective-permute-start(bf16[128,1664]{1,0:T(8,128)(2,1)S(1)} %constant_dynamic-update-slice_fusion.refs_0_), channel_id=1, source_target_pairs={{464,0},{81,1},{448,16},{65,17},{496,32},{113,33},{480,48},{97,49}... | collective-permute-start | bytes 1277960 | tf_op jit(solution)/shard_map/ppermute | solution.py:44
  16.8 0.7 copy-start.2
  36.9 15.8 %collective-permute-start.5 = (bf16[128,1664]{1,0:T(8,128)(2,1)S(1)}, bf16[128,1664]{1,0:T(8,128)(2,1)S(1)}, u32[]{:S(2)}, u32[]{:S(2)}) collective-permute-start(bf16[128,1664]{1,0:T(8,128)(2,1)S(1)} %collective-permute-done.2.refs_3_.refs_4_), channel_id=1, source_target_pairs={{48,0},{497,1},{32,16},{481,17},{80,32},{17,33},{64,48},{1,49},{11... | collective-permute-start | bytes 1277960 | tf_op jit(solution)/shard_map/ppermute | solution.py:44
  40.2 19.4 %collective-permute-start.4 = (bf16[128,1664]{1,0:T(8,128)(2,1)S(1)}, bf16[128,1664]{1,0:T(8,128)(2,1)S(1)}, u32[]{:S(2)}, u32[]{:S(2)}) collective-permute-start(bf16[128,1664]{1,0:T(8,128)(2,1)S(1)} %collective-permute-done.2.refs_3_.refs_4_), channel_id=1, source_target_pairs={{32,0},{481,1},{48,16},{497,17},{64,32},{1,33},{80,48},{17,49},{96... | collective-permute-start | bytes 1277960 | tf_op jit(solution)/shard_map/ppermute | solution.py:44
  44.1 15.6 %collective-permute-start.3 = (bf16[128,1664]{1,0:T(8,128)(2,1)S(1)}, bf16[128,1664]{1,0:T(8,128)(2,1)S(1)}, u32[]{:S(2)}, u32[]{:S(2)}) collective-permute-start(bf16[128,1664]{1,0:T(8,128)(2,1)S(1)} %collective-permute-done.2.refs_3_.refs_4_), channel_id=1, source_target_pairs={{16,0},{17,1},{0,16},{1,17},{48,32},{49,33},{32,48},{33,49},{80,64... | collective-permute-start | bytes 1277960 | tf_op jit(solution)/shard_map/ppermute | solution.py:44
  46.0 13.7 %collective-permute-start.1 = (bf16[128,1664]{1,0:T(8,128)(2,1)S(1)}, bf16[128,1664]{1,0:T(8,128)(2,1)S(1)}, u32[]{:S(2)}, u32[]{:S(2)}) collective-permute-start(bf16[128,1664]{1,0:T(8,128)(2,1)S(1)} %collective-permute-done.refs_1_.refs_2_), channel_id=1, source_target_pairs={{448,0},{65,1},{464,16},{81,17},{480,32},{97,33},{496,48},{113,49}... | collective-permute-start | bytes 1277960 | tf_op jit(solution)/shard_map/ppermute | solution.py:44
  79.4 13.2 %copy-start = (bf16[128,640]{1,0:T(8,128)(2,1)S(1)}, bf16[128,640]{1,0:T(8,128)(2,1)}, u32[]{:S(2)}) copy-start(bf16[128,640]{1,0:T(8,128)(2,1)} %refs_1_.1) | copy-start | bytes 491524
  93.9 15.5 %collective-permute-start.6 = (bf16[128,640]{1,0:T(8,128)(2,1)S(1)}, bf16[128,640]{1,0:T(8,128)(2,1)S(1)}, u32[]{:S(2)}, u32[]{:S(2)}) collective-permute-start(bf16[128,640]{1,0:T(8,128)(2,1)S(1)} %get-tuple-element.31), channel_id=1, source_target_pairs={{0,448},{1,65},{16,464},{17,81},{32,480},{33,97},{48,496},{49,113}... | collective-permute-start | bytes 491528 | tf_op jit(solution)/shard_map/ppermute | solution.py:48
  100.3 14.6 %collective-permute-start.8 = (bf16[128,640]{1,0:T(8,128)(2,1)S(1)}, bf16[128,640]{1,0:T(8,128)(2,1)S(1)}, u32[]{:S(2)}, u32[]{:S(2)}) collective-permute-start(bf16[128,640]{1,0:T(8,128)(2,1)S(1)} %get-tuple-element.33), channel_id=1, source_target_pairs={{0,48},{1,497},{16,32},{17,481},{32,80},{33,17},{48,64},{49,1},{64... | collective-permute-start | bytes 491528 | tf_op jit(solution)/shard_map/ppermute | solution.py:48
  104.8 10.2 %collective-permute-start.9 = (bf16[128,640]{1,0:T(8,128)(2,1)S(1)}, bf16[128,640]{1,0:T(8,128)(2,1)S(1)}, u32[]{:S(2)}, u32[]{:S(2)}) collective-permute-start(bf16[128,640]{1,0:T(8,128)(2,1)S(1)} %get-tuple-element.34), channel_id=1, source_target_pairs={{0,32},{1,481},{16,48},{17,497},{32,64},{33,1},{48,80},{49,17},{64... | collective-permute-start | bytes 491528 | tf_op jit(solution)/shard_map/ppermute | solution.py:48
  106.7 8.3 %collective-permute-start.10 = (bf16[128,640]{1,0:T(8,128)(2,1)S(1)}, bf16[128,640]{1,0:T(8,128)(2,1)S(1)}, u32[]{:S(2)}, u32[]{:S(2)}) collective-permute-start(bf16[128,640]{1,0:T(8,128)(2,1)S(1)} %get-tuple-element.35), channel_id=1, source_target_pairs={{0,16},{1,17},{16,0},{17,1},{32,48},{33,49},{48,32},{49,33},{64,80... | collective-permute-start | bytes 491528 | tf_op jit(solution)/shard_map/ppermute | solution.py:48
  109.4 14.8 %collective-permute-start.7 = (bf16[128,640]{1,0:T(8,128)(2,1)S(1)}, bf16[128,640]{1,0:T(8,128)(2,1)S(1)}, u32[]{:S(2)}, u32[]{:S(2)}) collective-permute-start(bf16[128,640]{1,0:T(8,128)(2,1)S(1)} %add_convert_fusion.1), channel_id=1, source_target_pairs={{0,464},{1,81},{16,448},{17,65},{32,496},{33,113},{48,480},{49,97}... | collective-permute-start | bytes 491528 | tf_op jit(solution)/shard_map/ppermute | solution.py:48
  115.1 13.6 %collective-permute-start.11 = (bf16[128,640]{1,0:T(8,128)(2,1)S(1)}, bf16[128,640]{1,0:T(8,128)(2,1)S(1)}, u32[]{:S(2)}, u32[]{:S(2)}) collective-permute-start(bf16[128,640]{1,0:T(8,128)(2,1)S(1)} %add_convert_fusion), channel_id=1, source_target_pairs={{0,96},{1,417},{16,112},{17,433},{32,128},{33,449},{48,144},{49,46... | collective-permute-start | bytes 491528 | tf_op jit(solution)/shard_map/ppermute | solution.py:48

commit v10 on v8

--- a/solution.py
+++ b/solution.py
@@ -21,14 +21,8 @@
     (3, 4), (3, 5), (3, 6),
 )
 BATCHES = (((0, 1, 2), (3, 4, 5, 6)), ((3,), (4, 5, 6)), ((0,), (0, 1)), ((1,), (2,)))
-FAR = (
-    (((2,), (3, 4, 5, 6)),),
-    (((0, 1), (4, 5, 6)), ((2,), (4,)), ((3,), (5, 6)), ((1,), (2,))),
-)
-NEAR = (
-    (((0, 1), (3, 4, 5, 6)), ((0,), (0, 1)), ((1,), (2,)), ((3,), (4, 5, 6))),
-    (((0, 1, 2), (3,)), ((0,), (1,))),
-)
+STRAIGHT = (((0, 1, 2), (3, 4, 5, 6)), ((0,), (0, 1)), ((1,), (2,)), ((3,), (4, 5, 6)))
+TURNED = (((0, 1), (3, 4, 5, 6)), ((2,), (3, 4)), ((0,), (1,)), ((1,), (2,)), ((3,), (5, 6)))
 F32, BF16 = jnp.float32, jnp.bfloat16
 
 
@@ -202,22 +196,16 @@
     far = [e for e, _, _ in SECOND]
     near = [0] + [e for e, _, _ in FIRST]
     block = 2 * rows * rows * ds
-    given = call(
-        lambda *refs: gradient_kernel(far, *FAR, *refs),
-        [jax.ShapeDtypeStruct((rows, ds), BF16)] * len(far),
-        14 * block,
+    both = call(
+        lambda *refs: gradient_kernel(far + near, STRAIGHT, TURNED, *refs),
+        [jax.ShapeDtypeStruct((rows, ds), BF16)] * len(far)
+        + [jax.ShapeDtypeStruct((rows, ds), F32)] * len(near),
+        32 * block,
         tiles,
         student,
         *blocks[1:],
     )
-    kept = call(
-        lambda *refs: gradient_kernel(near, *NEAR, *refs),
-        [jax.ShapeDtypeStruct((rows, ds), F32)] * len(near),
-        18 * block,
-        tiles,
-        student,
-        *blocks[1:],
-    )
+    given, kept = both[: len(far)], both[len(far) :]
     sums = dict(zip(near, kept, strict=True))
     for (_, target, step), value in zip(SECOND, given, strict=True):
         sums[target] = sums[target] + give(value, step).astype(F32)

time: 131 us -> 130 us (level)
  waiting for transfers between devices: 38.5 us -> 37.1 us
    ppermute x6, waiting for transfers between devices: 11.2 us -> 9.79 us  [give(): return lax.ppermute(block, ROW, moves(step, True))]
    pallas_call x4 -> x3, Pallas kernels: 3.6 us -> 3.39 us  [call(): pl.pallas_call(kernel, out_shape=out_shape, in_specs=specs, out_specs=[vm...]
  transfers between devices with their start and end apart: 12 -> 12, of which waited for: 6 -> 6; matrix products, arithmetic and copies ran while one was open for 2% -> 2% of each run, Pallas kernels for 1% -> 0%
where the time goes in v10:
time: 130 us; the launch traced here: 129 us
  starting transfers between devices  53 us (41%)
  waiting for transfers between devices  37.1 us (29%)
  blocking collectives  30.6 us (24%)
  local copies, waits for them, and re-layouts  3.64 us (3%)
  Pallas kernels  3.39 us (3%)
    ppermute x6, starting transfers between devices, fetch(): return lax.ppermute(block, ROW, moves(step, False))  28.2 us
    ppermute x6, waiting for transfers between devices, fetch(): return lax.ppermute(block, ROW, moves(step, False))  27.3 us
    ppermute x6, starting transfers between devices, give(): return lax.ppermute(block, ROW, moves(step, True))  24.8 us
    all_to_all x1, blocking collectives, on_device(): parts = lax.all_to_all(partial, TENSOR, 0, 0)  17.4 us
    all_to_all x1, blocking collectives, on_device(): tiles = lax.all_to_all(copies, TENSOR, 0, 0)  13.2 us
    ppermute x6, waiting for transfers between devices, give(): return lax.ppermute(block, ROW, moves(step, True))  9.79 us
    pallas_call x3, Pallas kernels, call(): pl.pallas_call(kernel, out_shape=out_shape, in_specs=specs, out_specs=[vm...  3.39 us
  transfers between devices with their start and end apart: 12, of which 6 were waited for; matrix products, arithmetic and copies ran while one was open for 2% of the time, Pallas kernels for 0%

profile of v10, /device:TPU:2, one launch (start us, length us, event | category | flops | bytes accessed | tf_op | source)
XLA Modules:
  0.0 129.3 jit_solution(5933601167100880498)
XLA Ops:
  0.0 0.0 copy-start.1
  0.0 1.0 constant_dynamic-update-slice_fusion.1
  1.0 0.0 copy-done.1
  1.1 12.3 %collective-permute-start.2 = (bf16[128,1664]{1,0:T(8,128)(2,1)S(1)}, bf16[128,1664]{1,0:T(8,128)(2,1)S(1)}, u32[]{:S(2)}, u32[]{:S(2)}) collective-permute-start(bf16[128,1664]{1,0:T(8,128)(2,1)S(1)} %constant_dynamic-update-slice_fusion.refs_0_), channel_id=1, source_target_pairs={{96,0},{417,1},{112,16},{433,17},{128,32},{449,33},{144,48},{465,4... | collective-permute-start | bytes 1277960 | tf_op jit(solution)/shard_map/ppermute | solution.py:45
  13.3 3.4 %collective-permute-start = (bf16[128,1664]{1,0:T(8,128)(2,1)S(1)}, bf16[128,1664]{1,0:T(8,128)(2,1)S(1)}, u32[]{:S(2)}, u32[]{:S(2)}) collective-permute-start(bf16[128,1664]{1,0:T(8,128)(2,1)S(1)} %constant_dynamic-update-slice_fusion.refs_0_), channel_id=1, source_target_pairs={{464,0},{81,1},{448,16},{65,17},{496,32},{113,33},{480,48},{97,49}... | collective-permute-start | bytes 1277960 | tf_op jit(solution)/shard_map/ppermute | solution.py:45
  16.8 0.0 copy-start.2
  16.8 0.6 copy-done.2
  17.5 0.2 reduce-window.4
  17.6 0.6 fusion.1
  18.2 1.4 %stack.35.where_ref = s32[10]{0:T(128)S(1)} concatenate(s32[1]{0:T(128)} %bitcast.1, s32[1]{0:T(128)} %bitcast.2, s32[1]{0:T(128)} %bitcast.3, s32[1]{0:T(128)} %bitcast.4, s32[1]{0:T(128)} %bitcast.5, s32[1]{0:T(128)} %bitcast.6, s32[1]{0:T(128)} %bitcast.7, s32[1]{0:T(128)} %bitcast.8, s32[1]{0:T(128)} %bitcast.9, s32[1]{0:T(128)} %bitcast.10), dimensions={0} | concatenate | bytes 80 | tf_op jit(solution)/shard_map/stack | solution.py:169
  19.6 17.3 %collective-permute-done.2.refs_3_.refs_4_ = bf16[128,1664]{1,0:T(8,128)(2,1)S(1)} collective-permute-done((bf16[128,1664]{1,0:T(8,128)(2,1)S(1)}, bf16[128,1664]{1,0:T(8,128)(2,1)S(1)}, u32[]{:S(2)}, u32[]{:S(2)}) %collective-permute-start.2) | collective-permute-done | bytes 426016 | tf_op jit(solution)/shard_map/ppermute | solution.py:45
  36.9 3.3 %collective-permute-start.5 = (bf16[128,1664]{1,0:T(8,128)(2,1)S(1)}, bf16[128,1664]{1,0:T(8,128)(2,1)S(1)}, u32[]{:S(2)}, u32[]{:S(2)}) collective-permute-start(bf16[128,1664]{1,0:T(8,128)(2,1)S(1)} %collective-permute-done.2.refs_3_.refs_4_), channel_id=1, source_target_pairs={{48,0},{497,1},{32,16},{481,17},{80,32},{17,33},{64,48},{1,49},{11... | collective-permute-start | bytes 1277960 | tf_op jit(solution)/shard_map/ppermute | solution.py:45
  40.2 3.8 %collective-permute-start.4 = (bf16[128,1664]{1,0:T(8,128)(2,1)S(1)}, bf16[128,1664]{1,0:T(8,128)(2,1)S(1)}, u32[]{:S(2)}, u32[]{:S(2)}) collective-permute-start(bf16[128,1664]{1,0:T(8,128)(2,1)S(1)} %collective-permute-done.2.refs_3_.refs_4_), channel_id=1, source_target_pairs={{32,0},{481,1},{48,16},{497,17},{64,32},{1,33},{80,48},{17,49},{96... | collective-permute-start | bytes 1277960 | tf_op jit(solution)/shard_map/ppermute | solution.py:45
  44.1 1.9 %collective-permute-start.3 = (bf16[128,1664]{1,0:T(8,128)(2,1)S(1)}, bf16[128,1664]{1,0:T(8,128)(2,1)S(1)}, u32[]{:S(2)}, u32[]{:S(2)}) collective-permute-start(bf16[128,1664]{1,0:T(8,128)(2,1)S(1)} %collective-permute-done.2.refs_3_.refs_4_), channel_id=1, source_target_pairs={{16,0},{17,1},{0,16},{1,17},{48,32},{49,33},{32,48},{33,49},{80,64... | collective-permute-start | bytes 1277960 | tf_op jit(solution)/shard_map/ppermute | solution.py:45
  46.0 0.0 collective-permute-done.refs_1_.refs_2_
  46.0 3.5 %collective-permute-start.1 = (bf16[128,1664]{1,0:T(8,128)(2,1)S(1)}, bf16[128,1664]{1,0:T(8,128)(2,1)S(1)}, u32[]{:S(2)}, u32[]{:S(2)}) collective-permute-start(bf16[128,1664]{1,0:T(8,128)(2,1)S(1)} %collective-permute-done.refs_1_.refs_2_), channel_id=1, source_target_pairs={{448,0},{65,1},{464,16},{81,17},{480,32},{97,33},{496,48},{113,49}... | collective-permute-start | bytes 1277960 | tf_op jit(solution)/shard_map/ppermute | solution.py:45
  49.5 0.1 fusion
  49.6 0.1 select_reduce_fusion
  49.7 3.0 %collective-permute-done.5.refs_6_.refs_7_ = bf16[128,1664]{1,0:T(8,128)(2,1)S(1)} collective-permute-done((bf16[128,1664]{1,0:T(8,128)(2,1)S(1)}, bf16[128,1664]{1,0:T(8,128)(2,1)S(1)}, u32[]{:S(2)}, u32[]{:S(2)}) %collective-permute-start.5) | collective-permute-done | bytes 426016 | tf_op jit(solution)/shard_map/ppermute | solution.py:45
  52.7 6.9 %collective-permute-done.4.refs_5_.refs_6_ = bf16[128,1664]{1,0:T(8,128)(2,1)S(1)} collective-permute-done((bf16[128,1664]{1,0:T(8,128)(2,1)S(1)}, bf16[128,1664]{1,0:T(8,128)(2,1)S(1)}, u32[]{:S(2)}, u32[]{:S(2)}) %collective-permute-start.4) | collective-permute-done | bytes 426016 | tf_op jit(solution)/shard_map/ppermute | solution.py:45
  59.6 0.0 collective-permute-done.3.refs_4_.refs_5_
  59.6 0.1 collective-permute-done.1.refs_2_.refs_3_
  59.7 1.6 %shard_map.37 = bf16[8,288,128]{2,1,0:T(8,128)(2,1)S(1)} custom-call(bf16[128,1664]{1,0:T(8,128)(2,1)S(1)} %constant_dynamic-update-slice_fusion.refs_0_, bf16[128,1664]{1,0:T(8,128)(2,1)S(1)} %collective-permute-done.refs_1_.refs_2_, bf16[128,1664]{1,0:T(8,128)(2,1)S(1)} %collective-permute-done.1.refs_2_.refs_3_, ...), custom_call_target="tpu_custom_call" | custom-call | flops 981467136 | bytes 2981888 | tf_op jit(solution)/shard_map/pallas_call | solution.py:148
  61.3 17.4 %all_to_all.10.parts = bf16[8,288,128]{2,1,0:T(8,128)(2,1)S(1)} all-to-all(bf16[8,288,128]{2,1,0:T(8,128)(2,1)S(1)} %shard_map.37), channel_id=1, replica_groups=mesh['z'=16,'xl'=2,'y'=4,'xh'=2,'seq'=2] {'y','xh'}, dimensions={0} | all-to-all | bytes 1179648 | tf_op jit(solution)/shard_map/all_to_all | solution.py:185
  78.7 0.7 shard_map.38
  79.4 0.0 copy-start
  79.4 13.2 %all_to_all.11.refs_0_ = bf16[8,288,128]{2,1,0:T(8,128)(2,1)S(1)} all-to-all(bf16[8,288,128]{2,1,0:T(8,128)(2,1)S(1)} %shard_map.38), channel_id=1, replica_groups=mesh['z'=16,'xl'=2,'y'=4,'xh'=2,'seq'=2] {'y','xh'}, dimensions={0} | all-to-all | bytes 1179648 | tf_op jit(solution)/shard_map/all_to_all | solution.py:194
  92.6 0.0 copy-done
  92.6 1.1 shard_map.39
  93.8 6.5 %collective-permute-start.6 = (bf16[128,640]{1,0:T(8,128)(2,1)S(1)}, bf16[128,640]{1,0:T(8,128)(2,1)S(1)}, u32[]{:S(2)}, u32[]{:S(2)}) collective-permute-start(bf16[128,640]{1,0:T(8,128)(2,1)S(1)} %get-tuple-element.31), channel_id=1, source_target_pairs={{0,448},{1,65},{16,464},{17,81},{32,480},{33,97},{48,496},{49,113}... | collective-permute-start | bytes 491528 | tf_op jit(solution)/shard_map/ppermute | solution.py:49
  100.2 4.4 %collective-permute-start.8 = (bf16[128,640]{1,0:T(8,128)(2,1)S(1)}, bf16[128,640]{1,0:T(8,128)(2,1)S(1)}, u32[]{:S(2)}, u32[]{:S(2)}) collective-permute-start(bf16[128,640]{1,0:T(8,128)(2,1)S(1)} %get-tuple-element.33), channel_id=1, source_target_pairs={{0,48},{1,497},{16,32},{17,481},{32,80},{33,17},{48,64},{49,1},{64... | collective-permute-start | bytes 491528 | tf_op jit(solution)/shard_map/ppermute | solution.py:49
  104.7 1.9 %collective-permute-start.9 = (bf16[128,640]{1,0:T(8,128)(2,1)S(1)}, bf16[128,640]{1,0:T(8,128)(2,1)S(1)}, u32[]{:S(2)}, u32[]{:S(2)}) collective-permute-start(bf16[128,640]{1,0:T(8,128)(2,1)S(1)} %get-tuple-element.34), channel_id=1, source_target_pairs={{0,32},{1,481},{16,48},{17,497},{32,64},{33,1},{48,80},{49,17},{64... | collective-permute-start | bytes 491528 | tf_op jit(solution)/shard_map/ppermute | solution.py:49
  106.6 2.6 %collective-permute-start.10 = (bf16[128,640]{1,0:T(8,128)(2,1)S(1)}, bf16[128,640]{1,0:T(8,128)(2,1)S(1)}, u32[]{:S(2)}, u32[]{:S(2)}) collective-permute-start(bf16[128,640]{1,0:T(8,128)(2,1)S(1)} %get-tuple-element.35), channel_id=1, source_target_pairs={{0,16},{1,17},{16,0},{17,1},{32,48},{33,49},{48,32},{49,33},{64,80... | collective-permute-start | bytes 491528 | tf_op jit(solution)/shard_map/ppermute | solution.py:49
  109.2 0.0 collective-permute-done.6
  109.3 5.6 %collective-permute-start.7 = (bf16[128,640]{1,0:T(8,128)(2,1)S(1)}, bf16[128,640]{1,0:T(8,128)(2,1)S(1)}, u32[]{:S(2)}, u32[]{:S(2)}) collective-permute-start(bf16[128,640]{1,0:T(8,128)(2,1)S(1)} %add_convert_fusion.1), channel_id=1, source_target_pairs={{0,464},{1,81},{16,448},{17,65},{32,496},{33,113},{48,480},{49,97}... | collective-permute-start | bytes 491528 | tf_op jit(solution)/shard_map/ppermute | solution.py:49
  114.9 0.0 collective-permute-done.8
  114.9 0.0 collective-permute-done.9
  114.9 0.0 collective-permute-done.10
  114.9 0.1 add_convert_fusion
  115.0 3.8 %collective-permute-start.11 = (bf16[128,640]{1,0:T(8,128)(2,1)S(1)}, bf16[128,640]{1,0:T(8,128)(2,1)S(1)}, u32[]{:S(2)}, u32[]{:S(2)}) collective-permute-start(bf16[128,640]{1,0:T(8,128)(2,1)S(1)} %add_convert_fusion), channel_id=1, source_target_pairs={{0,96},{1,417},{16,112},{17,433},{32,128},{33,449},{48,144},{49,46... | collective-permute-start | bytes 491528 | tf_op jit(solution)/shard_map/ppermute | solution.py:49
  118.7 5.4 %collective-permute-done.7 = bf16[128,640]{1,0:T(8,128)(2,1)S(1)} collective-permute-done((bf16[128,640]{1,0:T(8,128)(2,1)S(1)}, bf16[128,640]{1,0:T(8,128)(2,1)S(1)}, u32[]{:S(2)}, u32[]{:S(2)}) %collective-permute-start.7) | collective-permute-done | bytes 163872 | tf_op jit(solution)/shard_map/ppermute | solution.py:49
  124.1 4.4 %collective-permute-done.11 = bf16[128,640]{1,0:T(8,128)(2,1)S(1)} collective-permute-done((bf16[128,640]{1,0:T(8,128)(2,1)S(1)}, bf16[128,640]{1,0:T(8,128)(2,1)S(1)}, u32[]{:S(2)}, u32[]{:S(2)}) %collective-permute-start.11) | collective-permute-done | bytes 163872 | tf_op jit(solution)/shard_map/ppermute | solution.py:49
  128.5 0.8 multiply_convert_fusion
  (5 shorter events, 0.1 us)
Async XLA Ops:
  0.0 1.0 copy-start.1
  1.1 35.9 %collective-permute-start.2 = (bf16[128,1664]{1,0:T(8,128)(2,1)S(1)}, bf16[128,1664]{1,0:T(8,128)(2,1)S(1)}, u32[]{:S(2)}, u32[]{:S(2)}) collective-permute-start(bf16[128,1664]{1,0:T(8,128)(2,1)S(1)} %constant_dynamic-update-slice_fusion.refs_0_), channel_id=1, source_target_pairs={{96,0},{417,1},{112,16},{433,17},{128,32},{449,33},{144,48},{465,4... | collective-permute-start | bytes 1277960 | tf_op jit(solution)/shard_map/ppermute | solution.py:45
  13.3 32.7 %collective-permute-start = (bf16[128,1664]{1,0:T(8,128)(2,1)S(1)}, bf16[128,1664]{1,0:T(8,128)(2,1)S(1)}, u32[]{:S(2)}, u32[]{:S(2)}) collective-permute-start(bf16[128,1664]{1,0:T(8,128)(2,1)S(1)} %constant_dynamic-update-slice_fusion.refs_0_), channel_id=1, source_target_pairs={{464,0},{81,1},{448,16},{65,17},{496,32},{113,33},{480,48},{97,49}... | collective-permute-start | bytes 1277960 | tf_op jit(solution)/shard_map/ppermute | solution.py:45
  16.8 0.7 copy-start.2
  36.9 15.8 %collective-permute-start.5 = (bf16[128,1664]{1,0:T(8,128)(2,1)S(1)}, bf16[128,1664]{1,0:T(8,128)(2,1)S(1)}, u32[]{:S(2)}, u32[]{:S(2)}) collective-permute-start(bf16[128,1664]{1,0:T(8,128)(2,1)S(1)} %collective-permute-done.2.refs_3_.refs_4_), channel_id=1, source_target_pairs={{48,0},{497,1},{32,16},{481,17},{80,32},{17,33},{64,48},{1,49},{11... | collective-permute-start | bytes 1277960 | tf_op jit(solution)/shard_map/ppermute | solution.py:45
  40.2 19.4 %collective-permute-start.4 = (bf16[128,1664]{1,0:T(8,128)(2,1)S(1)}, bf16[128,1664]{1,0:T(8,128)(2,1)S(1)}, u32[]{:S(2)}, u32[]{:S(2)}) collective-permute-start(bf16[128,1664]{1,0:T(8,128)(2,1)S(1)} %collective-permute-done.2.refs_3_.refs_4_), channel_id=1, source_target_pairs={{32,0},{481,1},{48,16},{497,17},{64,32},{1,33},{80,48},{17,49},{96... | collective-permute-start | bytes 1277960 | tf_op jit(solution)/shard_map/ppermute | solution.py:45
  44.1 15.6 %collective-permute-start.3 = (bf16[128,1664]{1,0:T(8,128)(2,1)S(1)}, bf16[128,1664]{1,0:T(8,128)(2,1)S(1)}, u32[]{:S(2)}, u32[]{:S(2)}) collective-permute-start(bf16[128,1664]{1,0:T(8,128)(2,1)S(1)} %collective-permute-done.2.refs_3_.refs_4_), channel_id=1, source_target_pairs={{16,0},{17,1},{0,16},{1,17},{48,32},{49,33},{32,48},{33,49},{80,64... | collective-permute-start | bytes 1277960 | tf_op jit(solution)/shard_map/ppermute | solution.py:45
  46.0 13.7 %collective-permute-start.1 = (bf16[128,1664]{1,0:T(8,128)(2,1)S(1)}, bf16[128,1664]{1,0:T(8,128)(2,1)S(1)}, u32[]{:S(2)}, u32[]{:S(2)}) collective-permute-start(bf16[128,1664]{1,0:T(8,128)(2,1)S(1)} %collective-permute-done.refs_1_.refs_2_), channel_id=1, source_target_pairs={{448,0},{65,1},{464,16},{81,17},{480,32},{97,33},{496,48},{113,49}... | collective-permute-start | bytes 1277960 | tf_op jit(solution)/shard_map/ppermute | solution.py:45
  79.4 13.2 %copy-start = (bf16[128,640]{1,0:T(8,128)(2,1)S(1)}, bf16[128,640]{1,0:T(8,128)(2,1)}, u32[]{:S(2)}) copy-start(bf16[128,640]{1,0:T(8,128)(2,1)} %refs_1_.1) | copy-start | bytes 491524
  93.8 15.5 %collective-permute-start.6 = (bf16[128,640]{1,0:T(8,128)(2,1)S(1)}, bf16[128,640]{1,0:T(8,128)(2,1)S(1)}, u32[]{:S(2)}, u32[]{:S(2)}) collective-permute-start(bf16[128,640]{1,0:T(8,128)(2,1)S(1)} %get-tuple-element.31), channel_id=1, source_target_pairs={{0,448},{1,65},{16,464},{17,81},{32,480},{33,97},{48,496},{49,113}... | collective-permute-start | bytes 491528 | tf_op jit(solution)/shard_map/ppermute | solution.py:49
  100.2 14.6 %collective-permute-start.8 = (bf16[128,640]{1,0:T(8,128)(2,1)S(1)}, bf16[128,640]{1,0:T(8,128)(2,1)S(1)}, u32[]{:S(2)}, u32[]{:S(2)}) collective-permute-start(bf16[128,640]{1,0:T(8,128)(2,1)S(1)} %get-tuple-element.33), channel_id=1, source_target_pairs={{0,48},{1,497},{16,32},{17,481},{32,80},{33,17},{48,64},{49,1},{64... | collective-permute-start | bytes 491528 | tf_op jit(solution)/shard_map/ppermute | solution.py:49
  104.7 10.2 %collective-permute-start.9 = (bf16[128,640]{1,0:T(8,128)(2,1)S(1)}, bf16[128,640]{1,0:T(8,128)(2,1)S(1)}, u32[]{:S(2)}, u32[]{:S(2)}) collective-permute-start(bf16[128,640]{1,0:T(8,128)(2,1)S(1)} %get-tuple-element.34), channel_id=1, source_target_pairs={{0,32},{1,481},{16,48},{17,497},{32,64},{33,1},{48,80},{49,17},{64... | collective-permute-start | bytes 491528 | tf_op jit(solution)/shard_map/ppermute | solution.py:49
  106.6 8.3 %collective-permute-start.10 = (bf16[128,640]{1,0:T(8,128)(2,1)S(1)}, bf16[128,640]{1,0:T(8,128)(2,1)S(1)}, u32[]{:S(2)}, u32[]{:S(2)}) collective-permute-start(bf16[128,640]{1,0:T(8,128)(2,1)S(1)} %get-tuple-element.35), channel_id=1, source_target_pairs={{0,16},{1,17},{16,0},{17,1},{32,48},{33,49},{48,32},{49,33},{64,80... | collective-permute-start | bytes 491528 | tf_op jit(solution)/shard_map/ppermute | solution.py:49
  109.3 14.8 %collective-permute-start.7 = (bf16[128,640]{1,0:T(8,128)(2,1)S(1)}, bf16[128,640]{1,0:T(8,128)(2,1)S(1)}, u32[]{:S(2)}, u32[]{:S(2)}) collective-permute-start(bf16[128,640]{1,0:T(8,128)(2,1)S(1)} %add_convert_fusion.1), channel_id=1, source_target_pairs={{0,464},{1,81},{16,448},{17,65},{32,496},{33,113},{48,480},{49,97}... | collective-permute-start | bytes 491528 | tf_op jit(solution)/shard_map/ppermute | solution.py:49
  115.0 13.5 %collective-permute-start.11 = (bf16[128,640]{1,0:T(8,128)(2,1)S(1)}, bf16[128,640]{1,0:T(8,128)(2,1)S(1)}, u32[]{:S(2)}, u32[]{:S(2)}) collective-permute-start(bf16[128,640]{1,0:T(8,128)(2,1)S(1)} %add_convert_fusion), channel_id=1, source_target_pairs={{0,96},{1,417},{16,112},{17,433},{32,128},{33,449},{48,144},{49,46... | collective-permute-start | bytes 491528 | tf_op jit(solution)/shard_map/ppermute | solution.py:49
